TPU v7x, 32 devices: a whole 2x2x4 slice. The times are simulated.
32 devices in a mesh: dp: 2 (over core), ctx: 4 (over y, x), tensor: 4 (over z).
Axes of the slice: x: 2, y: 2, z: 4, core: 2. Of those that a mesh axis runs over, the one named last changes fastest.
Arguments:
- tokens: bfloat16 [8192, 768], P(('dp', 'ctx')), may hold values from -6 to 6
- segments: int32 [8192], P(('dp', 'ctx')), may hold values from 0 to 2, as said below
- in_gain: float32 [2, 768], replicated, may hold values from 0.5 to 1.5
- gate_weight: bfloat16 [2, 768, 1536], P(None, None, 'tensor'), may hold values from -0.21875 to 0.21875
- value_weight: bfloat16 [2, 768, 1536], P(None, None, 'tensor'), may hold values from -0.21875 to 0.21875
- state_weight: bfloat16 [2, 768, 256], replicated, may hold values from -0.21875 to 0.21875
- step_weight: bfloat16 [2, 768, 24], P(None, None, 'tensor'), may hold values from -0.21875 to 0.21875
- value_filter: float32 [2, 4, 1536], P(None, None, 'tensor'), may hold values from -3 to 3
- value_offset: float32 [2, 1536], P(None, 'tensor'), may hold values from -1.5 to 1.5
- state_filter: float32 [2, 4, 256], replicated, may hold values from -3 to 3
- state_offset: float32 [2, 256], replicated, may hold values from -1.5 to 1.5
- step_bias: float32 [2, 24], P(None, 'tensor'), may hold values from -11 to -1
- decay_log: float32 [2, 24], P(None, 'tensor'), may hold values from 0 to 1.5
- skip_gain: float32 [2, 24], P(None, 'tensor'), may hold values from 0.5 to 1.5
- out_gain: float32 [2, 1536], P(None, 'tensor'), may hold values from 0.5 to 1.5
- out_weight: bfloat16 [2, 1536, 768], P(None, 'tensor'), may hold values from -0.15625 to 0.15625
- cotangent: bfloat16 [8192, 768], P(('dp', 'ctx')), may hold values from -6 to 6
Outputs:
- mixed: bfloat16 [8192, 768], P(('dp', 'ctx'))
- input_grad: bfloat16 [8192, 768], P(('dp', 'ctx'))
- grad_in_gain: float32 [2, 768], replicated
- grad_gate_weight: float32 [2, 768, 1536], P(None, None, 'tensor')
- grad_value_weight: float32 [2, 768, 1536], P(None, None, 'tensor')
- grad_state_weight: float32 [2, 768, 256], replicated
- grad_step_weight: float32 [2, 768, 24], P(None, None, 'tensor')
- grad_value_filter: float32 [2, 4, 1536], P(None, None, 'tensor')
- grad_value_offset: float32 [2, 1536], P(None, 'tensor')
- grad_state_filter: float32 [2, 4, 256], replicated
- grad_state_offset: float32 [2, 256], replicated
- grad_step_bias: float32 [2, 24], P(None, 'tensor')
- grad_decay_log: float32 [2, 24], P(None, 'tensor')
- grad_skip_gain: float32 [2, 24], P(None, 'tensor')
- grad_out_gain: float32 [2, 1536], P(None, 'tensor')
- grad_out_weight: float32 [2, 1536, 768], P(None, 'tensor')
Inputs may be any that keep to these rules, and one draw needn't show every extreme that they name: `segments`: along each sequence of 4096 tokens the numbers start at 0 and rise by 0 or 1 from one token to the next. Each sequence holds three documents: the first ends inside its first piece of 1024 tokens, the last begins inside its last piece, so the middle one reaches from the first piece to the last.
All inputs are finite; a program needn't handle non-finite values.
Results may differ from a plain program's by a relative error of at most 0.028.
Values sent between devices are 32-bit elements; how exact they have to be, the bound alone decides.
No kernel may reach another device: no remote copies, remote signals or barrier semaphores. Data moves between devices by JAX's collectives and lax.ppermute only.
A program may use at most 192 MiB of HBM per device.

v0:
```python
import jax
import jax.numpy as jnp
from jax import lax
from jax.sharding import PartitionSpec as P

CONV = 4
GROUP = 256
LAYERS = 2
INNER = 1536


EPSILON = 1e-05
PRECISE = lax.Precision.HIGHEST
FLOAT = jnp.float32
BFLOAT = jnp.bfloat16


def entering(shard, axis, combine, identity, reverse):
    count, index = (lax.axis_size(axis), lax.axis_index(axis))
    everything = jax.tree.map(lambda part: lax.all_gather(part, axis), shard)
    start = jax.tree.map(
        lambda part, zero: jnp.broadcast_to(jnp.asarray(zero, part.dtype), part.shape),
        shard,
        identity,
    )

    def step(k, before):
        at = count - 1 - k if reverse else k
        reached = at > index if reverse else at < index
        new = combine(before, jax.tree.map(lambda part: part[at], everything))
        return jax.tree.map(lambda a, b: jnp.where(reached, a, b), new, before)

    return lax.fori_loop(0, count, step, start)


def passed_along(shard, axis, by):
    count = lax.axis_size(axis)
    pairs = [(i, i + by) for i in range(count) if 0 <= i + by < count]
    return lax.ppermute(shard, axis, pairs)


def silu_slope(value):
    sigma = jax.nn.sigmoid(value)
    return sigma * (1.0 + value * (1.0 - sigma))


def times_trans(left, right):
    return lax.dot_general(left, right, (((1,), (1,)), ((), ())), preferred_element_type=FLOAT)


def outer_sum(left, right):
    return lax.dot_general(left, right, (((0,), (0,)), ((), ())), preferred_element_type=FLOAT)


def join_forward(earlier, later):
    return (earlier[0] * later[0], later[0][:, None, None] * earlier[1] + later[1])


def join_backward(earlier, later):
    return (later[0] * earlier[0], later[1] + later[0][:, None, None] * earlier[1])


def pass_state(dev_keep, dev_state):
    ident = (jnp.ones_like(dev_keep), jnp.zeros_like(dev_state))
    _, accum = entering((dev_keep, dev_state), "ctx", join_forward, ident, False)
    return accum


def pass_back(dev_keep, dev_pull):
    ident = (jnp.ones_like(dev_keep), jnp.zeros_like(dev_pull))
    _, accum = entering((dev_keep, dev_pull), "ctx", join_backward, ident, True)
    return accum


def ssd_forward(values, write_vec, read_vec, steps, log_decay, seg_blocks, seg_before):
    blocks, span = seg_blocks.shape
    heads_here = steps.shape[1]
    vals = values.reshape(blocks, span, heads_here, -1)
    step_blk = steps.reshape(blocks, span, heads_here)
    step_lead = jnp.swapaxes(step_blk, 1, 2)
    cumlog = jnp.cumsum(log_decay.reshape(blocks, span, heads_here), axis=1)
    cum_lead = jnp.swapaxes(cumlog, 1, 2)
    write_blk = write_vec.reshape(blocks, span, -1)
    read_blk = read_vec.reshape(blocks, span, -1)
    places = jnp.arange(span)
    lower = places[:, None] >= places[None, :]
    within = (lower[None] & (seg_blocks[:, :, None] == seg_blocks[:, None, :]))[:, None]
    spread = cum_lead[:, :, :, None] - cum_lead[:, :, None, :]
    decay = jnp.where(within, jnp.exp(jnp.where(within, spread, 0.0)), 0.0)
    intersection = jnp.einsum("cin,cjn->cij", read_blk, write_blk, preferred_element_type=FLOAT)
    mixing = intersection[:, None] * decay * step_lead[:, :, None, :]
    output = jnp.einsum("chij,cjhp->cihp", mixing, vals, precision=PRECISE)
    enter = jnp.where((seg_blocks == seg_before[:, None])[..., None], jnp.exp(cumlog), 0.0)
    final_seg = seg_blocks[:, -1]
    tail = jnp.where(
        (seg_blocks == final_seg[:, None])[..., None], jnp.exp(cumlog[:, -1:, :] - cumlog), 0.0
    )
    retain = jnp.where((final_seg == seg_before)[:, None], jnp.exp(cumlog[:, -1, :]), 0.0)
    local_state = jnp.einsum(
        "cjh,cjhp,cjn->chpn", tail * step_blk, vals, write_blk, precision=PRECISE
    )

    def advance(state, item):
        return (item[0][:, None, None] * state + item[1], state)

    dev_state, local_in = lax.scan(
        advance, jnp.zeros(local_state.shape[1:], FLOAT), (retain, local_state)
    )
    running = jnp.cumprod(retain, axis=0)
    prefix = jnp.concatenate([jnp.ones_like(running[:1]), running[:-1]], axis=0)
    incoming = pass_state(running[-1], dev_state)
    states_in = local_in + prefix[:, :, None, None] * incoming[None]
    output = (
        output
        + jnp.einsum("cin,chpn->cihp", read_blk, states_in, precision=PRECISE) * enter[..., None]
    )
    kept = (
        vals,
        write_blk,
        read_blk,
        step_blk,
        step_lead,
        decay,
        intersection,
        mixing,
        enter,
        tail,
        retain,
        states_in,
    )
    return (output.reshape(values.shape[0], -1), kept)


def ssd_backward(grad_out, kept):
    (
        vals,
        write_blk,
        read_blk,
        step_blk,
        step_lead,
        decay,
        intersection,
        mixing,
        enter,
        tail,
        retain,
        states_in,
    ) = kept
    blocks, span, heads_here, head_size = vals.shape
    grad_blk = grad_out.reshape(vals.shape)
    pairing = jnp.einsum("cihp,cjhp->chij", grad_blk, vals, preferred_element_type=FLOAT)
    grad_vals = jnp.einsum("chij,cihp->cjhp", mixing, grad_blk, precision=PRECISE)
    weighted = pairing * intersection[:, None] * decay
    grad_intersection = jnp.sum(weighted * 0.0 + pairing * decay * step_lead[:, :, None, :], axis=1)
    grad_read = jnp.einsum("cij,cjn->cin", grad_intersection, write_blk, precision=PRECISE)
    grad_write = jnp.einsum("cij,cin->cjn", grad_intersection, read_blk, precision=PRECISE)
    grad_steps = jnp.swapaxes(jnp.sum(weighted, axis=2), 1, 2)
    flow = weighted * step_lead[:, :, None, :]
    grad_cum = jnp.swapaxes(jnp.sum(flow, axis=3) - jnp.sum(flow, axis=2), 1, 2)
    grad_read = grad_read + jnp.einsum(
        "cih,cihp,chpn->cin", enter, grad_blk, states_in, precision=PRECISE
    )
    grad_enter = jnp.einsum("cihp,chpn,cin->cih", grad_blk, states_in, read_blk, precision=PRECISE)
    grad_cum = grad_cum + grad_enter * enter
    pulls = jnp.einsum("cih,cihp,cin->chpn", enter, grad_blk, read_blk, precision=PRECISE)

    def retreat(later, item):
        current = item[1] + item[0][:, None, None] * later
        return (current, current)

    dev_pull, local_back = lax.scan(
        retreat, jnp.zeros(pulls.shape[1:], FLOAT), (retain, pulls), reverse=True
    )
    suffix = jnp.cumprod(retain[::-1], axis=0)[::-1]
    beyond = pass_back(suffix[0], dev_pull)
    grad_in = local_back + suffix[:, :, None, None] * beyond[None]
    grad_next = jnp.concatenate([grad_in[1:], beyond[None]], axis=0)
    along = jnp.einsum("chpn,cjn->cjhp", grad_next, write_blk, precision=PRECISE)
    tail_step = tail * step_blk
    grad_vals = grad_vals + tail_step[..., None] * along
    grad_write = grad_write + jnp.einsum(
        "cjh,cjhp,chpn->cjn", tail_step, vals, grad_next, precision=PRECISE
    )
    reach = jnp.sum(vals * along, axis=3)
    grad_steps = grad_steps + tail * reach
    tail_flow = tail_step * reach
    grad_retain = jnp.einsum("chpn,chpn->ch", grad_next, states_in, precision=PRECISE)
    grad_last = jnp.sum(tail_flow, axis=1) + grad_retain * retain
    grad_cum = grad_cum - tail_flow
    grad_cum = grad_cum.at[:, -1, :].add(grad_last)
    grad_log = jnp.cumsum(grad_cum[:, ::-1, :], axis=1)[:, ::-1, :]
    row_count = blocks * span
    return (
        grad_vals.reshape(row_count, -1),
        grad_write.reshape(row_count, -1),
        grad_read.reshape(row_count, -1),
        grad_steps.reshape(row_count, heads_here),
        grad_log.reshape(row_count, heads_here),
    )


def forward_layer(resid, weights, geometry):
    (
        gain_in,
        gate_w,
        value_w,
        state_w,
        step_w,
        value_filt,
        value_off,
        state_filt,
        state_off,
        bias_step,
        decay_param,
        skip_param,
        gain_out,
        out_w,
    ) = weights
    conv_masks, seg_blocks, seg_before = geometry
    row_count = resid.shape[0]
    lane_count = gate_w.shape[1]
    state_size = state_w.shape[1] // 2
    heads_here = step_w.shape[1]
    inv_rms = lax.rsqrt(jnp.mean(resid * resid, axis=1, keepdims=True) + EPSILON)
    scaled = resid * inv_rms
    normed_in = (scaled * gain_in).astype(BFLOAT)
    gate_pre = jnp.dot(normed_in, gate_w, preferred_element_type=FLOAT)
    value_pre = jnp.dot(normed_in, value_w, preferred_element_type=FLOAT)
    state_pre = jnp.dot(normed_in, state_w, preferred_element_type=FLOAT)
    step_raw = jnp.dot(normed_in, step_w, preferred_element_type=FLOAT)
    pre_conv = jnp.concatenate([value_pre, state_pre], axis=1)
    edge_rows = passed_along(pre_conv[row_count - (CONV - 1) :], "ctx", 1)
    padded = jnp.concatenate([edge_rows, pre_conv], axis=0)
    filters = jnp.concatenate([value_filt, state_filt], axis=1)
    offsets = jnp.concatenate([value_off, state_off])
    conv_sum = jnp.zeros_like(pre_conv) + offsets
    for offset in range(CONV):
        conv_sum = (
            conv_sum + filters[offset] * padded[offset : offset + row_count] * conv_masks[offset]
        )
    activated = jax.nn.silu(conv_sum)
    values = activated[:, :lane_count].astype(BFLOAT)
    write_vec = activated[:, lane_count : lane_count + state_size].astype(BFLOAT)
    read_vec = activated[:, lane_count + state_size :].astype(BFLOAT)
    shifted = step_raw + bias_step
    steps = jax.nn.softplus(shifted)
    log_decay = -jnp.exp(decay_param) * steps
    scan_out, kept = ssd_forward(
        values, write_vec, read_vec, steps, log_decay, seg_blocks, seg_before
    )
    head_vals = values.reshape(row_count, heads_here, -1)
    ssm_out = scan_out + (skip_param[:, None] * head_vals).reshape(row_count, lane_count)
    gate_act = jax.nn.silu(gate_pre)
    gated = ssm_out * gate_act
    out_in = (gated * gain_out).astype(BFLOAT)
    partial_value = jnp.dot(out_in, out_w, preferred_element_type=FLOAT)
    squares = jnp.sum(gated * gated, axis=1)
    branch, total_sq = lax.psum((partial_value, squares), "tensor")
    inv_norm = lax.rsqrt(total_sq / INNER + EPSILON)[:, None]
    saved = (
        scaled,
        inv_rms,
        normed_in,
        gate_pre,
        padded,
        conv_sum,
        head_vals,
        shifted,
        log_decay,
        kept,
        ssm_out,
        gate_act,
        gated,
        out_in,
        branch,
        inv_norm,
    )
    return (resid + inv_norm * branch, saved)


def backward_layer(upstream, weights, saved, geometry):
    (
        gain_in,
        gate_w,
        value_w,
        state_w,
        step_w,
        value_filt,
        value_off,
        state_filt,
        state_off,
        bias_step,
        decay_param,
        skip_param,
        gain_out,
        out_w,
    ) = weights
    (
        scaled,
        inv_rms,
        normed_in,
        gate_pre,
        padded,
        conv_sum,
        head_vals,
        shifted,
        log_decay,
        kept,
        ssm_out,
        gate_act,
        gated,
        out_in,
        branch,
        inv_norm,
    ) = saved
    conv_masks = geometry[0]
    row_count = upstream.shape[0]
    lane_count = gate_w.shape[1]
    grad_branch = (inv_norm * upstream).astype(BFLOAT)
    grad_inv = jnp.sum(upstream * branch, axis=1, keepdims=True)
    grad_squares = -0.5 * grad_inv * inv_norm * inv_norm * inv_norm / INNER
    grad_out_w = outer_sum(out_in, grad_branch)
    grad_out_in = times_trans(grad_branch, out_w)
    grad_gain_out = jnp.sum(grad_out_in * gated, axis=0)
    grad_gated = grad_out_in * gain_out + 2.0 * grad_squares * gated
    grad_ssm_low = (grad_gated * gate_act).astype(BFLOAT)
    grad_gate = grad_gated * ssm_out * silu_slope(gate_pre)
    grad_heads = grad_ssm_low.astype(FLOAT).reshape(head_vals.shape)
    grad_skip = jnp.sum(grad_heads * head_vals, axis=(0, 2))
    grad_vals, grad_write, grad_read, grad_steps, grad_log = ssd_backward(grad_ssm_low, kept)
    grad_write, grad_read = lax.psum((grad_write, grad_read), "tensor")
    grad_vals = grad_vals + (skip_param[:, None] * grad_heads).reshape(row_count, lane_count)
    grad_act = jnp.concatenate([grad_vals, grad_write, grad_read], axis=1)
    grad_conv = grad_act * silu_slope(conv_sum)
    grad_offsets = jnp.sum(grad_conv, axis=0)
    filters = jnp.concatenate([value_filt, state_filt], axis=1)
    grad_filters = jnp.stack(
        [
            jnp.sum(grad_conv * padded[offset : offset + row_count] * conv_masks[offset], axis=0)
            for offset in range(CONV)
        ]
    )
    grad_pad = jnp.zeros(padded.shape, FLOAT)
    for offset in range(CONV):
        grad_pad = grad_pad + jnp.pad(
            grad_conv * filters[offset] * conv_masks[offset], ((offset, CONV - 1 - offset), (0, 0))
        )
    spill = passed_along(grad_pad[: CONV - 1], "ctx", -1)
    grad_pre = grad_pad[CONV - 1 :] + jnp.pad(spill, ((row_count - (CONV - 1), 0), (0, 0)))
    grad_steps = grad_steps - jnp.exp(decay_param) * grad_log
    grad_decay = jnp.sum(grad_log * log_decay, axis=0)
    grad_shifted = grad_steps * jax.nn.sigmoid(shifted)
    grad_bias = jnp.sum(grad_shifted, axis=0)
    gate_low = grad_gate.astype(BFLOAT)
    value_low = grad_pre[:, :lane_count].astype(BFLOAT)
    state_low = grad_pre[:, lane_count:].astype(BFLOAT)
    step_low = grad_shifted.astype(BFLOAT)
    grad_gate_w = outer_sum(normed_in, gate_low)
    grad_value_w = outer_sum(normed_in, value_low)
    grad_state_w = outer_sum(normed_in, state_low)
    grad_step_w = outer_sum(normed_in, step_low)
    leader = (lax.axis_index("tensor") == 0).astype(FLOAT)
    grad_normed = (
        times_trans(gate_low, gate_w)
        + times_trans(value_low, value_w)
        + times_trans(step_low, step_w)
        + leader * times_trans(state_low, state_w)
    )
    grad_normed = lax.psum(grad_normed, "tensor")
    grad_gain_in = jnp.sum(grad_normed * scaled, axis=0)
    grad_scaled = grad_normed * gain_in
    upstream = upstream + inv_rms * (
        grad_scaled - scaled * jnp.mean(grad_scaled * scaled, axis=1, keepdims=True)
    )
    grads = (
        grad_gain_in,
        grad_gate_w,
        grad_value_w,
        grad_state_w,
        grad_step_w,
        grad_filters[:, :lane_count],
        grad_offsets[:lane_count],
        grad_filters[:, lane_count:],
        grad_offsets[lane_count:],
        grad_bias,
        grad_decay,
        grad_skip,
        grad_gain_out,
        grad_out_w,
    )
    return (upstream, grads)


def local(
    tokens,
    segments,
    in_gain,
    gate_weight,
    value_weight,
    state_weight,
    step_weight,
    value_filter,
    value_offset,
    state_filter,
    state_offset,
    step_bias,
    decay_log,
    skip_gain,
    out_gain,
    out_weight,
    cotangent,
):
    row_count = tokens.shape[0]
    halo_seg = passed_along(segments[row_count - (CONV - 1) :], "ctx", 1)
    seg_ext = jnp.concatenate([halo_seg, segments])
    conv_masks = [
        (seg_ext[offset : offset + row_count] == segments).astype(FLOAT)[:, None]
        for offset in range(CONV)
    ]
    seg_blocks = segments.reshape(-1, GROUP)
    seg_before = jnp.concatenate([halo_seg[CONV - 2 :], seg_blocks[:-1, -1]])
    geometry = (conv_masks, seg_blocks, seg_before)
    params = (
        in_gain,
        gate_weight,
        value_weight,
        state_weight,
        step_weight,
        value_filter,
        value_offset,
        state_filter,
        state_offset,
        step_bias,
        decay_log,
        skip_gain,
        out_gain,
        out_weight,
    )
    resid = tokens.astype(FLOAT)
    saved_all = []
    for depth in range(LAYERS):
        resid, saved = forward_layer(resid, tuple((param[depth] for param in params)), geometry)
        saved_all.append(saved)
    mixed = resid.astype(BFLOAT)
    upstream = cotangent.astype(FLOAT)
    layer_grads = [None] * LAYERS
    for depth in range(LAYERS - 1, -1, -1):
        upstream, grads = backward_layer(
            upstream, tuple((param[depth] for param in params)), saved_all[depth], geometry
        )
        layer_grads[depth] = grads
    stacked = tuple(
        (jnp.stack([layer_grads[depth][member] for depth in range(LAYERS)]) for member in range(14))
    )
    stacked = lax.psum(
        (
            stacked[0],
            stacked[1],
            stacked[2],
            stacked[3],
            stacked[4],
            stacked[5],
            stacked[6],
            stacked[7],
            stacked[8],
            stacked[9],
            stacked[10],
            stacked[11],
            stacked[12],
            stacked[13],
        ),
        ("dp", "ctx"),
    )
    return (
        mixed,
        upstream.astype(BFLOAT),
        stacked[0],
        stacked[1],
        stacked[2],
        stacked[3],
        stacked[4],
        stacked[5],
        stacked[6],
        stacked[7],
        stacked[8],
        stacked[9],
        stacked[10],
        stacked[11],
        stacked[12],
        stacked[13],
    )


def solution(mesh):
    placed = (
        P(("dp", "ctx"), None),
        P(("dp", "ctx")),
        P(),
        P(None, None, "tensor"),
        P(None, None, "tensor"),
        P(),
        P(None, None, "tensor"),
        P(None, None, "tensor"),
        P(None, "tensor"),
        P(),
        P(),
        P(None, "tensor"),
        P(None, "tensor"),
        P(None, "tensor"),
        P(None, "tensor"),
        P(None, "tensor", None),
        P(("dp", "ctx"), None),
    )
    return jax.shard_map(
        local,
        mesh=mesh,
        in_specs=placed,
        out_specs=(
            P(("dp", "ctx"), None),
            P(("dp", "ctx"), None),
            P(),
            P(None, None, "tensor"),
            P(None, None, "tensor"),
            P(),
            P(None, None, "tensor"),
            P(None, None, "tensor"),
            P(None, "tensor"),
            P(),
            P(),
            P(None, "tensor"),
            P(None, "tensor"),
            P(None, "tensor"),
            P(None, "tensor"),
            P(None, "tensor", None),
        ),
        check_vma=False,
    )
```

profile of v0, /device:TPU:0, one launch (start us, length us, event | category | flops | bytes accessed | tf_op | source)
XLA Modules:
  0.0 1291.3 jit_solution(6507122760042638106)
XLA Ops:
  36.5 13.2 %reduce-window.26 = f32[4,6,2,128]{3,2,1,0:T(2,128)} reduce-window(f32[4,6,2,128]{3,2,1,0:T(2,128)} %copy.469, f32[]{:T(128)} %constant.319.clone.1), window={size=1x1x1x128 pad=0_0x0_0x0_0x127_0}, to_apply=%region_1.2 | reduce-window | flops 780288 | bytes 49156 | tf_op jit(solution)/shard_map/reduce-window
  86.2 7.8 all-gather.4
  120.1 12.3 all-gather
  164.1 12.5 psum.168
  176.6 106.4 %all-reduce.25.cloned.1.call-done = f32[1024,768]{1,0:T(8,128)} async-done(((f32[1024,768]{1,0:T(8,128)}), f32[1024,768]{1,0:T(8,128)}) %all-reduce.25.cloned.1.call-update) | async-done | bytes 3145744 | tf_op jit(solution)/shard_map/psum | solution.py:258
  305.1 7.7 all-gather.5
  339.7 9.6 while.124
  349.3 12.8 all-gather.1
  393.2 8.2 all-gather.6
  405.4 10.9 psum.170
  416.3 92.7 %all-reduce.27.cloned.1.call-done = f32[1024,768]{1,0:T(8,128)} async-done(((f32[1024,768]{1,0:T(8,128)}), f32[1024,768]{1,0:T(8,128)}) %all-reduce.27.cloned.1.call-update) | async-done | bytes 3145744 | tf_op jit(solution)/shard_map/psum | solution.py:258
  525.1 12.2 while.126
  537.2 14.2 %all-gather.2 = f32[24,64,128]{2,1,0:T(8,128)} all-gather(f32[6,64,128]{2,1,0:T(8,128)} %get-tuple-element.763), channel_id=4, replica_groups=mesh['dp'=2,'ctx'=4,'tensor'=4] {'ctx'}, dimensions={0}, use_global_device_ids=true | all-gather | bytes 983040 | tf_op jit(solution)/shard_map/all_gather | solution.py:20
  551.5 8.9 while.127
  616.4 39.5 %all-reduce.39.cloned.1.call-done = (f32[1024,128]{0,1:T(8,128)}, f32[1024,128]{0,1:T(8,128)}) async-done(((f32[1024,128]{0,1:T(8,128)}, f32[1024,128]{0,1:T(8,128)}), (f32[1024,128]{0,1:T(8,128)}, f32[1024,128]{0,1:T(8,128)})) %all-reduce.39.cloned.1.call-update) | async-done | bytes 1048592 | tf_op jit(solution)/shard_map/psum | solution.py:331
  666.6 7.9 collective-permute-done.3
  681.6 9.3 all-gather.7
  705.3 95.8 %all-reduce.29.cloned.1.call-done = f32[1024,768]{1,0:T(8,128)} async-done(((f32[1024,768]{1,0:T(8,128)}), f32[1024,768]{1,0:T(8,128)}) %all-reduce.29.cloned.1.call-update) | async-done | bytes 3145744 | tf_op jit(solution)/shard_map/psum | solution.py:369
  820.2 11.7 all-gather.3
  888.3 42.4 %all-reduce.37.cloned.1.call-done = (f32[1024,128]{0,1:T(8,128)}, f32[1024,128]{0,1:T(8,128)}) async-done(((f32[1024,128]{0,1:T(8,128)}, f32[1024,128]{0,1:T(8,128)}), (f32[1024,128]{0,1:T(8,128)}, f32[1024,128]{0,1:T(8,128)})) %all-reduce.37.cloned.1.call-update) | async-done | bytes 1048592 | tf_op jit(solution)/shard_map/psum | solution.py:331
  941.0 7.7 collective-permute-done.4
  971.8 103.5 %all-reduce.31.cloned.1.call-done = f32[1024,768]{1,0:T(8,128)} async-done(((f32[1024,768]{1,0:T(8,128)}), f32[1024,768]{1,0:T(8,128)}) %all-reduce.31.cloned.1.call-update) | async-done | bytes 3145744 | tf_op jit(solution)/shard_map/psum | solution.py:369
  1084.9 47.9 %all-reduce.33.cloned.1.call-done = (f32[2,768]{1,0:T(2,128)}, f32[2,768,6]{1,2,0:T(8,128)}, f32[2,4,384]{2,1,0:T(4,128)}, f32[2,384]{1,0:T(2,128)}, f32[2,4,256...) async-done(((f32[2,768]{1,0:T(2,128)}, f32[2,768,6]{1,2,0:T(8,128)}, f32[2,4,384]{2,1,0:T(4,128)}, ...) | async-done | bytes 71840 | tf_op jit(solution)/shard_map/psum | solution.py:455
  1134.2 135.8 %all-reduce.35.cloned.1.call-done = (f32[2,768,384]{2,1,0:T(8,128)}, f32[2,768,384]{2,1,0:T(8,128)}, f32[2,768,256]{2,1,0:T(8,128)}, f32[2,384,768]{2,1,0:T(8,128)}) async-done(((f32[2,768,384]{2,1,0:T(8,128)}, f32[2,768,384]{2,1,0:T(8,128)}, f32[2,768,256]{2,1,0:T(8,128)}, f32[2,384,768]{2,1,0:T(8,128)}), (f32[2,768,384]{2,1,0:T(8,128)}, f32[2,768,384]{2,1,0:T(8,128)}, f32[2,768,256]{2,1,0:T(8,128)}, ...) | async-done | bytes 8650768 | tf_op jit(solution)/shard_map/psum | solution.py:455
  (922 shorter events, 500.4 us)
Async XLA Ops:
  7.2 275.7 %all-reduce.25.cloned.1.call-start = ((), (), s32[]{:S(2)}) async-start(), calls=%async_computation | async-start | bytes 6291456 | tf_op jit(solution)/shard_map/psum | solution.py:258
  8.7 67.6 %collective-permute-start.1 = (s32[3]{0:T(128)}, s32[3]{0:T(128)}, u32[]{:S(2)}, u32[]{:S(2)}) collective-permute-start(s32[3]{0:T(128)} %slice.380), channel_id=1, source_target_pairs={{0,4},{4,8},{8,12},{1,5},{5,9},{9,13},{2,6},{6,10},{10,14},{3,7},{... | collective-permute-start | bytes 44 | tf_op jit(solution)/shard_map/ppermute | solution.py:39
  17.1 138.3 %copy-start.4 = (bf16[1024,768]{1,0:T(8,128)(2,1)}, bf16[1024,768]{1,0:T(8,128)(2,1)S(1)}, u32[]{:S(2)}) copy-start(bf16[1024,768]{1,0:T(8,128)(2,1)S(1)} %fusion.16) | copy-start | bytes 4718596
  18.8 86.0 %copy-start.6 = (f32[1024,384]{0,1:T(8,128)}, f32[1024,384]{0,1:T(8,128)S(1)}, u32[]{:S(2)}) copy-start(f32[1024,384]{0,1:T(8,128)S(1)} %fusion.116) | copy-start | bytes 4718596
  22.2 75.8 %collective-permute-start = (f32[3,640]{0,1:T(8,128)}, f32[3,640]{0,1:T(8,128)}, u32[]{:S(2)}, u32[]{:S(2)}) collective-permute-start(f32[3,640]{0,1:T(8,128)} %fusion.173), channel_id=1, source_target_pairs={{0,4},{4,8},{8,12},{1,5},{5,9},{9,13},{2,6},{6,10},{10,14},{3,7},{... | collective-permute-start | bytes 23048 | tf_op jit(solution)/shard_map/ppermute | solution.py:39
  161.3 121.6 %copy-start.14 = (bf16[1024,768]{1,0:T(8,128)(2,1)S(1)}, bf16[1024,768]{1,0:T(8,128)(2,1)}, u32[]{:S(2)}) copy-start(bf16[1024,768]{1,0:T(8,128)(2,1)} %param.37) | copy-start | bytes 4718596
  161.4 347.6 %all-reduce.27.cloned.1.call-start = ((), (), s32[]{:S(2)}) async-start(), calls=%async_computation.1 | async-start | bytes 6291456 | tf_op jit(solution)/shard_map/psum | solution.py:258
  176.5 109.0 %copy-start.162 = (f32[1024]{0:T(1024)}, f32[1024]{0:T(1024)S(1)}, u32[]{:S(2)}) copy-start(f32[1024]{0:T(1024)S(1)} %psum.168) | copy-start | bytes 12292
  176.5 109.0 %copy-start.140 = (f32[1024]{0:T(1024)}, f32[1024]{0:T(1024)S(1)}, u32[]{:S(2)}) copy-start(f32[1024]{0:T(1024)S(1)} %add_rsqrt_fusion.2) | copy-start | bytes 12292
  290.3 24.6 %collective-permute-start.2 = (f32[3,640]{0,1:T(8,128)S(1)}, f32[3,640]{0,1:T(8,128)}, u32[]{:S(2)}, u32[]{:S(2)}) collective-permute-start(f32[3,640]{0,1:T(8,128)S(1)} %fusion.172), channel_id=1, source_target_pairs={{0,4},{4,8},{8,12},{1,5},{5,9},{9,13},{2,6},{6,10},{10,14},{3,7},{... | collective-permute-start | bytes 23048 | tf_op jit(solution)/shard_map/ppermute | solution.py:39
  389.5 266.5 %all-reduce.39.cloned.1.call-start = ((), (), s32[]{:S(2)}) async-start(), calls=%async_computation.7 | async-start | bytes 2097152 | tf_op jit(solution)/shard_map/psum | solution.py:331
  605.1 196.0 %all-reduce.29.cloned.1.call-start = ((), (), s32[]{:S(2)}) async-start(), calls=%async_computation.2 | async-start | bytes 6291456 | tf_op jit(solution)/shard_map/psum | solution.py:369
  663.0 11.5 collective-permute-start.3
  680.5 250.2 %all-reduce.37.cloned.1.call-start = ((), (), s32[]{:S(2)}) async-start(), calls=%async_computation.6 | async-start | bytes 2097152 | tf_op jit(solution)/shard_map/psum | solution.py:331
  703.2 97.8 %copy-start.3 = (f32[1024,768]{1,0:T(8,128)S(1)}, f32[1024,768]{1,0:T(8,128)}, u32[]{:S(2)}) copy-start(f32[1024,768]{1,0:T(8,128)} %copy-done.2) | copy-start | bytes 9437188
  879.6 195.7 %all-reduce.31.cloned.1.call-start = ((), (), s32[]{:S(2)}) async-start(), calls=%async_computation.3 | async-start | bytes 6291456 | tf_op jit(solution)/shard_map/psum | solution.py:369
  937.1 11.5 collective-permute-start.4
  954.8 178.0 %all-reduce.33.cloned.1.call-start = ((), (), s32[]{:S(2)}) async-start(), calls=%async_computation.4 | async-start | bytes 174080 | tf_op jit(solution)/shard_map/psum | solution.py:455
  970.3 105.1 %copy-start.15 = (bf16[1024,768]{1,0:T(8,128)(2,1)S(1)}, bf16[1024,768]{1,0:T(8,128)(2,1)}, u32[]{:S(2)}) copy-start(bf16[1024,768]{1,0:T(8,128)(2,1)} %param.37) | copy-start | bytes 4718596
  970.3 105.1 %copy-start.132 = (f32[768]{0:T(1024)S(1)}, f32[768]{0:T(1024)}, u32[]{:S(2)}) copy-start(f32[768]{0:T(1024)} %copy-done.131) | copy-start | bytes 9220
  970.3 105.1 %copy-start.134 = (f32[1024]{0:T(1024)S(1)}, f32[1024]{0:T(1024)}, u32[]{:S(2)}) copy-start(f32[1024]{0:T(1024)} %copy-done.133) | copy-start | bytes 12292
  971.8 107.0 %copy-start.95 = (f32[1,768,256]{2,1,0:T(8,128)S(1)}, f32[1,768,256]{2,1,0:T(8,128)}, u32[]{:S(2)}) copy-start(f32[1,768,256]{2,1,0:T(8,128)} %convolution_bitcast_fusion.6) | copy-start | bytes 2359300
  971.8 107.0 %copy-start.96 = (f32[1,768,256]{2,1,0:T(8,128)S(1)}, f32[1,768,256]{2,1,0:T(8,128)}, u32[]{:S(2)}) copy-start(f32[1,768,256]{2,1,0:T(8,128)} %convolution_bitcast_fusion.7) | copy-start | bytes 2359300
  1078.8 191.3 %all-reduce.35.cloned.1.call-start = ((), (), s32[]{:S(2)}) async-start(), calls=%async_computation.5 | async-start | bytes 17301504 | tf_op jit(solution)/shard_map/psum | solution.py:455
  (239 other events, 1242.3 us)
Sparse Core Ops, SparseCore 0:
  161.5 121.3 all-reduce.24
  389.6 119.3 all-reduce.26
  605.2 50.6 all-reduce.38
  680.6 120.3 all-reduce.28
  879.8 50.8 all-reduce.36
  954.9 120.3 all-reduce.30
  1080.7 52.0 all-reduce.32
  1138.6 131.4 all-reduce.34
where the time goes:
time: 1300 us; the launch traced here: 1290 us
  waiting for transfers between devices  680 us (52%)
  other arithmetic  174 us (13%)
  local copies, waits for them, and re-layouts  159 us (12%)
  matrix products  138 us (11%)
  blocking collectives  107 us (8%)
  between operations  17.2 us (1%)
  starting transfers between devices  16.2 us (1%)
    psum x2, waiting for transfers between devices, backward_layer(): grad_normed = lax.psum(grad_normed, 'tensor')  199 us
    psum x2, waiting for transfers between devices, forward_layer(): branch, total_sq = lax.psum((partial_value, squares), 'tensor')  199 us
    psum x2, waiting for transfers between devices, local(): lax.psum((stacked[0], stacked[1], stacked[2], stacked[3], stacked[4], sta...  184 us
    all_gather x8, blocking collectives, entering(): everything = jax.tree.map(lambda part: lax.all_gather(part, axis), shard)  84 us
    psum x2, waiting for transfers between devices, backward_layer(): grad_write, grad_read = lax.psum((grad_write, grad_read), 'tensor')  81.9 us
    another operation x18, other arithmetic  47.2 us
    unnamed x528, local copies, waits for them, and re-layouts  41.9 us
    dot_general x10, matrix products, times_trans(): lax.dot_general(left, right, (((1,), (1,)), ((), ())), preferred_element_...  26.1 us
  transfers between devices with their start and end apart: 13, of which 10 were waited for; matrix products, arithmetic and copies ran while one was open for 12% of the time, Pallas kernels for 0%

commit v1 on v0

v1 whole, which is shorter than its diff:
```python
import functools

import jax
import jax.numpy as jnp
from jax import lax
from jax.experimental import pallas as pl
from jax.experimental.pallas import tpu as pltpu
from jax.sharding import PartitionSpec as P

CONV = 4
GROUP = 256
LAYERS = 2
INNER = 1536
EDGE = 8
LANES = 128


EPSILON = 1e-05
PRECISE = lax.Precision.HIGHEST
FLOAT = jnp.float32
BFLOAT = jnp.bfloat16
VMEM_BYTES = 56 * 1024 * 1024


def nn(left, right, precision=None):
    return lax.dot_general(
        left, right, (((1,), (0,)), ((), ())), precision=precision, preferred_element_type=FLOAT
    )


def nt(left, right, precision=None):
    return lax.dot_general(
        left, right, (((1,), (1,)), ((), ())), precision=precision, preferred_element_type=FLOAT
    )


def tn(left, right, precision=None):
    return lax.dot_general(
        left, right, (((0,), (0,)), ((), ())), precision=precision, preferred_element_type=FLOAT
    )


def sigmoid(value):
    return 1.0 / (1.0 + jnp.exp(-value))


def softplus(value):
    small = jnp.exp(-jnp.abs(value))
    series = small * (1.0 - small * (0.5 - small * (1.0 / 3.0 - small * 0.25)))
    return jnp.maximum(value, 0.0) + jnp.where(small < 0.01, series, jnp.log(1.0 + small))


def silu_slope(value):
    sigma = sigmoid(value)
    return sigma * (1.0 + value * (1.0 - sigma))


def spread_matrix(lane_count, heads):
    size = lane_count // heads
    head = lax.broadcasted_iota(jnp.int32, (LANES, lane_count), 0)
    lane = lax.broadcasted_iota(jnp.int32, (LANES, lane_count), 1)
    return jnp.where((lane >= head * size) & (lane < (head + 1) * size), 1.0, 0.0).astype(FLOAT)


def triangle(span, upper):
    row = lax.broadcasted_iota(jnp.int32, (span, span), 0)
    col = lax.broadcasted_iota(jnp.int32, (span, span), 1)
    return jnp.where(col >= row if upper else col <= row, 1.0, 0.0).astype(FLOAT)


def within_block(seg_col, seg_row):
    span = seg_col.shape[0]
    row = lax.broadcasted_iota(jnp.int32, (span, span), 0)
    col = lax.broadcasted_iota(jnp.int32, (span, span), 1)
    return (row >= col) & (seg_col == seg_row)


def call(body, grid, inputs, outputs, scratch=(), reverse=False, flops=0):
    def place(b):
        return grid - 1 - b if reverse else b

    def spec_of(shape, kind):
        if isinstance(kind, pl.BlockSpec):
            return kind
        if kind == "smem":
            return pl.BlockSpec(memory_space=pltpu.SMEM)
        if kind == "rows":
            return pl.BlockSpec((shape[0] // grid, shape[1]), lambda b: (place(b), 0))
        if kind == "lead":
            return pl.BlockSpec((None,) + tuple(shape[1:]), lambda b: (place(b),) + (0,) * (len(shape) - 1))
        return pl.BlockSpec(tuple(shape), lambda b: (0,) * len(shape))

    moved = sum(a.size * a.dtype.itemsize for a, _ in inputs)
    return pl.pallas_call(
        body,
        grid=(grid,),
        in_specs=[spec_of(a.shape, kind) for a, kind in inputs],
        out_specs=[spec_of(shape, kind) for shape, _, kind in outputs],
        out_shape=[jax.ShapeDtypeStruct(shape, dtype) for shape, dtype, _ in outputs],
        scratch_shapes=list(scratch),
        compiler_params=pltpu.CompilerParams(
            dimension_semantics=("arbitrary",), vmem_limit_bytes=VMEM_BYTES
        ),
        cost_estimate=pl.CostEstimate(flops=int(flops), bytes_accessed=int(2 * moved), transcendentals=0),
    )(*[a for a, _ in inputs])


def project_kernel(
    resid, halo, gain, gate_w, value_w, state_w, step_w, filt, off, bias, rate, meta,
    normed_o, gate_o, pre_o, pre_halo_o, conv_o, vals_o, wr_o, shifted_o, cum_o, local_o, retain_o, pay_o,
    ext, state,
):
    b = pl.program_id(0)
    span = resid.shape[0]
    lanes = value_w.shape[1]
    heads_rows = state.shape[0]

    def normalise(x):
        x = x.astype(FLOAT)
        inv = lax.rsqrt(jnp.mean(x * x, axis=1, keepdims=True) + EPSILON)
        return (x * inv * gain[...]).astype(BFLOAT)

    @pl.when(b == 0)
    def _():
        edge = normalise(halo[...])
        edge_pre = jnp.concatenate([nn(edge, value_w[...]), nn(edge, state_w[...])], axis=1)
        ext[0:EDGE] = edge_pre
        pre_halo_o[...] = edge_pre
        state[...] = jnp.zeros_like(state)

    @pl.when(b > 0)
    def _():
        ext[0:EDGE] = ext[span : span + EDGE]

    normed = normalise(resid[...])
    normed_o[...] = normed
    gate_o[...] = nn(normed, gate_w[...])
    ext[EDGE : span + EDGE, 0:lanes] = nn(normed, value_w[...])
    ext[EDGE : span + EDGE, lanes:] = nn(normed, state_w[...])
    pre = ext[EDGE : span + EDGE]
    pre_o[...] = pre
    conv_sum = off[...] + filt[CONV - 1 : CONV] * pre
    for k in range(CONV - 1):
        at = EDGE - (CONV - 1) + k
        conv_sum = conv_sum + filt[k : k + 1] * (ext[at : at + span] * meta[:, k : k + 1])
    conv_o[...] = conv_sum
    activated = conv_sum * sigmoid(conv_sum)
    vals = activated[:, :lanes].astype(BFLOAT)
    write_read = activated[:, lanes:].astype(BFLOAT)
    vals_o[...] = vals
    wr_o[...] = write_read
    write = write_read[:, : write_read.shape[1] // 2]

    shifted = nn(normed, step_w[...]) + bias[...]
    shifted_o[...] = shifted
    steps = softplus(shifted)
    log_decay = -rate[...] * steps
    cum = nn(triangle(span, False), log_decay, PRECISE)
    cum_o[...] = cum
    last = cum[span - 1 : span]
    tail_step = meta[:, 4:5] * jnp.exp(last - cum) * steps
    heads = HEADS_OF(lanes)
    spread = spread_matrix(lanes, heads)
    weight = nn(tail_step, spread, PRECISE)
    local = tn((weight * vals.astype(FLOAT)).astype(BFLOAT), write)
    retain = meta[span - 1 : span, 3:4] * jnp.exp(last)
    retain_o[...] = jnp.broadcast_to(retain, retain_o.shape)
    size = heads_rows // heads
    local_o[...] = state[...]

    @pl.when(b == 0)
    def _():
        pay_o[heads_rows:] = jnp.ones_like(pay_o[heads_rows:])

    for h in range(heads):
        rows = slice(h * size, (h + 1) * size)
        state[rows] = retain[:, h : h + 1] * state[rows] + local[rows]
    pay_o[0:heads_rows] = state[...]
    pay_o[heads_rows:] = pay_o[heads_rows:] * retain


def HEADS_OF(lanes):
    return lanes // 64


def inside_kernel(vals, wr, cum, shifted, meta, seg_row, y_o):
    lanes = vals.shape[1]
    heads = HEADS_OF(lanes)
    size = lanes // heads
    half = wr.shape[1] // 2
    mask = within_block(meta[:, 5:6], seg_row[...])
    mixed = jnp.where(mask, nt(wr[:, half:], wr[:, :half]), 0.0)
    cum_v = cum[...]
    cum_t = cum_v.T
    step_t = softplus(shifted[...]).T
    for h in range(heads):
        gap = jnp.where(mask, cum_v[:, h : h + 1] - cum_t[h : h + 1, :], 0.0)
        mixing = (mixed * jnp.exp(gap) * step_t[h : h + 1, :]).astype(BFLOAT)
        y_o[:, h * size : (h + 1) * size] = nn(mixing, vals[:, h * size : (h + 1) * size])


def fold_in(me, count, payload, acc, reverse, heads):
    rows = acc.shape[0]
    size = rows // heads
    acc[...] = jnp.zeros_like(acc)
    for k in range(count):
        at = count - 1 - k if reverse else k
        reached = at > me if reverse else at < me

        @pl.when(reached)
        def _():
            keep = payload[at, rows : rows + 1]
            for h in range(heads):
                part = slice(h * size, (h + 1) * size)
                acc[part] = keep[:, h : h + 1] * acc[part] + payload[at, part]


def gated_kernel(
    me, payload, local, retain, y, wr, vals, cum, meta, gate, skip, gain, out_w, *rest, last_layer
):
    if last_layer:
        cot, ssm_o, states_o, partial_o, sq_o, dot_o, acc = rest
    else:
        ssm_o, states_o, partial_o, sq_o, acc = rest
    b = pl.program_id(0)
    lanes = vals.shape[1]
    heads = HEADS_OF(lanes)
    rows = acc.shape[0]
    size = rows // heads
    half = wr.shape[1] // 2

    @pl.when(b == 0)
    def _():
        fold_in(me[0], payload.shape[0], payload, acc, False, heads)

    states = local[...] + acc[...]
    states_o[...] = states
    for h in range(heads):
        part = slice(h * size, (h + 1) * size)
        acc[part] = retain[0:1, h : h + 1] * acc[part]
    enter = meta[:, 3:4] * jnp.exp(cum[...])
    enter_lanes = nn(enter, spread_matrix(lanes, heads), PRECISE)
    carried = nt(wr[:, half:], states.astype(BFLOAT)) * enter_lanes
    ssm = y[...] + carried + skip[...] * vals[...].astype(FLOAT)
    ssm_o[...] = ssm
    gate_v = gate[...]
    gated = ssm * (gate_v * sigmoid(gate_v))
    partial = nn((gated * gain[...]).astype(BFLOAT), out_w[...])
    partial_o[...] = partial
    ones = jnp.ones((8, lanes), FLOAT)
    sq_o[...] = nt(ones, gated * gated, PRECISE)[0:1]
    if last_layer:
        ones = jnp.ones((8, partial.shape[1]), FLOAT)
        dot_o[...] = nt(ones, partial * cot[...].astype(FLOAT), PRECISE)[0:1]


def ungate_kernel(
    upstream, cols, out_w, gain, gate, ssm, vals, wr, cum, meta, retain,
    grad_ssm_o, gate_low_o, grad_out_w_o, small_o, later_o, pay_o,
    state,
):
    b = pl.program_id(0)
    lanes = vals.shape[1]
    heads = HEADS_OF(lanes)
    rows = state.shape[0]
    size = rows // heads
    half = wr.shape[1] // 2

    @pl.when(b == 0)
    def _():
        state[...] = jnp.zeros_like(state)
        grad_out_w_o[...] = jnp.zeros_like(grad_out_w_o)
        small_o[...] = jnp.zeros_like(small_o)
        pay_o[rows:] = jnp.ones_like(pay_o[rows:])

    inv_norm = cols[:, 0:1]
    grad_branch = (inv_norm * upstream[...].astype(FLOAT)).astype(BFLOAT)
    gate_v = gate[...]
    sigma = sigmoid(gate_v)
    gate_act = gate_v * sigma
    ssm_v = ssm[...]
    gated = ssm_v * gate_act
    out_in = (gated * gain[...]).astype(BFLOAT)
    grad_out_w_o[...] += tn(out_in, grad_branch)
    grad_out_in = nt(grad_branch, out_w[...])
    small_o[0:1] += jnp.sum(grad_out_in * gated, axis=0, keepdims=True)
    grad_gated = grad_out_in * gain[...] - (cols[:, 1:2] * inv_norm * inv_norm * inv_norm / INNER) * gated
    grad_ssm = (grad_gated * gate_act).astype(BFLOAT)
    grad_ssm_o[...] = grad_ssm
    gate_low_o[...] = (grad_gated * ssm_v * (sigma * (1.0 + gate_v * (1.0 - sigma)))).astype(BFLOAT)
    grad_wide = grad_ssm.astype(FLOAT)
    small_o[1:2] += jnp.sum(grad_wide * vals[...].astype(FLOAT), axis=0, keepdims=True)
    enter = meta[:, 3:4] * jnp.exp(cum[...])
    enter_lanes = nn(enter, spread_matrix(lanes, heads), PRECISE)
    pulls = tn((enter_lanes * grad_wide).astype(BFLOAT), wr[:, half:])
    later_o[...] = state[...]
    keep = retain[0:1]
    for h in range(heads):
        part = slice(h * size, (h + 1) * size)
        state[part] = keep[:, h : h + 1] * state[part] + pulls[part]
    pay_o[0:rows] = state[...]
    pay_o[rows:] = pay_o[rows:] * keep


def unmix_kernel(
    me, payload, later, retain, grad_ssm, vals, wr, cum, shifted, meta, seg_row, states, conv, pre, before, pre_halo,
    filt, rate, skip,
    low_o, edge_o, step_low_o, spill_o, small_o, small2_o,
    acc, flows, ext,
):
    b = pl.program_id(0)
    blocks = pl.num_programs(0)
    span, lanes = vals.shape
    heads = HEADS_OF(lanes)
    rows = acc.shape[0]
    size = rows // heads
    half = wr.shape[1] // 2
    write, read = wr[:, :half], wr[:, half:]

    @pl.when(b == 0)
    def _():
        fold_in(me[0], payload.shape[0], payload, acc, True, heads)
        small_o[...] = jnp.zeros_like(small_o)
        small2_o[...] = jnp.zeros_like(small2_o)
        for k in range(CONV - 1):
            ext[k, span:] = jnp.zeros_like(ext[k, span:])

    @pl.when(b > 0)
    def _():
        for k in range(CONV - 1):
            ext[k, span:] = ext[k, 0:EDGE]

    grad_next = later[...] + acc[...]
    keep = retain[0:1]
    states_v = states[...]
    spread = spread_matrix(lanes, heads)
    meet = jnp.sum(grad_next * states_v, axis=1, keepdims=True)
    grad_retain = tn(jnp.broadcast_to(meet, (rows, LANES)) * spread.T, jnp.ones((rows, 8), FLOAT), PRECISE)
    grad_retain = grad_retain.T[0:1]
    for h in range(heads):
        part = slice(h * size, (h + 1) * size)
        acc[part] = keep[:, h : h + 1] * acc[part]

    cum_v = cum[...]
    cum_t = cum_v.T
    shifted_v = shifted[...]
    steps = softplus(shifted_v)
    step_t = steps.T
    seg_mask = within_block(meta[:, 5:6], seg_row[...])
    inter = jnp.where(seg_mask, nt(read, write), 0.0)
    grad_inter = jnp.zeros((span, span), FLOAT)
    flows[...] = jnp.zeros_like(flows)
    parts = []
    row_sums = jnp.zeros((span, LANES), FLOAT)
    lane_no = lax.broadcasted_iota(jnp.int32, (span, LANES), 1)
    for h in range(heads):
        part = slice(h * size, (h + 1) * size)
        decay = jnp.exp(jnp.where(seg_mask, cum_v[:, h : h + 1] - cum_t[h : h + 1, :], 0.0))
        decay_inter = decay * inter
        step_h = step_t[h : h + 1, :]
        mixing = (decay_inter * step_h).astype(BFLOAT)
        grad_h = grad_ssm[:, part]
        parts.append(tn(mixing, grad_h))
        pairing = nt(grad_h, vals[:, part])
        grad_inter = grad_inter + pairing * decay * step_h
        weighted = pairing * decay_inter
        col = jnp.sum(weighted, axis=0, keepdims=True)
        flows[h : h + 1, :] = col
        row_sums = row_sums + jnp.where(
            lane_no == h, jnp.sum(weighted * step_h, axis=1, keepdims=True), 0.0
        )
    grad_vals = jnp.concatenate(parts, axis=1)
    grad_steps = flows[...].T
    grad_cum = row_sums - grad_steps * steps
    grad_inter = jnp.where(seg_mask, grad_inter, 0.0).astype(BFLOAT)
    grad_read = nn(grad_inter, write)
    grad_write = tn(grad_inter, read)

    vals_f = vals[...].astype(FLOAT)
    grad_f = grad_ssm[...].astype(FLOAT)
    enter = meta[:, 3:4] * jnp.exp(cum_v)
    enter_lanes = nn(enter, spread, PRECISE)
    states_low = states_v.astype(BFLOAT)
    grad_read = grad_read + nn((enter_lanes * grad_f).astype(BFLOAT), states_low)
    out_of = nt(read, states_low)
    grad_cum = grad_cum + enter * nt(grad_f * out_of, spread, PRECISE)
    next_low = grad_next.astype(BFLOAT)
    along = nt(write, next_low)
    last = cum_v[span - 1 : span]
    tail = meta[:, 4:5] * jnp.exp(last - cum_v)
    tail_step = tail * steps
    tail_lanes = nn(tail_step, spread, PRECISE)
    grad_vals = grad_vals + tail_lanes * along + skip[...] * grad_f
    grad_write = grad_write + nn((tail_lanes * vals_f).astype(BFLOAT), next_low)
    reach = nt(vals_f * along, spread, PRECISE)
    grad_steps = grad_steps + tail * reach
    tail_flow = tail_step * reach
    grad_last = jnp.sum(tail_flow, axis=0, keepdims=True) + grad_retain * keep
    grad_log = nn(triangle(span, True), grad_cum - tail_flow, PRECISE) + grad_last
    rate_v = rate[...]
    log_decay = -rate_v * steps
    small2_o[0:1] += jnp.sum(grad_log * log_decay, axis=0, keepdims=True)
    grad_shifted = (grad_steps - rate_v * grad_log) * sigmoid(shifted_v)
    small2_o[1:2] += jnp.sum(grad_shifted, axis=0, keepdims=True)
    step_low_o[...] = grad_shifted.astype(BFLOAT)

    grad_conv = jnp.concatenate([grad_vals, grad_write, grad_read], axis=1) * silu_slope(conv[...])
    small_o[CONV : CONV + 1] += jnp.sum(grad_conv, axis=0, keepdims=True)
    pre_v = pre[...]
    small_o[CONV - 1 : CONV] += jnp.sum(grad_conv * pre_v, axis=0, keepdims=True)
    grad_pre = filt[CONV - 1 : CONV] * grad_conv
    first = blocks - 1 - b == 0
    for k in range(CONV - 1):
        lag = CONV - 1 - k
        masked = grad_conv * meta[:, k : k + 1]
        ext[k, 0:span] = masked
        ahead = ext[k, lag : lag + span]
        row_no = lax.broadcasted_iota(jnp.int32, (span, 1), 0)
        own = jnp.where(row_no < span - lag, ahead, 0.0)
        edge = jnp.where(first, pre_halo[...], before[...])
        head_rows = ext[k, 0:EDGE]
        edge_sum = jnp.zeros((1, head_rows.shape[1]), FLOAT)
        for t in range(lag):
            edge_sum = edge_sum + head_rows[t : t + 1] * edge[EDGE - lag + t : EDGE - lag + t + 1]
        small_o[k : k + 1] += jnp.sum(own * pre_v, axis=0, keepdims=True) + edge_sum
        grad_pre = grad_pre + filt[k : k + 1] * ahead
    low_o[...] = grad_pre.astype(BFLOAT)

    @pl.when(b == 0)
    def _():
        edge_o[...] = grad_pre[span - EDGE :]

    spill_o[...] = jnp.zeros_like(spill_o)
    for k in range(CONV - 1):
        lag = CONV - 1 - k
        for t in range(lag):
            at = EDGE - lag + t
            spill_o[at : at + 1] += filt[k : k + 1] * ext[k, t : t + 1]


def weights_kernel(
    normed, low, edge, spill, gate_low, step_low, gate_w, value_w, state_w, step_w,
    grad_normed_o, gate_o, value_o, state_o, step_o,
):
    b = pl.program_id(0)
    blocks = pl.num_programs(0)
    span = low.shape[0]
    lanes = value_w.shape[1]

    @pl.when(b == 0)
    def _():
        gate_o[...] = jnp.zeros_like(gate_o)
        value_o[...] = jnp.zeros_like(value_o)
        state_o[...] = jnp.zeros_like(state_o)
        step_o[...] = jnp.zeros_like(step_o)

    patch = (edge[...] + spill[...]).astype(FLOAT)
    padded = jnp.concatenate([jnp.zeros((span - EDGE, patch.shape[1]), FLOAT), patch], axis=0)
    row_no = lax.broadcasted_iota(jnp.int32, (span, 1), 0)
    use = (row_no >= span - EDGE) & (b == blocks - 1)
    low_v = jnp.where(use, padded, low[...].astype(FLOAT)).astype(BFLOAT)
    value_low, state_low = low_v[:, :lanes], low_v[:, lanes:]
    normed_v = normed[...]
    gate_o[...] += tn(normed_v, gate_low[...])
    value_o[...] += tn(normed_v, value_low)
    state_o[...] += tn(normed_v, state_low)
    step_o[...] += tn(normed_v, step_low[...])
    grad_normed_o[...] = (
        nt(gate_low[...], gate_w[...])
        + nt(value_low, value_w[...])
        + nt(state_low, state_w[...])
        + nt(step_low[...], step_w[...])
    )


def passed_along(shard, axis, by):
    count = lax.axis_size(axis)
    pairs = [(i, i + by) for i in range(count) if 0 <= i + by < count]
    return lax.ppermute(shard, axis, pairs)


def pad_lanes(array):
    return jnp.pad(array, ((0, 0), (0, LANES - array.shape[1])))


def prepare(params):
    (
        gain_in, gate_w, value_w, state_w, step_w, value_filt, value_off, state_filt, state_off,
        bias_step, decay_param, skip_param, gain_out, out_w,
    ) = params
    heads = step_w.shape[1]
    size = value_w.shape[1] // heads
    filt = jnp.concatenate([value_filt, state_filt], axis=1)
    return dict(
        gain=gain_in[None],
        gate_w=gate_w,
        value_w=value_w,
        state_w=state_w,
        step_w=pad_lanes(step_w),
        filt=jnp.pad(filt, ((0, 8 - CONV), (0, 0))),
        off=jnp.concatenate([value_off, state_off])[None],
        bias=pad_lanes(bias_step[None]),
        rate=pad_lanes(jnp.exp(decay_param)[None]),
        skip=jnp.repeat(skip_param, size)[None],
        gain_out=gain_out[None],
        out_w=out_w,
    )


def forward_layer(resid, halo, w, geometry, me, cot):
    meta, seg_row = geometry
    n, d = resid.shape
    grid = n // GROUP
    lanes = w["value_w"].shape[1]
    chans = lanes + w["state_w"].shape[1]
    state = w["state_w"].shape[1] // 2
    pay = (lanes + 8, state)
    normed, gate, pre, pre_halo, conv, vals, wr, shifted, cum, local, retain, payload = call(
        project_kernel, grid,
        [
            (resid, "rows"), (halo, "whole"), (w["gain"], "whole"), (w["gate_w"], "whole"),
            (w["value_w"], "whole"), (w["state_w"], "whole"), (w["step_w"], "whole"), (w["filt"], "whole"),
            (w["off"], "whole"), (w["bias"], "whole"), (w["rate"], "whole"), (meta, "rows"),
        ],
        [
            ((n, d), BFLOAT, "rows"), ((n, lanes), FLOAT, "rows"), ((n, chans), FLOAT, "rows"),
            ((EDGE, chans), FLOAT, "whole"), ((n, chans), FLOAT, "rows"), ((n, lanes), BFLOAT, "rows"),
            ((n, chans - lanes), BFLOAT, "rows"), ((n, LANES), FLOAT, "rows"), ((n, LANES), FLOAT, "rows"),
            ((grid, lanes, state), FLOAT, "lead"), ((grid, 8, LANES), FLOAT, "lead"), (pay, FLOAT, "whole"),
        ],
        [pltpu.VMEM((GROUP + EDGE, chans), FLOAT), pltpu.VMEM((lanes, state), FLOAT)],
        flops=2 * n * d * (lanes + chans),
    )
    everything = lax.all_gather(payload, "ctx")
    (y,) = call(
        inside_kernel, grid,
        [(vals, "rows"), (wr, "rows"), (cum, "rows"), (shifted, "rows"), (meta, "rows"), (seg_row, "lead")],
        [((n, lanes), FLOAT, "rows")],
        flops=4 * n * GROUP * lanes,
    )
    row = ((grid, 1, GROUP), FLOAT, "lead")
    outs = call(
        functools.partial(gated_kernel, last_layer=cot is not None), grid,
        [
            (me, "smem"), (everything, "whole"), (local, "lead"), (retain, "lead"), (y, "rows"), (wr, "rows"),
            (vals, "rows"), (cum, "rows"), (meta, "rows"), (gate, "rows"), (w["skip"], "whole"),
            (w["gain_out"], "whole"), (w["out_w"], "whole"),
        ] + ([(cot, "rows")] if cot is not None else []),
        [
            ((n, lanes), FLOAT, "rows"), ((grid, lanes, state), FLOAT, "lead"), ((n, d), FLOAT, "rows"), row,
        ] + ([row] if cot is not None else []),
        [pltpu.VMEM((lanes, state), FLOAT)],
        flops=2 * n * d * lanes,
    )
    ssm, states = outs[0], outs[1]
    saved = (normed, gate, pre, pre_halo, conv, vals, wr, shifted, cum, retain, ssm, states)
    return outs[2:], saved


def backward_layer(upstream, cols, w, saved, geometry, me):
    meta, seg_row = geometry
    normed, gate, pre, pre_halo, conv, vals, wr, shifted, cum, retain, ssm, states = saved
    n, d = upstream.shape
    grid = n // GROUP
    lanes = vals.shape[1]
    chans = pre.shape[1]
    state = wr.shape[1] // 2
    pay = (lanes + 8, state)
    grad_ssm, gate_low, grad_out_w, small, later, payload = call(
        ungate_kernel, grid,
        [
            (upstream, "rows"), (cols, "rows"), (w["out_w"], "whole"), (w["gain_out"], "whole"), (gate, "rows"),
            (ssm, "rows"), (vals, "rows"), (wr, "rows"), (cum, "rows"), (meta, "rows"), (retain, "lead"),
        ],
        [
            ((n, lanes), BFLOAT, "rows"), ((n, lanes), BFLOAT, "rows"), ((lanes, d), FLOAT, "whole"),
            ((8, lanes), FLOAT, "whole"), ((grid, lanes, state), FLOAT, "lead"), (pay, FLOAT, "whole"),
        ],
        [pltpu.VMEM((lanes, state), FLOAT)],
        reverse=True,
        flops=4 * n * d * lanes,
    )
    everything = lax.all_gather(payload, "ctx")
    strip = GROUP // EDGE
    before = pl.BlockSpec((EDGE, chans), lambda b: (jnp.maximum((grid - 1 - b) * strip - 1, 0), 0))
    low, edge, step_low, spill, small_c, small_h = call(
        unmix_kernel, grid,
        [
            (me, "smem"), (everything, "whole"), (later, "lead"), (retain, "lead"), (grad_ssm, "rows"),
            (vals, "rows"), (wr, "rows"), (cum, "rows"), (shifted, "rows"), (meta, "rows"), (seg_row, "lead"),
            (states, "lead"), (conv, "rows"), (pre, "rows"), (pre, before), (pre_halo, "whole"),
            (w["filt"], "whole"), (w["rate"], "whole"), (w["skip"], "whole"),
        ],
        [
            ((n, chans), BFLOAT, "rows"), ((EDGE, chans), FLOAT, "whole"), ((n, LANES), BFLOAT, "rows"),
            ((EDGE, chans), FLOAT, "whole"), ((8, chans), FLOAT, "whole"), ((8, LANES), FLOAT, "whole"),
        ],
        [
            pltpu.VMEM((lanes, state), FLOAT), pltpu.VMEM((LANES, GROUP), FLOAT),
            pltpu.VMEM((CONV - 1, GROUP + EDGE, chans), FLOAT),
        ],
        reverse=True,
        flops=12 * n * GROUP * lanes,
    )
    spill = passed_along(spill, "ctx", -1)
    grad_normed, grad_gate_w, grad_value_w, grad_state_w, grad_step_w = call(
        weights_kernel, grid,
        [
            (normed, "rows"), (low, "rows"), (edge, "whole"), (spill, "whole"), (gate_low, "rows"),
            (step_low, "rows"), (w["gate_w"], "whole"), (w["value_w"], "whole"), (w["state_w"], "whole"),
            (w["step_w"], "whole"),
        ],
        [
            ((n, d), FLOAT, "rows"), ((d, lanes), FLOAT, "whole"), ((d, lanes), FLOAT, "whole"),
            ((d, chans - lanes), FLOAT, "whole"), ((d, LANES), FLOAT, "whole"),
        ],
        flops=4 * n * d * (lanes + chans),
    )
    heads = HEADS_OF(lanes)
    grads = dict(
        gate=grad_gate_w,
        value=grad_value_w,
        state=grad_state_w,
        step=grad_step_w[:, :heads],
        value_filter=small_c[:CONV, :lanes],
        value_offset=small_c[CONV, :lanes],
        state_filter=small_c[:CONV, lanes:],
        state_offset=small_c[CONV, lanes:],
        bias=small_h[1, :heads],
        decay=small_h[0, :heads],
        skip=jnp.sum(small[1].reshape(heads, -1), axis=1),
        gain_out=small[0],
        out=grad_out_w,
    )
    return grad_normed, grads


def total_over(grads, gain_in):
    every = ("dp", "ctx", "tensor")
    wide = lax.psum((grads["gate"], grads["value"], grads["out"]), ("dp", "ctx"))
    state = lax.psum((grads["state"], grads["state_filter"], grads["state_offset"]), every)
    rest = ("step", "value_filter", "value_offset", "bias", "decay", "skip", "gain_out")
    others = lax.psum((gain_in,) + tuple(grads[name] for name in rest), ("dp", "ctx"))
    return (
        others[0], wide[0], wide[1], state[0], others[1], others[2], others[3], state[1], state[2],
        others[4], others[5], others[6], others[7], wide[2],
    )


def local(tokens, segments, *rest):
    params, cotangent = rest[:-1], rest[-1]
    n = tokens.shape[0]
    me = lax.axis_index("ctx").astype(jnp.int32).reshape(1)
    halo = passed_along(tokens[n - EDGE :].astype(FLOAT), "ctx", 1)
    halo_seg = passed_along(segments[n - EDGE :], "ctx", 1)
    seg_ext = jnp.concatenate([halo_seg, segments])
    seg_blocks = segments.reshape(-1, GROUP)
    seg_before = jnp.concatenate([halo_seg[EDGE - 1 :], seg_blocks[:-1, -1]])
    first = EDGE - (CONV - 1)
    columns = [seg_ext[first + k : first + k + n] == segments for k in range(CONV - 1)]
    columns.append((seg_blocks == seg_before[:, None]).reshape(n))
    columns.append((seg_blocks == seg_blocks[:, -1:]).reshape(n))
    columns.append(segments)
    columns += [jnp.zeros_like(segments)] * (8 - len(columns))
    meta = jnp.stack([column.astype(FLOAT) for column in columns], axis=1)
    geometry = (meta, segments.astype(FLOAT).reshape(-1, 1, GROUP))
    weights = [prepare(tuple(param[depth] for param in params)) for depth in range(LAYERS)]

    resid = tokens.astype(FLOAT)
    entering, saved_all, norms = [resid], [], []
    for depth in range(LAYERS - 1):
        (partial, squares), saved = forward_layer(resid, halo, weights[depth], geometry, me, None)
        saved_all.append(saved)
        branch, total_sq = lax.psum((partial, squares.reshape(n)), "tensor")
        inv_norm = lax.rsqrt(total_sq / INNER + EPSILON)[:, None]
        norms.append((inv_norm, branch))
        resid = resid + inv_norm * branch
        entering.append(resid)
        halo = passed_along(resid[n - EDGE :], "ctx", 1)
    (partial, squares, dots), saved = forward_layer(
        resid, halo, weights[LAYERS - 1], geometry, me, cotangent
    )
    saved_all.append(saved)
    total_sq, grad_inv = lax.psum((squares, dots), "tensor")
    inv_norm = lax.rsqrt(total_sq.reshape(n) / INNER + EPSILON)[:, None]
    grad_inv = grad_inv.reshape(n)[:, None]
    branch = lax.psum(partial, "tensor")
    mixed = (resid + inv_norm * branch).astype(BFLOAT)

    upstream = cotangent.astype(FLOAT)
    layer_grads = [None] * LAYERS
    for depth in range(LAYERS - 1, -1, -1):
        if depth < LAYERS - 1:
            inv_norm, branch = norms[depth]
            grad_inv = jnp.sum(upstream * branch, axis=1, keepdims=True)
        cols = jnp.concatenate([inv_norm, grad_inv, jnp.zeros((n, 6), FLOAT)], axis=1)
        grad_normed, grads = backward_layer(upstream, cols, weights[depth], saved_all[depth], geometry, me)
        grad_normed = lax.psum(grad_normed, "tensor")
        x = entering[depth]
        inv_rms = lax.rsqrt(jnp.mean(x * x, axis=1, keepdims=True) + EPSILON)
        scaled = x * inv_rms
        gain_grad = jnp.sum(grad_normed * scaled, axis=0)
        inner = grad_normed * weights[depth]["gain"]
        upstream = upstream + inv_rms * (inner - scaled * jnp.mean(inner * scaled, axis=1, keepdims=True))
        layer_grads[depth] = total_over(grads, gain_grad)
    stacked = [jnp.stack([layer_grads[depth][i] for depth in range(LAYERS)]) for i in range(14)]
    return (mixed, upstream.astype(BFLOAT), *stacked)


def solution(mesh):
    split = P(None, None, "tensor")
    lane = P(None, "tensor")
    rows = P(("dp", "ctx"), None)
    weights = (P(), split, split, P(), split, split, lane, P(), P(), lane, lane, lane, lane, P(None, "tensor", None))
    return jax.shard_map(
        local,
        mesh=mesh,
        in_specs=(rows, P(("dp", "ctx")), *weights, rows),
        out_specs=(rows, rows, *weights),
        check_vma=False,
    )
```

time: 1300 us -> 1090 us (0.84)
  Pallas kernels: 0 us -> 141 us
  matrix products: 138 us -> 0 us
  other arithmetic: 174 us -> 51 us
  local copies, waits for them, and re-layouts: 159 us -> 56.3 us
  blocking collectives: 107 us -> 157 us
  waiting for transfers between devices: 680 us -> 640 us
    pallas_call x0 -> x12, Pallas kernels: none -> 141 us  [call(): pl.pallas_call(body, grid=(grid,), in_specs=[spec_of(a.shape, kind) for a...]
    dot_general x54 -> x0, matrix products: 138 us -> none  [the longest x10 26.1 us: times_trans(): lax.dot_general(left, right, (((1,), (1,)), ((), ())), preferred_element_...]
    psum x2 -> x4, blocking collectives: 23.4 us -> 105 us  [the longest x1 43.3 us: total_over(): lax.psum((gain_in,) + tuple((grads[name] for name in rest)), ('dp', 'ctx'))]
    another operation x40 -> x15, other arithmetic: 62.7 us -> 17.2 us  [the longest x14 16.4 us: local(): jnp.stack([layer_grads[depth][i] for depth in range(LAYERS)])]
    reshape x24 -> x1, local copies, waits for them, and re-layouts: 36.6 us -> 0.7 us  [local(): seg_blocks = segments.reshape(-1, GROUP)]
    unnamed x528 -> x106, local copies, waits for them, and re-layouts: 41.9 us -> 6.83 us
    psum x8 -> x5, waiting for transfers between devices: 664 us -> 630 us  [the longest x1 218 us: local(): branch = lax.psum(partial, 'tensor')]
    all_gather x8 -> x4, blocking collectives: 84 us -> 51.9 us  [the longest x2 27.3 us: backward_layer(): everything = lax.all_gather(payload, 'ctx')]
  transfers between devices with their start and end apart: 13 -> 10, of which waited for: 10 -> 7; matrix products, arithmetic and copies ran while one was open for 12% -> 7% of each run, Pallas kernels for 0% -> 0%
where the time goes in v1:
time: 1090 us; the launch traced here: 1080 us
  waiting for transfers between devices  640 us (59%)
  blocking collectives  157 us (14%)
  Pallas kernels  141 us (13%)
  local copies, waits for them, and re-layouts  56.3 us (5%)
  other arithmetic  51 us (5%)
  starting transfers between devices  15.2 us (1%)
  between operations  14.7 us (1%)
    psum x1, waiting for transfers between devices, local(): branch = lax.psum(partial, 'tensor')  218 us
    pallas_call x12, Pallas kernels, call(): pl.pallas_call(body, grid=(grid,), in_specs=[spec_of(a.shape, kind) for a...  141 us
    psum x1, waiting for transfers between devices, local(): grad_normed = lax.psum(grad_normed, 'tensor')  119 us
    psum x1, waiting for transfers between devices, total_over(): lax.psum((grads['gate'], grads['value'], grads['out']), ('dp', 'ctx'))  115 us
    psum x1, waiting for transfers between devices, local(): branch, total_sq = lax.psum((partial, squares.reshape(n)), 'tensor')  108 us
    psum x1, waiting for transfers between devices, total_over(): lax.psum((grads['state'], grads['state_filter'], grads['state_offset']),...  69.7 us
    psum x1, blocking collectives, total_over(): lax.psum((gain_in,) + tuple((grads[name] for name in rest)), ('dp', 'ctx'))  43.3 us
    psum x1, blocking collectives, total_over(): lax.psum((grads['state'], grads['state_filter'], grads['state_offset']),...  39.1 us
  transfers between devices with their start and end apart: 10, of which 7 were waited for; matrix products, arithmetic and copies ran while one was open for 7% of the time, Pallas kernels for 0%

profile of v1, /device:TPU:0, one launch (start us, length us, event | category | flops | bytes accessed | tf_op | source)
XLA Modules:
  0.0 1075.9 jit_solution(17399599328340597075)
XLA Ops:
  51.3 13.8 %shard_map.288 = (bf16[1024,768]{1,0:T(8,128)(2,1)}, f32[1024,384]{1,0:T(8,128)}, f32[1024,640]{1,0:T(8,128)}, f32[8,640]{1,0:T(8,128)}, f32[1024,640]{1,0:T(8,1...) custom-call(f32[1024,768]{1,0:T(8,128)} %convert_element_type.35.res, ...), custom_call_target="tpu_custom_call" | custom-call | flops 1610612736 | bytes 9999360 | tf_op jit(solution)/shard_map/pallas_call | solution.py:94
  65.2 12.1 %all-gather = f32[1568,128]{1,0:T(8,128)} all-gather(f32[392,128]{1,0:T(8,128)} %get-tuple-element.83), channel_id=2, replica_groups=mesh['dp'=2,'ctx'=4,'tensor'=4] {'ctx'}, dimensions={0}, use_global_device_ids=true | all-gather | bytes 1003520 | tf_op jit(solution)/shard_map/all_gather | solution.py:534
  83.1 9.2 shard_map.290
  93.6 12.3 %psum.245 = f32[1024]{0:T(1024)S(1)} all-reduce(f32[1024]{0:T(1024)S(1)} %bitcast.108), channel_id=1, replica_groups=mesh['dp'=2,'ctx'=4,'tensor'=4] {'tensor'}, use_global_device_ids=true, to_apply=%region_0.1 | all-reduce | flops 1024 | bytes 8192 | tf_op jit(solution)/shard_map/psum | solution.py:674
  106.0 108.3 %all-reduce.20.cloned.1.call-done = f32[1024,768]{1,0:T(8,128)} async-done(((f32[1024,768]{1,0:T(8,128)}), f32[1024,768]{1,0:T(8,128)}) %all-reduce.20.cloned.1.call-update) | async-done | bytes 3145744 | tf_op jit(solution)/shard_map/psum | solution.py:674
  228.4 13.8 %shard_map.291 = (bf16[1024,768]{1,0:T(8,128)(2,1)}, f32[1024,384]{1,0:T(8,128)}, f32[1024,640]{1,0:T(8,128)}, f32[8,640]{1,0:T(8,128)}, f32[1024,640]{1,0:T(8,1...) custom-call(f32[1024,768]{1,0:T(8,128)} %copy-done, ...), custom_call_target="tpu_custom_call" | custom-call | flops 1610612736 | bytes 9999360 | tf_op jit(solution)/shard_map/pallas_call | solution.py:94
  242.2 12.5 %all-gather.1 = f32[1568,128]{1,0:T(8,128)} all-gather(f32[392,128]{1,0:T(8,128)} %get-tuple-element.93), channel_id=3, replica_groups=mesh['dp'=2,'ctx'=4,'tensor'=4] {'ctx'}, dimensions={0}, use_global_device_ids=true | all-gather | bytes 1003520 | tf_op jit(solution)/shard_map/all_gather | solution.py:534
  254.8 5.9 shard_map.292.y
  260.6 12.2 %shard_map.293 = (f32[1024,384]{1,0:T(8,128)}, f32[4,384,128]{2,1,0:T(8,128)}, f32[1024,768]{1,0:T(8,128)}, f32[4,1,256]{2,1,0:T(1,128)}, f32[4,1,256]{2,1,0:T(1,128)}) custom-call(s32[1]{0:T(128)} %bitcast.me, f32[4,392,128]{2,1,0:T(8,128)} %bitcast.81, f32[4,384,128]{2,1,0:T(8,128)} %get-tuple-element.94.local, f32[4,8,128]{2,1,0:T(8,128)} %get-tuple-element.95.retain, ...), custom_call_target="tpu_custom_call" | custom-call | flops 603979776 | bytes 17569800 | tf_op jit(solution)/shard_map/pallas_call | solution.py:94
  272.8 10.4 all-reduce.12
  284.3 9.0 shard_map.294
  293.3 13.5 %all-gather.2 = f32[1568,128]{1,0:T(8,128)} all-gather(f32[392,128]{1,0:T(8,128)} %get-tuple-element.106), channel_id=4, replica_groups=mesh['dp'=2,'ctx'=4,'tensor'=4] {'ctx'}, dimensions={0}, use_global_device_ids=true | all-gather | bytes 1003520 | tf_op jit(solution)/shard_map/all_gather | solution.py:583
  306.8 22.1 %shard_map.295 = (bf16[1024,640]{1,0:T(8,128)(2,1)}, f32[8,640]{1,0:T(8,128)}, bf16[1024,128]{1,0:T(8,128)(2,1)}, f32[8,640]{1,0:T(8,128)}, f32[8,640]{1,0:T(8,128)}, /*index=5*/f32[8,128]{1,0:T(8,128)}) custom-call(s32[1]{0:T(128)} %bitcast.me, f32[4,392,128]{2,1,0:T(8,128)} %bitcast.79, f32[4,384,128]{2,1,0:T(8,128)} %get-tuple-element.107.later, ...), custom_call_target="tpu_custom_call" | custom-call | flops 1207959552 | bytes 26963976 | tf_op jit(solution)/shard_map/pallas_call | solution.py:94
  335.4 9.1 shard_map.296
  344.8 118.6 %all-reduce.22.cloned.1.call-done = f32[1024,768]{1,0:T(8,128)} async-done(((f32[1024,768]{1,0:T(8,128)}), f32[1024,768]{1,0:T(8,128)}) %all-reduce.22.cloned.1.call-update) | async-done | bytes 3145744 | tf_op jit(solution)/shard_map/psum | solution.py:698
  472.0 9.0 shard_map.297
  481.0 13.8 %all-gather.3 = f32[1568,128]{1,0:T(8,128)} all-gather(f32[392,128]{1,0:T(8,128)} %get-tuple-element.121), channel_id=5, replica_groups=mesh['dp'=2,'ctx'=4,'tensor'=4] {'ctx'}, dimensions={0}, use_global_device_ids=true | all-gather | bytes 1003520 | tf_op jit(solution)/shard_map/all_gather | solution.py:583
  494.8 22.1 %shard_map.298 = (bf16[1024,640]{1,0:T(8,128)(2,1)}, f32[8,640]{1,0:T(8,128)}, bf16[1024,128]{1,0:T(8,128)(2,1)}, f32[8,640]{1,0:T(8,128)}, f32[8,640]{1,0:T(8,128)}, /*index=5*/f32[8,128]{1,0:T(8,128)}) custom-call(s32[1]{0:T(128)} %bitcast.me, f32[4,392,128]{2,1,0:T(8,128)} %bitcast.78, f32[4,384,128]{2,1,0:T(8,128)} %get-tuple-element.122.later, ...), custom_call_target="tpu_custom_call" | custom-call | flops 1207959552 | bytes 26963976 | tf_op jit(solution)/shard_map/pallas_call | solution.py:94
  523.4 9.2 shard_map.299
  547.8 39.1 %all-reduce.8 = (f32[1,4,256]{2,1,0:T(4,128)}, f32[1,4,256]{2,1,0:T(4,128)}, f32[1,256]{1,0:T(1,128)}, f32[1,256]{1,0:T(1,128)}) all-reduce(f32[1,4,256]{2,1,0:T(4,128)} %slice_bitcast_fusion.14, f32[1,4,256]{2,1,0:T(4,128)S(1)} %slice_bitcast_fusion.15, ...), channel_id=1, replica_groups=mesh['dp'=2,'ctx'=4,'tensor'=4] {'dp','ctx','tensor'}, use_global_device_ids=true, to_apply=%region_29.30 | all-reduce | flops 2560 | bytes 20480 | tf_op jit(solution)/shard_map/psum | solution.py:641
  593.8 69.7 %all-reduce.24.cloned.1.call-done = (f32[1,768,256]{2,1,0:T(8,128)}, f32[1,768,256]{2,1,0:T(8,128)}) async-done(((f32[1,768,256]{2,1,0:T(8,128)}, f32[1,768,256]{2,1,0:T(8,128)}), (f32[1,768,256]{2,1,0:T(8,128)}, f32[1,768,256]{2,1,0:T(8,128)})) %all-reduce.24.cloned.1.call-update) | async-done | bytes 1572880 | tf_op jit(solution)/shard_map/psum | solution.py:641
  666.2 115.3 %all-reduce.26.cloned.1.call-done = (f32[1,768,384]{2,1,0:T(8,128)}, f32[1,768,384]{2,1,0:T(8,128)}, f32[1,768,384]{2,1,0:T(8,128)}, f32[1,768,384]{2,1,0:T(8,12...) async-done(((f32[1,768,384]{2,1,0:T(8,128)}, f32[1,768,384]{2,1,0:T(8,128)}, f32[1,768,384]{2,1,0:T(8,128)}, f32[1,768,384]{2,1,0:T(8,128)}, f32[1,384,768]{2,1,0:T(8,128)}, ...) | async-done | bytes 7077904 | tf_op jit(solution)/shard_map/psum | solution.py:640
  788.8 218.3 %all-reduce.28.cloned.1.call-done = (f32[1024,768]{1,0:T(8,128)}, f32[1024,768]{1,0:T(8,128)}) async-done(((f32[1024,768]{1,0:T(8,128)}, f32[1024,768]{1,0:T(8,128)}), (f32[1024,768]{1,0:T(8,128)}, f32[1024,768]{1,0:T(8,128)})) %all-reduce.28.cloned.1.call-update) | async-done | bytes 6291472 | tf_op jit(solution)/shard_map/psum | solution.py:687
  1015.1 43.3 %all-reduce.10 = (f32[1,768]{1,0:T(1,128)}, f32[1,768]{1,0:T(1,128)}, f32[1,768,6]{2,1,0:T(8,128)}, f32[1,768,6]{2,1,0:T(8,128)}, f32[1,4,384]{2,1,0:T(4,128)S(1...) all-reduce(f32[1,768]{1,0:T(1,128)S(1)} %copy-done.22, ...), channel_id=1, replica_groups=mesh['dp'=2,'ctx'=4,'tensor'=4] {'dp','ctx'}, use_global_device_ids=true, to_apply=%region_15.16 | all-reduce | flops 15396 | bytes 123168 | tf_op jit(solution)/shard_map/psum | solution.py:643
  (225 shorter events, 138.7 us)
Async XLA Ops:
  7.2 17.7 %copy-start.37 = (f32[2,6]{1,0:T(2,128)S(1)}, f32[2,6]{1,0:T(2,128)}, u32[]{:S(2)}) copy-start(f32[2,6]{1,0:T(2,128)} %param.28) | copy-start | bytes 148
  7.2 23.3 %copy-start.29 = (f32[2,384]{1,0:T(2,128)S(1)}, f32[2,384]{1,0:T(2,128)}, u32[]{:S(2)}) copy-start(f32[2,384]{1,0:T(2,128)} %param.31) | copy-start | bytes 9220
  7.2 25.9 %copy-start.28 = (f32[2,384]{1,0:T(2,128)S(1)}, f32[2,384]{1,0:T(2,128)}, u32[]{:S(2)}) copy-start(f32[2,384]{1,0:T(2,128)} %param.25) | copy-start | bytes 9220
  7.2 207.1 %all-reduce.20.cloned.1.call-start = ((), (), s32[]{:S(2)}) async-start(), calls=%async_computation | async-start | bytes 6291456 | tf_op jit(solution)/shard_map/psum | solution.py:674
  8.5 38.9 %collective-permute-start.1 = (s32[8]{0:T(128)}, s32[8]{0:T(128)}, u32[]{:S(2)}, u32[]{:S(2)}) collective-permute-start(s32[8]{0:T(128)} %slice.177), channel_id=1, source_target_pairs={{0,4},{4,8},{8,12},{1,5},{5,9},{9,13},{2,6},{6,10},{10,14},{3,7},{... | collective-permute-start | bytes 104 | tf_op jit(solution)/shard_map/ppermute | solution.py:479
  15.2 36.1 %collective-permute-start = (f32[8,768]{1,0:T(8,128)}, f32[8,768]{1,0:T(8,128)}, u32[]{:S(2)}, u32[]{:S(2)}) collective-permute-start(f32[8,768]{1,0:T(8,128)} %slice_convert_fusion), channel_id=1, source_target_pairs={{0,4},{4,8},{8,12},{1,5},{5,9},{9,13},{2,6},{6,10},{10,14},{3,7},{... | collective-permute-start | bytes 73736 | tf_op jit(solution)/shard_map/ppermute | solution.py:479
  19.4 30.9 %copy-start.14 = (f32[1024]{0:T(1024)}, f32[1024]{0:T(1024)S(1)}, u32[]{:S(2)}) copy-start(f32[1024]{0:T(1024)S(1)} %convert_element_type.37) | copy-start | bytes 12292
  21.5 21.9 %copy-start.6 = (bf16[2,384,768]{2,1,0:T(8,128)(2,1)S(1)}, bf16[2,384,768]{2,1,0:T(8,128)(2,1)}, u32[]{:S(2)}) copy-start(bf16[2,384,768]{2,1,0:T(8,128)(2,1)} %param.32) | copy-start | bytes 3538948
  24.9 21.0 %copy-start.7 = (bf16[2,768,384]{2,1,0:T(8,128)(2,1)S(1)}, bf16[2,768,384]{2,1,0:T(8,128)(2,1)}, u32[]{:S(2)}) copy-start(bf16[2,768,384]{2,1,0:T(8,128)(2,1)} %param.21) | copy-start | bytes 3538948
  24.9 21.0 %copy-start.8 = (bf16[2,768,384]{2,1,0:T(8,128)(2,1)S(1)}, bf16[2,768,384]{2,1,0:T(8,128)(2,1)}, u32[]{:S(2)}) copy-start(bf16[2,768,384]{2,1,0:T(8,128)(2,1)} %param.20) | copy-start | bytes 3538948
  92.4 371.0 %all-reduce.22.cloned.1.call-start = ((), (), s32[]{:S(2)}) async-start(), calls=%async_computation.1 | async-start | bytes 6291456 | tf_op jit(solution)/shard_map/psum | solution.py:698
  106.0 115.2 %copy-start.23 = (f32[384]{0:T(512)S(1)}, f32[384]{0:T(512)}, u32[]{:S(2)}) copy-start(f32[384]{0:T(512)} %get-tuple-element.204) | copy-start | bytes 4612
  106.0 115.2 %copy-start.27 = (f32[1,256]{1,0:T(1,128)S(1)}, f32[1,256]{1,0:T(1,128)}, u32[]{:S(2)}) copy-start(f32[1,256]{1,0:T(1,128)} %get-tuple-element.274) | copy-start | bytes 3076
  106.0 115.2 %copy-start.39 = (f32[1,6]{1,0:T(1,128)S(1)}, f32[1,6]{1,0:T(1,128)}, u32[]{:S(2)}) copy-start(f32[1,6]{1,0:T(1,128)} %get-tuple-element.280) | copy-start | bytes 76
  106.0 115.7 %copy-start.40 = (f32[1,6]{1,0:T(1,128)S(1)}, f32[1,6]{1,0:T(1,128)}, u32[]{:S(2)}) copy-start(f32[1,6]{1,0:T(1,128)} %get-tuple-element.278) | copy-start | bytes 76
  106.0 116.2 %copy-start.32 = (f32[6]{0:T(128)S(1)}, f32[6]{0:T(128)}, u32[]{:S(2)}) copy-start(f32[6]{0:T(128)} %get-tuple-element.276) | copy-start | bytes 76
  106.0 117.5 %copy-start.15 = (bf16[1,768,6]{1,0,2:T(2,128)(2,1)S(1)}, bf16[1,768,6]{1,0,2:T(2,128)(2,1)}, u32[]{:S(2)}) copy-start(bf16[1,768,6]{1,0,2:T(2,128)(2,1)} %get-tuple-element.251) | copy-start | bytes 27652
  217.7 10.1 collective-permute-start.2
  328.9 5.9 collective-permute-start.3
  344.5 118.9 %copy-start.1 = (f32[1024,768]{1,0:T(8,128)S(1)}, f32[1024,768]{1,0:T(8,128)}, u32[]{:S(2)}) copy-start(f32[1024,768]{1,0:T(8,128)} %copy-done) | copy-start | bytes 9437188
  344.6 319.0 %all-reduce.24.cloned.1.call-start = ((), (), s32[]{:S(2)}) async-start(), calls=%async_computation.2 | async-start | bytes 3145728 | tf_op jit(solution)/shard_map/psum | solution.py:641
  517.0 5.9 collective-permute-start.4
  532.6 248.8 %all-reduce.26.cloned.1.call-start = ((), (), s32[]{:S(2)}) async-start(), calls=%async_computation.3 | async-start | bytes 14155776 | tf_op jit(solution)/shard_map/psum | solution.py:640
  533.2 473.9 %all-reduce.28.cloned.1.call-start = ((), (), s32[]{:S(2)}) async-start(), calls=%async_computation.4 | async-start | bytes 12582912 | tf_op jit(solution)/shard_map/psum | solution.py:687
  (36 other events, 144.6 us)
Sparse Core Ops, SparseCore 0:
  92.5 121.7 all-reduce.19
  344.7 118.6 all-reduce.21
  532.8 130.7 all-reduce.23
  668.6 112.7 all-reduce.25
  783.7 223.3 all-reduce.27

commit v2 on v1

v2 whole, which is shorter than its diff:
```python
import functools

import jax
import jax.numpy as jnp
from jax import lax
from jax.experimental import pallas as pl
from jax.experimental.pallas import tpu as pltpu
from jax.sharding import PartitionSpec as P

CONV = 4
GROUP = 256
LAYERS = 2
INNER = 1536
EDGE = 8
LANES = 128


EPSILON = 1e-05
PRECISE = lax.Precision.HIGHEST
FLOAT = jnp.float32
BFLOAT = jnp.bfloat16
VMEM_BYTES = 56 * 1024 * 1024


def nn(left, right, precision=None):
    return lax.dot_general(
        left, right, (((1,), (0,)), ((), ())), precision=precision, preferred_element_type=FLOAT
    )


def nt(left, right, precision=None):
    return lax.dot_general(
        left, right, (((1,), (1,)), ((), ())), precision=precision, preferred_element_type=FLOAT
    )


def tn(left, right, precision=None):
    return lax.dot_general(
        left, right, (((0,), (0,)), ((), ())), precision=precision, preferred_element_type=FLOAT
    )


def sigmoid(value):
    return 1.0 / (1.0 + jnp.exp(-value))


def softplus(value):
    small = jnp.exp(-jnp.abs(value))
    series = small * (1.0 - small * (0.5 - small * (1.0 / 3.0 - small * 0.25)))
    return jnp.maximum(value, 0.0) + jnp.where(small < 0.01, series, jnp.log(1.0 + small))


def silu_slope(value):
    sigma = sigmoid(value)
    return sigma * (1.0 + value * (1.0 - sigma))


def spread_matrix(lane_count, heads):
    size = lane_count // heads
    head = lax.broadcasted_iota(jnp.int32, (LANES, lane_count), 0)
    lane = lax.broadcasted_iota(jnp.int32, (LANES, lane_count), 1)
    return jnp.where((lane >= head * size) & (lane < (head + 1) * size), 1.0, 0.0).astype(FLOAT)


def triangle(span, upper):
    row = lax.broadcasted_iota(jnp.int32, (span, span), 0)
    col = lax.broadcasted_iota(jnp.int32, (span, span), 1)
    return jnp.where(col >= row if upper else col <= row, 1.0, 0.0).astype(FLOAT)


def within_block(seg_col, seg_row):
    span = seg_col.shape[0]
    row = lax.broadcasted_iota(jnp.int32, (span, span), 0)
    col = lax.broadcasted_iota(jnp.int32, (span, span), 1)
    return (row >= col) & (seg_col == seg_row)


def call(body, grid, inputs, outputs, scratch=(), reverse=False, flops=0, aliases=None, deps=()):
    def place(b):
        return grid - 1 - b if reverse else b

    def spec_of(shape, kind):
        if isinstance(kind, pl.BlockSpec):
            return kind
        if kind == "smem":
            return pl.BlockSpec(memory_space=pltpu.SMEM)
        if kind == "rows":
            return pl.BlockSpec((shape[0] // grid, shape[1]), lambda b: (place(b), 0))
        if kind == "lead":
            return pl.BlockSpec((None,) + tuple(shape[1:]), lambda b: (place(b),) + (0,) * (len(shape) - 1))
        return pl.BlockSpec(tuple(shape), lambda b: (0,) * len(shape))

    known = len(inputs)
    inputs = list(inputs) + [(dep, pl.BlockSpec(memory_space=pl.ANY)) for dep in deps]

    def run(*refs):
        body(*refs[:known], *refs[len(inputs) :])

    moved = sum(a.size * a.dtype.itemsize for a, _ in inputs)
    return pl.pallas_call(
        run,
        grid=(grid,),
        in_specs=[spec_of(a.shape, kind) for a, kind in inputs],
        out_specs=[spec_of(shape, kind) for shape, _, kind in outputs],
        out_shape=[jax.ShapeDtypeStruct(shape, dtype) for shape, dtype, _ in outputs],
        scratch_shapes=list(scratch),
        input_output_aliases=aliases or {},
        compiler_params=pltpu.CompilerParams(
            dimension_semantics=("arbitrary",), vmem_limit_bytes=VMEM_BYTES
        ),
        cost_estimate=pl.CostEstimate(flops=int(flops), bytes_accessed=int(2 * moved), transcendentals=0),
    )(*[a for a, _ in inputs])


def column(row):
    return jnp.broadcast_to(row, (8, row.shape[1])).T[:, 0:1]


def summed(b, core, mine, other):
    span = GROUP
    per = mine.shape[0] // span
    use = b // per == core
    rows = pl.ds(pl.multiple_of((b % per) * span, span), span)
    return jnp.where(use, mine[rows], other[rows]), use, b % per


def branch_of(b, core, mine, other):
    total, use, at = summed(b, core, mine, other)
    size = mine.shape[0] - EDGE
    squares = jnp.where(use, mine[size : size + 1], other[size : size + 1])
    row = squares[:, 0:GROUP]
    for k in range(1, size // GROUP):
        row = jnp.where(at == k, squares[:, k * GROUP : (k + 1) * GROUP], row)
    return total, lax.rsqrt(column(row) / INNER + EPSILON)


def project_kernel(flags, *refs, first_layer):
    if first_layer:
        (tokens, got, halo), refs = refs[:3], refs[3:]
    else:
        (resid, mine, other, halo, edge), refs = refs[:5], refs[5:]
    (
        gain, value_w, state_w, step_w, filt, misc, meta,
        resid_o, normed_o, pre_o, pre_halo_o, conv_o, vals_o, wr_o, shifted_o, cum_o, local_o, retain_o, pay_o,
        ext, state,
    ) = refs
    b = pl.program_id(0)
    span = GROUP
    lanes = value_w.shape[1]
    heads_rows = state.shape[0]

    def normalise(x):
        inv = lax.rsqrt(jnp.mean(x * x, axis=1, keepdims=True) + EPSILON)
        return (x * inv * gain[...]).astype(BFLOAT)

    @pl.when(b == 0)
    def _():
        rows = halo[...]
        if not first_layer:
            inv = lax.rsqrt(column(edge[EDGE : EDGE + 1, 512 - LANES : 512])[LANES - EDGE :] / INNER + EPSILON)
            rows = rows + inv * edge[0:EDGE]
        normed = normalise(rows)
        edge_pre = jnp.concatenate([nn(normed, value_w[...]), nn(normed, state_w[...])], axis=1)
        ext[0:EDGE] = edge_pre
        pre_halo_o[...] = edge_pre
        state[...] = jnp.zeros_like(state)

    @pl.when(b > 0)
    def _():
        ext[0:EDGE] = ext[span : span + EDGE]

    if first_layer:
        x = jnp.where(flags[1] == 1, tokens[...].astype(FLOAT), got[...])
    else:
        branch, inv_norm = branch_of(b, flags[2], mine, other)
        x = resid[...] + inv_norm * branch
    resid_o[...] = x
    normed = normalise(x)
    normed_o[...] = normed
    ext[EDGE : span + EDGE, 0:lanes] = nn(normed, value_w[...])
    ext[EDGE : span + EDGE, lanes:] = nn(normed, state_w[...])
    pre = ext[EDGE : span + EDGE]
    pre_o[...] = pre
    conv_sum = filt[CONV : CONV + 1] + filt[CONV - 1 : CONV] * pre
    for k in range(CONV - 1):
        at = EDGE - (CONV - 1) + k
        conv_sum = conv_sum + filt[k : k + 1] * (ext[at : at + span] * meta[:, k : k + 1])
    conv_o[...] = conv_sum
    activated = conv_sum * sigmoid(conv_sum)
    vals = activated[:, :lanes].astype(BFLOAT)
    write_read = activated[:, lanes:].astype(BFLOAT)
    vals_o[...] = vals
    wr_o[...] = write_read
    write = write_read[:, : write_read.shape[1] // 2]

    shifted = nt(normed, step_w[...]) + misc[2:3, 0:LANES]
    shifted_o[...] = shifted
    steps = softplus(shifted)
    log_decay = -misc[3:4, 0:LANES] * steps
    cum = nn(triangle(span, False), log_decay, PRECISE)
    cum_o[...] = cum
    last = cum[span - 1 : span]
    tail_step = meta[:, 4:5] * jnp.exp(last - cum) * steps
    heads = HEADS_OF(lanes)
    spread = spread_matrix(lanes, heads)
    weight = nn(tail_step, spread, PRECISE)
    local = tn((weight * vals.astype(FLOAT)).astype(BFLOAT), write)
    retain = meta[span - 1 : span, 3:4] * jnp.exp(last)
    retain_o[...] = jnp.broadcast_to(retain, retain_o.shape)
    size = heads_rows // heads
    local_o[...] = state[...]

    @pl.when(b == 0)
    def _():
        pay_o[heads_rows:] = jnp.ones_like(pay_o[heads_rows:])

    for h in range(heads):
        rows = slice(h * size, (h + 1) * size)
        state[rows] = retain[:, h : h + 1] * state[rows] + local[rows]
    pay_o[0:heads_rows] = state[...]
    pay_o[heads_rows:] = pay_o[heads_rows:] * retain


def HEADS_OF(lanes):
    return lanes // 64


def inside_kernel(normed, gate_w, vals, wr, cum, shifted, meta, seg_row, gate_o, y_o):
    lanes = vals.shape[1]
    heads = HEADS_OF(lanes)
    size = lanes // heads
    half = wr.shape[1] // 2
    gate_o[...] = nn(normed[...], gate_w[...])
    mask = within_block(meta[:, 5:6], seg_row[...])
    mixed = jnp.where(mask, nt(wr[:, half:], wr[:, :half]), 0.0)
    cum_v = cum[...]
    cum_t = cum_v.T
    step_t = softplus(shifted[...]).T
    for h in range(heads):
        gap = jnp.where(mask, cum_v[:, h : h + 1] - cum_t[h : h + 1, :], 0.0)
        mixing = (mixed * jnp.exp(gap) * step_t[h : h + 1, :]).astype(BFLOAT)
        y_o[:, h * size : (h + 1) * size] = nn(mixing, vals[:, h * size : (h + 1) * size])


def fold_in(me, count, payload, acc, reverse, heads):
    rows = acc.shape[0]
    size = rows // heads
    acc[...] = jnp.zeros_like(acc)
    for k in range(count):
        at = count - 1 - k if reverse else k
        reached = at > me if reverse else at < me

        @pl.when(reached)
        def _():
            keep = payload[at, rows : rows + 1]
            for h in range(heads):
                part = slice(h * size, (h + 1) * size)
                acc[part] = keep[:, h : h + 1] * acc[part] + payload[at, part]


def gated_kernel(
    flags, payload, local, retain, y, wr, vals, cum, meta, gate, misc, out_w, *rest, last_layer
):
    if last_layer:
        cot, got, ssm_o, states_o, partial_o, sums_o, cot_o, acc = rest
    else:
        ssm_o, states_o, partial_o, acc = rest
    b = pl.program_id(0)
    span, lanes = vals.shape
    heads = HEADS_OF(lanes)
    rows = acc.shape[0]
    size = rows // heads
    half = wr.shape[1] // 2

    @pl.when(b == 0)
    def _():
        fold_in(flags[0], payload.shape[0], payload, acc, False, heads)

    states = local[...] + acc[...]
    states_o[...] = states
    for h in range(heads):
        part = slice(h * size, (h + 1) * size)
        acc[part] = retain[0:1, h : h + 1] * acc[part]
    enter = meta[:, 3:4] * jnp.exp(cum[...])
    enter_lanes = nn(enter, spread_matrix(lanes, heads), PRECISE)
    carried = nt(wr[:, half:], states.astype(BFLOAT)) * enter_lanes
    ssm = y[...] + carried + misc[1:2] * vals[...].astype(FLOAT)
    ssm_o[...] = ssm
    gate_v = gate[...]
    gated = ssm * (gate_v * sigmoid(gate_v))
    partial = nn((gated * misc[0:1]).astype(BFLOAT), out_w[...])
    squares = nt(jnp.ones((8, lanes), FLOAT), gated * gated, PRECISE)
    if last_layer:
        partial_o[...] = partial
        sums_o[...] = jnp.zeros_like(sums_o)
        sums_o[0:1] = squares[0:1]
        given = jnp.where(flags[1] == 1, cot[...].astype(FLOAT), got[...])
        cot_o[...] = given
        sums_o[1:2] = nt(jnp.ones((8, partial.shape[1]), FLOAT), partial * given, PRECISE)[0:1]
    else:
        per = partial_o.shape[0] // 2
        inner = (per - EDGE) // span
        base = pl.multiple_of((b // inner) * per, EDGE)
        partial_o[pl.ds(pl.multiple_of(base + (b % inner) * span, EDGE), span)] = partial
        foot = pl.ds(pl.multiple_of(base + inner * span, EDGE), EDGE)

        @pl.when(b % inner == 0)
        def _():
            partial_o[foot] = jnp.zeros((EDGE, partial.shape[1]), FLOAT)

        for k in range(inner):

            @pl.when(b % inner == k)
            def _():
                partial_o[foot, k * span : (k + 1) * span] = squares


def ungate_kernel(flags, *refs, last_layer):
    if last_layer:
        (upstream, sums), refs = refs[:2], refs[2:]
    else:
        (cot, above_mine, above_other, above_x, above_gain, mine, other), refs = refs[:7], refs[7:]
    (normed, out_w, misc, gate, ssm, vals, wr, cum, meta, retain), refs = refs[:10], refs[10:]
    if not last_layer:
        (up_o, gain_o), refs = refs[:2], refs[2:]
    grad_ssm_o, gate_low_o, packed_o, small_o, later_o, pay_o, state, grad_gate_w_o, grad_out_w_o = refs
    b = pl.program_id(0)
    block = pl.num_programs(0) - 1 - b
    lanes = vals.shape[1]
    heads = HEADS_OF(lanes)
    rows = state.shape[0]
    size = rows // heads
    half = wr.shape[1] // 2

    @pl.when(b == 0)
    def _():
        state[...] = jnp.zeros_like(state)
        grad_out_w_o[...] = jnp.zeros_like(grad_out_w_o)
        grad_gate_w_o[...] = jnp.zeros_like(grad_gate_w_o)
        small_o[...] = jnp.zeros_like(small_o)
        pay_o[rows:] = jnp.ones_like(pay_o[rows:])
        if not last_layer:
            gain_o[...] = jnp.zeros_like(gain_o)

    if last_layer:
        up = upstream[...]
        sums_t = sums[...].T
        inv_norm = lax.rsqrt(sums_t[:, 0:1] / INNER + EPSILON)
        grad_inv = sums_t[:, 1:2]
    else:
        grad_normed, _, _ = summed(block, flags[2], above_mine, above_other)
        x = above_x[...]
        inv_rms = lax.rsqrt(jnp.mean(x * x, axis=1, keepdims=True) + EPSILON)
        scaled = x * inv_rms
        gain_o[0:1] += jnp.sum(grad_normed * scaled, axis=0, keepdims=True)
        inner = grad_normed * above_gain[...]
        up = cot[...] + inv_rms * (inner - scaled * jnp.mean(inner * scaled, axis=1, keepdims=True))
        up_o[...] = up
        branch, inv_norm = branch_of(block, flags[2], mine, other)
        grad_inv = jnp.sum(up * branch, axis=1, keepdims=True)

    grad_branch = (inv_norm * up).astype(BFLOAT)
    gate_v = gate[...]
    sigma = sigmoid(gate_v)
    gate_act = gate_v * sigma
    ssm_v = ssm[...]
    gated = ssm_v * gate_act
    gain = misc[0:1]
    out_in = (gated * gain).astype(BFLOAT)
    grad_out_w_o[...] += tn(out_in, grad_branch)
    grad_out_in = nt(grad_branch, out_w[...])
    small_o[0:1] += jnp.sum(grad_out_in * gated, axis=0, keepdims=True)
    grad_gated = grad_out_in * gain - (grad_inv * inv_norm * inv_norm * inv_norm / INNER) * gated
    grad_ssm = (grad_gated * gate_act).astype(BFLOAT)
    grad_ssm_o[...] = grad_ssm
    gate_low = (grad_gated * ssm_v * (sigma * (1.0 + gate_v * (1.0 - sigma)))).astype(BFLOAT)
    gate_low_o[...] = gate_low
    grad_gate_w_o[...] += tn(normed[...], gate_low)
    grad_wide = grad_ssm.astype(FLOAT)
    small_o[1:2] += jnp.sum(grad_wide * vals[...].astype(FLOAT), axis=0, keepdims=True)
    enter = meta[:, 3:4] * jnp.exp(cum[...])
    enter_lanes = nn(enter, spread_matrix(lanes, heads), PRECISE)
    pulls = tn((enter_lanes * grad_wide).astype(BFLOAT), wr[:, half:])
    later_o[...] = state[...]
    keep = retain[0:1]
    for h in range(heads):
        part = slice(h * size, (h + 1) * size)
        state[part] = keep[:, h : h + 1] * state[part] + pulls[part]
    pay_o[0:rows] = state[...]
    pay_o[rows:] = pay_o[rows:] * keep

    @pl.when(block == 0)
    def _():
        count = packed_o.shape[0]
        size = grad_gate_w_o.shape[0] // count
        half = size // 2
        for j in range(count):
            packed_o[j, 0:size] = grad_gate_w_o[j * size : (j + 1) * size]
            packed_o[j, size : size + half] = grad_out_w_o[j * half : (j + 1) * half, 0:lanes]
            packed_o[j, size + half :] = grad_out_w_o[j * half : (j + 1) * half, lanes:]


def unmix_kernel(
    flags, payload, later, retain, grad_ssm, vals, wr, cum, shifted, meta, seg_row, states, conv, pre, before, pre_halo,
    filt, misc,
    low_o, edge_o, step_low_o, spill_o, small_o, small2_o,
    acc, flows, ext,
):
    b = pl.program_id(0)
    blocks = pl.num_programs(0)
    span, lanes = vals.shape
    heads = HEADS_OF(lanes)
    rows = acc.shape[0]
    size = rows // heads
    half = wr.shape[1] // 2
    write, read = wr[:, :half], wr[:, half:]

    @pl.when(b == 0)
    def _():
        fold_in(flags[0], payload.shape[0], payload, acc, True, heads)
        small_o[...] = jnp.zeros_like(small_o)
        small2_o[...] = jnp.zeros_like(small2_o)
        for k in range(CONV - 1):
            ext[k, span:] = jnp.zeros_like(ext[k, span:])

    @pl.when(b > 0)
    def _():
        for k in range(CONV - 1):
            ext[k, span:] = ext[k, 0:EDGE]

    grad_next = later[...] + acc[...]
    keep = retain[0:1]
    states_v = states[...]
    spread = spread_matrix(lanes, heads)
    meet = jnp.sum(grad_next * states_v, axis=1, keepdims=True)
    grad_retain = tn(jnp.broadcast_to(meet, (rows, LANES)) * spread.T, jnp.ones((rows, 8), FLOAT), PRECISE)
    grad_retain = grad_retain.T[0:1]
    for h in range(heads):
        part = slice(h * size, (h + 1) * size)
        acc[part] = keep[:, h : h + 1] * acc[part]

    cum_v = cum[...]
    cum_t = cum_v.T
    shifted_v = shifted[...]
    steps = softplus(shifted_v)
    step_t = steps.T
    seg_mask = within_block(meta[:, 5:6], seg_row[...])
    inter = jnp.where(seg_mask, nt(read, write), 0.0)
    grad_inter = jnp.zeros((span, span), FLOAT)
    flows[...] = jnp.zeros_like(flows)
    parts = []
    row_sums = jnp.zeros((span, LANES), FLOAT)
    lane_no = lax.broadcasted_iota(jnp.int32, (span, LANES), 1)
    for h in range(heads):
        part = slice(h * size, (h + 1) * size)
        decay = jnp.exp(jnp.where(seg_mask, cum_v[:, h : h + 1] - cum_t[h : h + 1, :], 0.0))
        decay_inter = decay * inter
        step_h = step_t[h : h + 1, :]
        mixing = (decay_inter * step_h).astype(BFLOAT)
        grad_h = grad_ssm[:, part]
        parts.append(tn(mixing, grad_h))
        pairing = nt(grad_h, vals[:, part])
        grad_inter = grad_inter + pairing * decay * step_h
        weighted = pairing * decay_inter
        col = jnp.sum(weighted, axis=0, keepdims=True)
        flows[h : h + 1, :] = col
        row_sums = row_sums + jnp.where(
            lane_no == h, jnp.sum(weighted * step_h, axis=1, keepdims=True), 0.0
        )
    grad_vals = jnp.concatenate(parts, axis=1)
    grad_steps = flows[...].T
    grad_cum = row_sums - grad_steps * steps
    grad_inter = jnp.where(seg_mask, grad_inter, 0.0).astype(BFLOAT)
    grad_read = nn(grad_inter, write)
    grad_write = tn(grad_inter, read)

    vals_f = vals[...].astype(FLOAT)
    grad_f = grad_ssm[...].astype(FLOAT)
    enter = meta[:, 3:4] * jnp.exp(cum_v)
    enter_lanes = nn(enter, spread, PRECISE)
    states_low = states_v.astype(BFLOAT)
    grad_read = grad_read + nn((enter_lanes * grad_f).astype(BFLOAT), states_low)
    out_of = nt(read, states_low)
    grad_cum = grad_cum + enter * nt(grad_f * out_of, spread, PRECISE)
    next_low = grad_next.astype(BFLOAT)
    along = nt(write, next_low)
    last = cum_v[span - 1 : span]
    tail = meta[:, 4:5] * jnp.exp(last - cum_v)
    tail_step = tail * steps
    tail_lanes = nn(tail_step, spread, PRECISE)
    grad_vals = grad_vals + tail_lanes * along + misc[1:2] * grad_f
    grad_write = grad_write + nn((tail_lanes * vals_f).astype(BFLOAT), next_low)
    reach = nt(vals_f * along, spread, PRECISE)
    grad_steps = grad_steps + tail * reach
    tail_flow = tail_step * reach
    grad_last = jnp.sum(tail_flow, axis=0, keepdims=True) + grad_retain * keep
    grad_log = nn(triangle(span, True), grad_cum - tail_flow, PRECISE) + grad_last
    rate_v = misc[3:4, 0:LANES]
    log_decay = -rate_v * steps
    small2_o[0:1] += jnp.sum(grad_log * log_decay, axis=0, keepdims=True)
    grad_shifted = (grad_steps - rate_v * grad_log) * sigmoid(shifted_v)
    small2_o[1:2] += jnp.sum(grad_shifted, axis=0, keepdims=True)
    step_low_o[...] = grad_shifted.astype(BFLOAT)

    grad_conv = jnp.concatenate([grad_vals, grad_write, grad_read], axis=1) * silu_slope(conv[...])
    small_o[CONV : CONV + 1] += jnp.sum(grad_conv, axis=0, keepdims=True)
    pre_v = pre[...]
    small_o[CONV - 1 : CONV] += jnp.sum(grad_conv * pre_v, axis=0, keepdims=True)
    grad_pre = filt[CONV - 1 : CONV] * grad_conv
    first = blocks - 1 - b == 0
    for k in range(CONV - 1):
        lag = CONV - 1 - k
        masked = grad_conv * meta[:, k : k + 1]
        ext[k, 0:span] = masked
        ahead = ext[k, lag : lag + span]
        row_no = lax.broadcasted_iota(jnp.int32, (span, 1), 0)
        own = jnp.where(row_no < span - lag, ahead, 0.0)
        edge = jnp.where(first, pre_halo[...], before[...])
        head_rows = ext[k, 0:EDGE]
        edge_sum = jnp.zeros((1, head_rows.shape[1]), FLOAT)
        for t in range(lag):
            edge_sum = edge_sum + head_rows[t : t + 1] * edge[EDGE - lag + t : EDGE - lag + t + 1]
        small_o[k : k + 1] += jnp.sum(own * pre_v, axis=0, keepdims=True) + edge_sum
        grad_pre = grad_pre + filt[k : k + 1] * ahead
    low_o[...] = grad_pre.astype(BFLOAT)

    @pl.when(b == 0)
    def _():
        edge_o[...] = grad_pre[span - EDGE :]

    spill_o[...] = jnp.zeros_like(spill_o)
    for k in range(CONV - 1):
        lag = CONV - 1 - k
        for t in range(lag):
            at = EDGE - lag + t
            spill_o[at : at + 1] += filt[k : k + 1] * ext[k, t : t + 1]


def common_places(count, size):
    for j in range(count):
        for group in range(3):
            at = group * count * size + j * size
            side, row = divmod(at, 3 * count * size // 2)
            yield j, group, side, row


def weights_kernel(
    normed, low, edge, spill, gate_low, step_low, gate_w, value_w, state_w, step_w,
    small, small_c, small_h,
    grad_normed_o, packed_o,
    value_a, common_a, step_a,
):
    b = pl.program_id(0)
    blocks = pl.num_programs(0)
    span = low.shape[0]
    lanes = value_w.shape[1]
    d = value_w.shape[0]

    @pl.when(b == 0)
    def _():
        value_a[...] = jnp.zeros_like(value_a)
        common_a[...] = jnp.zeros_like(common_a)
        step_a[...] = jnp.zeros_like(step_a)

    patch = edge[...] + spill[...]
    padded = jnp.concatenate([jnp.zeros((span - EDGE, patch.shape[1]), FLOAT), patch], axis=0)
    row_no = lax.broadcasted_iota(jnp.int32, (span, 1), 0)
    use = (row_no >= span - EDGE) & (b == blocks - 1)
    low_v = jnp.where(use, padded, low[...].astype(FLOAT)).astype(BFLOAT)
    value_low, state_low = low_v[:, :lanes], low_v[:, lanes:]
    normed_v = normed[...]
    value_a[...] += tn(normed_v, value_low)
    common_a[0:d] += tn(normed_v, state_low)
    step_a[...] += tn(step_low[...], normed_v)
    grad_normed_o[...] = (
        nt(gate_low[...], gate_w[...])
        + nt(value_low, value_w[...])
        + nt(state_low, state_w[...])
        + nn(step_low[...], step_w[...])
    )

    @pl.when(b == blocks - 1)
    def _():
        common_a[d : d + EDGE] = small_c[0:EDGE, lanes:]
        count = packed_o.shape[0]
        size = d // count
        rows = size
        for j in range(count):
            packed_o[j, 0:size] = value_a[j * size : (j + 1) * size]
        packed_o[0, rows : rows + 5] = small_c[0:5, 0:lanes]
        packed_o[0, rows + 5 : rows + 7] = small[0:2]
        packed_o[0, rows + 7 : rows + 8, 0:LANES] = small_h[0:1]
        packed_o[0, rows + 7 : rows + 8, LANES : 2 * LANES] = small_h[1:2]
        packed_o[0, rows + 7 : rows + 8, 2 * LANES :] = jnp.zeros((1, lanes - 2 * LANES), FLOAT)
        packed_o[1, rows : rows + 8] = jnp.zeros((8, lanes), FLOAT)
        packed_o[2, rows : rows + 8] = step_a[0:8, 0:lanes]
        packed_o[3, rows : rows + 8] = step_a[0:8, lanes:]
        rows += 8
        part = packed_o.shape[1] - rows
        for j, group, side, row in common_places(count, part):
            packed_o[j, rows:, group * LANES : (group + 1) * LANES] = common_a[
                row : row + part, side * LANES : (side + 1) * LANES
            ]


AXES = ("dp", "ctx", "tensor")


def move(shard, dest):
    sizes = [lax.axis_size(axis) for axis in AXES]
    pairs = []
    for dp in range(sizes[0]):
        for q in range(sizes[1]):
            for t in range(sizes[2]):
                to = dest(dp, q, t)
                if to is not None:
                    pairs.append(
                        ((dp * sizes[1] + q) * sizes[2] + t, (to[0] * sizes[1] + to[1]) * sizes[2] + to[2])
                    )
    return lax.ppermute(shard, AXES, pairs)


def other_core(dp, q, t):
    return dp ^ 1, q, t


def beside(dp, q, t):
    return dp, q, t ^ 1


def at_home(dp, t):
    return t // 2 == dp % 2


class Where:
    def __init__(self):
        self.core = lax.axis_index("dp") % 2
        self.q = lax.axis_index("ctx")
        self.t = lax.axis_index("tensor")
        self.high = self.t // 2
        self.low = self.t % 2
        self.home = self.core == self.high
        self.count = lax.axis_size("ctx")
        self.flags = jnp.stack([self.q, self.home, self.core, self.t]).astype(jnp.int32)
        self.outer = lax.axis_size("dp") // 2


def piece(array, at, count):
    size = array.shape[0] // count
    return lax.dynamic_slice_in_dim(array, at * size, size)


def in_order(w, pieces):
    size = pieces[0].shape[0]
    full = jnp.zeros((size * len(pieces),) + pieces[0].shape[1:], pieces[0].dtype)
    for k, part in enumerate(pieces):
        full = lax.dynamic_update_slice_in_dim(full, part, (w.q ^ k) * size, 0)
    return full


def from_core(w, array):
    got = move(array, lambda dp, q, t: (dp ^ 1, q, t) if at_home(dp, t) else None)
    return jnp.where(w.home, array, got)


def tie(w, array, event):
    first = event[(0,) * event.ndim].astype(array.dtype)
    return array + jnp.where(w.q > 1000, first, jnp.zeros_like(first))


def pack_kernel(flags, value, gate, out, taps, off, gain, bias, decay, skip, step, *outs, layers):
    lanes = value.shape[2]
    d = value.shape[1]
    size = d // 4
    half = size // 2
    heads = step.shape[2]
    for l, parts in layers:
        places = [(outs[number], at) for number, at in parts]
        (first, base), (second, then) = places
        rows = pl.ds(pl.multiple_of(flags[0] * size, size), size)
        first[base : base + size] = value[l, rows].astype(FLOAT)
        base += size
        first[base : base + 16] = jnp.zeros((16, lanes), FLOAT)
        first[base : base + CONV] = taps[l]
        first[base + CONV : base + CONV + 1] = off[l : l + 1]
        first[base + CONV + 1 : base + CONV + 2] = gain[l : l + 1]
        first[base + 6 : base + 7, 0:heads] = bias[l : l + 1]
        first[base + 7 : base + 8, 0:heads] = decay[l : l + 1]
        first[base + 8 : base + 9, 0:heads] = skip[l : l + 1]
        wide = jnp.concatenate([step[l].astype(FLOAT), jnp.zeros((d, LANES - heads), FLOAT)], axis=1).T
        first[base + 16 : base + 24] = wide[0:8, 0:lanes]
        first[base + 24 : base + 32] = wide[0:8, lanes:]
        second[then : then + size] = gate[l, rows].astype(FLOAT)
        half_rows = pl.ds(pl.multiple_of(flags[0] * half, half), half)
        wide = out[l, half_rows].astype(FLOAT)
        second[then + size : then + size + half] = wide[:, 0:lanes]
        second[then + size + half : then + 2 * size] = wide[:, lanes:]


def value_kernel(flags, value, own, state_taps, state_off, *rest, layer):
    pieces, (value_o, step_o, filt_o, misc_o) = rest[:-4], rest[-4:]
    d, lanes = value_o.shape
    size = d // len(pieces)
    heads = HEADS_OF(lanes)

    @pl.when(flags[1] == 1)
    def _():
        value_o[...] = value[...]

    @pl.when(flags[1] == 0)
    def _():
        for k, part in enumerate(pieces):
            at = pl.multiple_of((flags[0] ^ k) * size, size)
            value_o[pl.ds(at, size)] = part[0:size].astype(BFLOAT)

    small = jnp.where(flags[1] == 1, own[size : size + 32], pieces[0][size : size + 32])
    step_o[...] = jnp.zeros_like(step_o)
    step_o[0:16, 0:lanes] = jnp.concatenate([small[16:24], jnp.zeros((8, lanes), FLOAT)]).astype(BFLOAT)
    step_o[0:16, lanes:] = jnp.concatenate([small[24:32], jnp.zeros((8, lanes), FLOAT)]).astype(BFLOAT)
    filt_o[...] = jnp.zeros_like(filt_o)
    filt_o[0 : CONV + 1, 0:lanes] = small[0 : CONV + 1]
    filt_o[0:CONV, lanes:] = state_taps[layer]
    filt_o[CONV : CONV + 1, lanes:] = state_off[layer : layer + 1]
    misc_o[...] = jnp.zeros_like(misc_o)
    misc_o[0:1] = small[CONV + 1 : CONV + 2]
    skip = jnp.broadcast_to(small[8:9, 0:LANES], (8, LANES))
    misc_o[1:2] = nn(skip, spread_matrix(lanes, heads), PRECISE)[0:1]
    misc_o[2:3, 0:LANES] = small[6:7, 0:LANES]
    lane_no = lax.broadcasted_iota(jnp.int32, (1, LANES), 1)
    misc_o[3:4, 0:LANES] = jnp.where(lane_no < heads, jnp.exp(small[7:8, 0:LANES]), 0.0)


def gate_kernel(flags, gate, out, *rest, base):
    pieces, (gate_o, out_o) = rest[:-2], rest[-2:]
    d, lanes = gate_o.shape
    size = d // len(pieces)
    half = size // 2

    @pl.when(flags[1] == 1)
    def _():
        gate_o[...] = gate[...]
        out_o[...] = out[...]

    @pl.when(flags[1] == 0)
    def _():
        for k, part in enumerate(pieces):
            at = pl.multiple_of((flags[0] ^ k) * size, size)
            gate_o[pl.ds(at, size)] = part[base : base + size].astype(BFLOAT)
            at = pl.multiple_of((flags[0] ^ k) * half, half)
            out_o[pl.ds(at, half), 0:lanes] = part[base + size : base + size + half].astype(BFLOAT)
            out_o[pl.ds(at, half), lanes:] = part[base + size + half : base + 2 * size].astype(BFLOAT)


def fetch_part(packed):
    return move(packed, lambda dp, q, t: (dp, q, t ^ 2) if at_home(dp, t) else None)


def fetch_rest(w, part):
    return [part] + [
        move(part, lambda dp, q, t, k=k: None if at_home(dp, t) else (dp, q ^ k, t)) for k in range(1, w.count)
    ]


def layer_spec(shape, layer):
    return pl.BlockSpec((None,) + tuple(shape[1:]), lambda b: (layer,) + (0,) * (len(shape) - 1))


def delivered_kernel(flags, own, got, *rest):
    gate_o, value_o, out_o, rows_o, state_o, extra_o, gain_o, wide = rest[-8:]
    count = own.shape[0]
    d, lanes = value_o.shape
    size = d // count
    half = size // 2
    rows = 3 * size
    part = own.shape[1] - rows - 16

    def put(source):
        total = jnp.zeros((8, lanes), FLOAT)
        for j in range(count):
            k = flags[0] ^ j
            gate_o[j * size : (j + 1) * size] = source[k, 0:size]
            out_o[j * half : (j + 1) * half, 0:lanes] = source[k, size : size + half]
            out_o[j * half : (j + 1) * half, lanes:] = source[k, size + half : 2 * size]
            value_o[j * size : (j + 1) * size] = source[k, 2 * size : rows]
            rows_o[j * 8 : (j + 1) * 8] = source[k, rows : rows + 8]
            total = total + source[k, rows + 8 + part :]
        for j, group, side, row in common_places(count, part):
            wide[row : row + part, side * LANES : (side + 1) * LANES] = source[
                flags[0] ^ j, rows + 8 : rows + 8 + part, group * LANES : (group + 1) * LANES
            ]
        gain_o[...] = total
        state_o[...] = wide[0:d]
        extra_o[...] = wide[d : d + 8]

    @pl.when(flags[1] == 1)
    def _():
        put(own)

    @pl.when(flags[1] == 0)
    def _():
        put(got)


def joined_kernel(flags, have, got, out):
    own = pl.program_id(0) == flags[2]

    @pl.when(own)
    def _():
        out[...] = have[...].astype(BFLOAT)

    @pl.when(jnp.logical_not(own))
    def _():
        out[...] = got[...].astype(BFLOAT)


def halves(w, array):
    return piece(array, w.core, 2) + move(piece(array, 1 - w.core, 2), other_core)


def add_up(w, array, tied=None):
    first = halves(w, array)
    got = move(first, beside)
    part = first + (tied(first, got) if tied else got)
    return first, part, move(part, other_core)


def add_small(array):
    array = array + move(array, other_core)
    return array + move(array, beside)


def add_rows(w, array):
    part = halves(w, array)
    return piece(part, w.low, 2) + move(piece(part, 1 - w.low, 2), beside)


def hand_step(w, up, down):
    count = lax.axis_size("tensor")
    return (
        move(up, lambda dp, q, t: (dp, q, t + 1) if t + 1 < count else None),
        move(down, lambda dp, q, t: (dp, q, t - 1) if t > 0 else None),
    )


def hand_out(w, rows):
    up, down, steps = rows, rows, []
    for _ in range(lax.axis_size("tensor") - 1):
        up, down = hand_step(w, up, down)
        steps.append((up, down))
        up, down = tie(w, up, down), tie(w, down, up)
    return steps


def hand_out_end(w, rows, steps):
    def unit(j):
        total = jnp.where(w.t == j, rows, 0.0)
        for k, (up, down) in enumerate(steps, 1):
            total = jnp.where(w.t == j + k, up, jnp.where(w.t == j - k, down, total))
        return total

    units = [unit(j) for j in range(len(steps) + 1)]
    low, high = jnp.concatenate(units[:2]), jnp.concatenate(units[2:])
    have = jnp.where(w.core == 0, low, high)
    got = move(jnp.where(w.core == 0, high, low), other_core)
    (out,) = call(
        joined_kernel, 2,
        [(w.flags, "smem"), (have, "whole"), (got, "whole")],
        [((2 * have.shape[0], have.shape[1]), BFLOAT, "rows")],
    )
    return out


def over_outer(w, part):
    total = part
    for k in range(1, w.outer):
        size = 2 * w.outer
        total = total + move(part, lambda dp, q, t, k=k: ((dp + 2 * k) % size, q, t))
    return total


def total_start(w, packed, event):
    def at(k):
        return tie(w, lax.dynamic_index_in_dim(packed, w.q ^ k, 0, keepdims=False), event)

    return [at(0)] + [move(at(k), lambda dp, q, t, k=k: (dp, q ^ k, t)) for k in range(1, w.count)]


def total_middle(w, part_a, got, shard_rows, gains, event):
    part = over_outer(w, tie(w, sum(got[1:], got[0]), event))

    def across(array):
        return move(array, lambda dp, q, t: None if at_home(dp, t) else (dp, q, t ^ 2))

    main = jnp.concatenate([part_a, part[:shard_rows]])
    main_far = across(main)
    common = jnp.concatenate([part[shard_rows:], gains])
    common = common + move(common, other_core)
    common = common + move(common, beside)
    return jnp.concatenate([main, common]), jnp.concatenate([main_far, across(common)])


def total_spread(w, part, far, event):
    part = tie(w, part + far, event)
    got = [
        move(part, lambda dp, q, t, k=k: (dp, q ^ k, t) if at_home(dp, t) else None) for k in range(1, w.count)
    ]
    return part, got


def total_end(w, layer, part, got, shapes, before):
    own = jnp.stack([part] + got)
    got = move(own, lambda dp, q, t: (dp ^ 1, q, t) if at_home(dp, t) else None)
    inputs = [(w.flags, "smem"), (own, "whole"), (got, "whole")]
    aliases = {}
    if before is not None:
        aliases = {len(inputs) + i: i for i in range(len(before))}
        inputs += [(array, pl.BlockSpec(memory_space=pl.ANY)) for array in before]
    d, half = shapes[0][1], shapes[4][2]
    return call(
        delivered_kernel, 1, inputs, [(shape, FLOAT, layer_spec(shape, layer)) for shape in shapes],
        [pltpu.VMEM((6 * (own.shape[1] - 3 * d // 4 - 16), half), FLOAT)], aliases=aliases,
    )


def passed_along(shard, axis, by):
    count = lax.axis_size(axis)
    pairs = [(i, i + by) for i in range(count) if 0 <= i + by < count]
    return lax.ppermute(shard, axis, pairs)


def forward_layer(w, source, wts, geometry, given=None, deps=(), then=lambda event: ()):
    meta, seg_row = geometry
    first = len(source) == 3
    n, d = source[0].shape
    grid = n // GROUP
    lanes = wts["value_w"].shape[1]
    wide = wts["state_w"].shape[1]
    chans = lanes + wide
    state = wide // 2
    pay = (lanes + 8, state)
    if first:
        got = pl.BlockSpec((GROUP, d), lambda b: (b, 0))
        entry = [(source[0], "rows"), (source[1], got), (source[2], "whole")]
    else:
        entry = [(source[0], "rows")] + [(array, "whole") for array in source[1:]]
    x, normed, pre, pre_halo, conv, vals, wr, shifted, cum, local, retain, payload = call(
        functools.partial(project_kernel, first_layer=first), grid,
        [(w.flags, "smem")] + entry + [
            (wts["gain"], "whole"), (wts["value_w"], "whole"), (wts["state_w"], "whole"), (wts["step_w"], "whole"),
            (wts["filt"], "whole"), (wts["misc"], "whole"), (meta, "rows"),
        ],
        [
            ((n, d), FLOAT, "rows"), ((n, d), BFLOAT, "rows"), ((n, chans), FLOAT, "rows"),
            ((EDGE, chans), FLOAT, "whole"), ((n, chans), FLOAT, "rows"), ((n, lanes), BFLOAT, "rows"),
            ((n, wide), BFLOAT, "rows"), ((n, LANES), FLOAT, "rows"), ((n, LANES), FLOAT, "rows"),
            ((grid, lanes, state), FLOAT, "lead"), ((grid, 8, LANES), FLOAT, "lead"), (pay, FLOAT, "whole"),
        ],
        [pltpu.VMEM((GROUP + EDGE, chans), FLOAT), pltpu.VMEM((lanes, state), FLOAT)],
        flops=2 * n * d * chans,
        deps=deps,
    )
    everything = lax.all_gather(payload, "ctx")
    gate_w, out_w = wts["late"](payload)
    gate, y = call(
        inside_kernel, grid,
        [(normed, "rows"), (gate_w, "whole"), (vals, "rows"), (wr, "rows"), (cum, "rows"),
         (shifted, "rows"), (meta, "rows"), (seg_row, "lead")],
        [((n, lanes), FLOAT, "rows"), ((n, lanes), FLOAT, "rows")],
        flops=4 * n * GROUP * lanes,
        deps=then(payload),
    )
    last = given is not None
    extra = [(given[0], "rows"), (given[1], "rows")] if last else []
    if last:
        results = [((n, d), FLOAT, "rows"), ((grid, 8, GROUP), FLOAT, "lead"), ((n, d), FLOAT, "rows")]
    else:
        results = [((n + 2 * EDGE, d), FLOAT, "whole")]
    outs = call(
        functools.partial(gated_kernel, last_layer=last), grid,
        [
            (w.flags, "smem"), (everything, "whole"), (local, "lead"), (retain, "lead"), (y, "rows"), (wr, "rows"),
            (vals, "rows"), (cum, "rows"), (meta, "rows"), (gate, "rows"), (wts["misc"], "whole"), (out_w, "whole"),
        ] + extra,
        [((n, lanes), FLOAT, "rows"), ((grid, lanes, state), FLOAT, "lead")] + results,
        [pltpu.VMEM((lanes, state), FLOAT)],
        flops=2 * n * d * lanes,
    )
    ssm, states = outs[0], outs[1]
    saved = (normed, gate, pre, pre_halo, conv, vals, wr, shifted, cum, retain, ssm, states, gate_w, out_w)
    return x, outs[2:], saved


def backward_layer(w, source, wts, saved, geometry, deps):
    meta, seg_row = geometry
    normed, gate, pre, pre_halo, conv, vals, wr, shifted, cum, retain, ssm, states, gate_w, out_w = saved
    last = len(source) == 2
    n, d = source[0].shape
    grid = n // GROUP
    lanes = vals.shape[1]
    chans = pre.shape[1]
    state = wr.shape[1] // 2
    pay = (lanes + 8, state)
    if last:
        entry = [(source[0], "rows"), (source[1], "lead")]
        above = []
    else:
        kinds = ["rows", "whole", "whole", "rows", "whole", "whole", "whole"]
        entry = list(zip(source, kinds))
        above = [((n, d), FLOAT, "rows"), ((8, d), FLOAT, "whole")]
    outs = call(
        functools.partial(ungate_kernel, last_layer=last), grid,
        [(w.flags, "smem")] + entry + [
            (normed, "rows"), (out_w, "whole"), (wts["misc"], "whole"), (gate, "rows"), (ssm, "rows"),
            (vals, "rows"), (wr, "rows"), (cum, "rows"), (meta, "rows"), (retain, "lead"),
        ],
        above + [
            ((n, lanes), BFLOAT, "rows"), ((n, lanes), BFLOAT, "rows"), ((4, d // 2, lanes), FLOAT, "whole"),
            ((8, lanes), FLOAT, "whole"), ((grid, lanes, state), FLOAT, "lead"), (pay, FLOAT, "whole"),
        ],
        [pltpu.VMEM((lanes, state), FLOAT), pltpu.VMEM((d, lanes), FLOAT), pltpu.VMEM((lanes, d), FLOAT)],
        reverse=True,
        flops=6 * n * d * lanes,
        deps=deps[0],
    )
    above = outs[: len(above)]
    grad_ssm, gate_low, packed_a, small, later, payload = outs[len(above) :]
    everything = lax.all_gather(payload, "ctx")
    got_a = total_start(w, packed_a, everything)
    strip = GROUP // EDGE
    before = pl.BlockSpec((EDGE, chans), lambda b: (jnp.maximum((grid - 1 - b) * strip - 1, 0), 0))
    low, edge, step_low, spill, small_c, small_h = call(
        unmix_kernel, grid,
        [
            (w.flags, "smem"), (everything, "whole"), (later, "lead"), (retain, "lead"), (grad_ssm, "rows"),
            (vals, "rows"), (wr, "rows"), (cum, "rows"), (shifted, "rows"), (meta, "rows"), (seg_row, "lead"),
            (states, "lead"), (conv, "rows"), (pre, "rows"), (pre, before), (pre_halo, "whole"),
            (wts["filt"], "whole"), (wts["misc"], "whole"),
        ],
        [
            ((n, chans), BFLOAT, "rows"), ((EDGE, chans), FLOAT, "whole"), ((n, LANES), BFLOAT, "rows"),
            ((EDGE, chans), FLOAT, "whole"), ((8, chans), FLOAT, "whole"), ((8, LANES), FLOAT, "whole"),
        ],
        [
            pltpu.VMEM((lanes, state), FLOAT), pltpu.VMEM((LANES, GROUP), FLOAT),
            pltpu.VMEM((CONV - 1, GROUP + EDGE, chans), FLOAT),
        ],
        reverse=True,
        flops=12 * n * GROUP * lanes,
        deps=deps[1](payload),
    )
    spill = passed_along(spill, "ctx", -1)
    part_a = over_outer(w, sum(got_a[1:], got_a[0]))
    common = 144
    grad_normed, packed = call(
        weights_kernel, grid,
        [
            (normed, "rows"), (low, "rows"), (edge, "whole"), (spill, "whole"), (gate_low, "rows"),
            (step_low, "rows"), (gate_w, "whole"), (wts["value_w"], "whole"), (wts["state_w"], "whole"),
            (wts["step_w"], "whole"), (small, "whole"),
            (small_c, "whole"), (small_h, "whole"),
        ],
        [((n, d), FLOAT, "rows"), ((4, d // 4 + 8 + common, lanes), FLOAT, "whole")],
        [pltpu.VMEM((d, lanes), FLOAT), pltpu.VMEM((6 * common, chans - lanes), FLOAT), pltpu.VMEM((LANES, d), FLOAT)],
        flops=4 * n * d * (lanes + chans),
        deps=deps[2](low) + [part_a],
    )
    return grad_normed, (part_a, packed), above


def local(tokens, segments, *rest):
    params, cotangent = rest[:-1], rest[-1]
    (
        in_gain, gate_w, value_w, state_w, step_w, value_filt, value_off, state_filt, state_off,
        bias_step, decay_param, skip_param, gain_out, out_w,
    ) = params
    n, d = tokens.shape
    w = Where()
    heads = step_w.shape[2]
    lanes = value_w.shape[2]
    wide = state_w.shape[2]
    size = d // w.count

    def pack(layers, shapes, deps=()):
        return call(
            functools.partial(pack_kernel, layers=layers), 1,
            [(w.flags, "smem")] + [
                (array, "whole") for array in (
                    value_w, gate_w, out_w, value_filt, value_off, gain_out, bias_step, decay_param, skip_param, step_w
                )
            ],
            [(shape, FLOAT, "whole") for shape in shapes],
            deps=deps,
        )

    def early(l, own, pieces):
        value, step, filt, misc = call(
            functools.partial(value_kernel, layer=l), 1,
            [(w.flags, "smem"), (value_w, layer_spec(value_w.shape, l)), (own, "whole"), (state_filt, "whole"),
             (state_off, "whole")] + [(part, "whole") for part in pieces],
            [((d, lanes), BFLOAT, "whole"), ((LANES, d), BFLOAT, "whole"), ((8, lanes + wide), FLOAT, "whole"),
             ((8, lanes), FLOAT, "whole")],
        )
        return dict(gain=in_gain[l][None], value_w=value, step_w=step, state_w=state_w[l], filt=filt, misc=misc)

    def late(l, pieces, base, deps=()):
        return call(
            functools.partial(gate_kernel, base=base), 1,
            [(w.flags, "smem"), (gate_w, layer_spec(gate_w.shape, l)), (out_w, layer_spec(out_w.shape, l))]
            + [(part, "whole") for part in pieces],
            [((d, lanes), BFLOAT, "whole"), ((lanes, d), BFLOAT, "whole")],
            deps=deps,
        )

    near = (size + 32, lanes)
    far = (2 * size, lanes)
    both = (near[0] + far[0], lanes)
    pack_a, pack_b, pack_1 = pack(((0, ((0, 0), (1, 0))), (1, ((2, 0), (2, near[0])))), (near, far, both))
    part_a = fetch_part(pack_a)
    edge = jnp.concatenate([
        tokens[n - EDGE :].astype(FLOAT),
        jnp.pad(segments[n - EDGE :].astype(FLOAT)[None], ((0, EDGE - 1), (0, d - EDGE))),
    ])
    edge = passed_along(edge, "ctx", 1)
    segs = jnp.pad(segments.astype(FLOAT), (0, 8 * d - n)).reshape(8, d)
    body = jnp.concatenate([tokens.astype(FLOAT), segs])
    body = move(body, lambda dp, q, t: (dp ^ 1, q, t) if at_home(dp, t) else None)
    part_b = fetch_part(tie(w, pack_b, part_a))
    edge = from_core(w, edge)
    segs = jnp.where(w.home, segs, body[n:]).reshape(-1)[:n]
    seg_ext = jnp.concatenate([edge[EDGE, :EDGE], segs])
    seg_blocks = segs.reshape(-1, GROUP)
    seg_before = jnp.concatenate([seg_ext[EDGE - 1 : EDGE], seg_blocks[:-1, -1]])
    first = EDGE - (CONV - 1)
    columns = [seg_ext[first + k : first + k + n] == segs for k in range(CONV - 1)]
    columns.append((seg_blocks == seg_before[:, None]).reshape(n))
    columns.append((seg_blocks == seg_blocks[:, -1:]).reshape(n))
    columns.append(segs)
    columns += [jnp.zeros_like(segs)] * (8 - len(columns))
    meta = jnp.stack([column.astype(FLOAT) for column in columns], axis=1)
    geometry = (meta, segs.reshape(-1, 1, GROUP))

    wts = [early(0, pack_a, fetch_rest(w, part_a))]
    wts[0]["late"] = lambda event: late(0, fetch_rest(w, part_b), 0, [event])
    halo = edge[:EDGE]
    sent = {"pack": pack_1}

    def send_next(event):
        sent["part"] = fetch_part(tie(w, sent["pack"], part_b))
        return [sent["part"]]

    x_0, (partial,), saved_0 = forward_layer(
        w, (tokens, body, halo), wts[0], geometry, deps=[part_b], then=send_next
    )

    def meanwhile(first, got):
        pieces = fetch_rest(w, tie(w, sent["part"], first))
        wts.append(early(1, sent["pack"], pieces))
        wts[1]["late"] = lambda event: late(1, pieces, near[0])
        sent["cot"] = move(
            tie(w, cotangent.astype(FLOAT), first),
            lambda dp, q, t: (dp ^ 1, q, t) if at_home(dp, t) else None,
        )
        return tie(w, got, wts[1]["misc"])

    _, mine, other = add_up(w, partial, meanwhile)
    edge_1 = mine[mine.shape[0] - 2 * EDGE :]
    from_last = [
        move(edge_1, lambda dp, q, t, c=c: (dp - 1 + c, q + 1, t) if dp % 2 == 1 and q + 1 < w.count else None)
        for c in (0, 1)
    ]
    edge_1 = from_last[0] + from_last[1]

    x_1, (partial, sums, cot), saved_1 = forward_layer(
        w, (x_0, mine, other, halo, edge_1), wts[1], geometry, (cotangent, sent["cot"])
    )
    sums = add_small(sums)
    quarter = 2 * w.core + w.low
    half = halves(w, partial)
    branch = piece(half, w.low, 2) + move(tie(w, piece(half, 1 - w.low, 2), sums), beside)
    rows_sq = lax.dynamic_index_in_dim(sums, quarter, 0, keepdims=False)[0]
    mixed = piece(x_1, quarter, 4) + lax.rsqrt(rows_sq / INNER + EPSILON)[:, None] * branch
    mixed_first = hand_step(w, mixed, mixed)

    grad_normed, packed, _ = backward_layer(
        w, (cot, sums), wts[1], saved_1, geometry,
        ([half], lambda event: [mixed], lambda event: list(mixed_first)),
    )
    held = {}

    def gather(first, got):
        held["start"] = total_start(w, packed[1], first)
        held["start"] = sum(held["start"][1:], held["start"][0])
        return tie(w, got, held["start"])

    _, above_mine, above_other = add_up(w, grad_normed, gather)
    part_1 = packed[0]
    shard_rows = size + 8
    none = jnp.zeros((8, lanes), FLOAT)

    up, down = (tie(w, array, above_mine) for array in mixed_first)
    mixed_second = hand_step(w, up, down)
    mixed_third = hand_step(w, tie(w, mixed_second[0], mixed_second[1]), tie(w, mixed_second[1], mixed_second[0]))
    mixed_steps = [mixed_first, mixed_second, mixed_third]

    def middle(event):
        held["part"], held["far"] = total_middle(w, part_1, [held["start"]], shard_rows, none, event)
        return [held["part"]] + list(mixed_second)

    def spread(event):
        held["part"], held["got"] = total_spread(w, held["part"], held["far"], event)
        return [held["part"]] + list(mixed_third)

    grad_normed, packed, (upstream, gain_1) = backward_layer(
        w, (cot, above_mine, above_other, x_1, in_gain[1][None], mine, other), wts[0], saved_0, geometry,
        ((), middle, spread),
    )
    shapes = (
        (LAYERS, d, lanes), (LAYERS, d, lanes), (LAYERS, lanes, d), (LAYERS, 32, lanes), (LAYERS, d, wide),
        (LAYERS, 8, wide), (LAYERS, 8, lanes),
    )
    first_half = halves(w, grad_normed)
    got = total_start(w, packed[1], first_half)
    last_part = piece(first_half, w.low, 2) + move(piece(first_half, 1 - w.low, 2), beside)
    x = piece(x_0, quarter, 4)
    inv_rms = lax.rsqrt(jnp.mean(x * x, axis=1, keepdims=True) + EPSILON)
    scaled = x * inv_rms
    gain_0 = jnp.sum(last_part * scaled, axis=0)
    inner = last_part * in_gain[0]
    last = piece(upstream, quarter, 4) + inv_rms * (
        inner - scaled * jnp.mean(inner * scaled, axis=1, keepdims=True)
    )
    steps = hand_out(w, last)
    totals = total_end(w, 1, tie(w, held["part"], steps[0][0]), held["got"], shapes, None)
    held["mixed"] = hand_out_end(w, mixed, mixed_steps[:2] + [(tie(w, mixed_third[0], last), mixed_third[1])])
    gains = jnp.concatenate([gain_0.reshape(-1, lanes), 0.25 * gain_1[0].reshape(-1, lanes)])
    gains = jnp.pad(gains, ((0, 8 - gains.shape[0]), (0, 0)))
    part, far = total_middle(w, packed[0], got, shard_rows, gains, steps[0][0])
    part, got = total_spread(w, part, far, steps[1][0])
    input_grad = hand_out_end(w, last, steps)
    grad_gate, grad_value, grad_out, rows, state, extra, gains = total_end(w, 0, part, got, shapes, totals)
    step = jnp.concatenate([rows[:, 16:24], rows[:, 24:32]], axis=2)
    step = jnp.swapaxes(step[:, :heads], 1, 2)
    return (
        held["mixed"], input_grad, gains[0, :4].reshape(2, d), grad_gate, grad_value, state, step, rows[:, :CONV],
        rows[:, CONV], extra[:, :CONV], extra[:, CONV], rows[:, 7, LANES : LANES + heads], rows[:, 7, :heads],
        jnp.sum(rows[:, 6].reshape(LAYERS, heads, -1), axis=2), rows[:, 5], grad_out,
    )


def solution(mesh):
    split = P(None, None, "tensor")
    lane = P(None, "tensor")
    rows = P(("dp", "ctx"), None)
    weights = (P(), split, split, P(), split, split, lane, P(), P(), lane, lane, lane, lane, P(None, "tensor", None))
    return jax.shard_map(
        local,
        mesh=mesh,
        in_specs=(rows, P(("dp", "ctx")), *weights, rows),
        out_specs=(rows, rows, *weights),
        check_vma=False,
    )
```

time: 1090 us -> 741 us (0.68)
  waiting for transfers between devices: 640 us -> 192 us
  starting transfers between devices: 15.2 us -> 159 us
  blocking collectives: 157 us -> 47.9 us
  Pallas kernels: 141 us -> 189 us
  other arithmetic: 51 us -> 76.6 us
    psum x5 -> x0, waiting for transfers between devices: 630 us -> none  [the longest x1 218 us: local(): branch = lax.psum(partial, 'tensor')]
    ppermute x0 -> x71, waiting for transfers between devices: none -> 189 us  [move(): return lax.ppermute(shard, AXES, pairs)]
    ppermute x0 -> x71, starting transfers between devices: none -> 153 us  [move(): return lax.ppermute(shard, AXES, pairs)]
    psum x4 -> x0, blocking collectives: 105 us -> none  [the longest x1 43.3 us: total_over(): lax.psum((gain_in,) + tuple((grads[name] for name in rest)), ('dp', 'ctx'))]
    pallas_call x12 -> x21, Pallas kernels: 141 us -> 189 us  [call(): pl.pallas_call(run, grid=(grid,), in_specs=[spec_of(a.shape, kind) for a,...]
    add x0 -> x41, other arithmetic: none -> 47.7 us  [the longest x23 28 us: tie(): return array + jnp.where(w.q > 1000, first, jnp.zeros_like(first))]
    convert_element_type x6 -> x3, other arithmetic: 16 us -> 3.04 us  [the longest x1 1.64 us: local(): body = jnp.concatenate([tokens.astype(FLOAT), segs])]
    reduce_sum x5 -> x2, other arithmetic: 12.3 us -> 1.01 us  [the longest x1 0.65 us: local(): jnp.sum(rows[:, 6].reshape(LAYERS, heads, -1), axis=2)]
  transfers between devices with their start and end apart: 10 -> 74, of which waited for: 7 -> 25; matrix products, arithmetic and copies ran while one was open for 7% -> 11% of each run, Pallas kernels for 0% -> 16%
where the time goes in v2:
time: 741 us; the launch traced here: 729 us
  waiting for transfers between devices  192 us (26%)
  Pallas kernels  189 us (26%)
  starting transfers between devices  159 us (21%)
  other arithmetic  76.6 us (10%)
  local copies, waits for them, and re-layouts  49.1 us (7%)
  blocking collectives  47.9 us (6%)
  between operations  15.4 us (2%)
    pallas_call x21, Pallas kernels, call(): pl.pallas_call(run, grid=(grid,), in_specs=[spec_of(a.shape, kind) for a,...  189 us
    ppermute x71, waiting for transfers between devices, move(): return lax.ppermute(shard, AXES, pairs)  189 us
    ppermute x71, starting transfers between devices, move(): return lax.ppermute(shard, AXES, pairs)  153 us
    add x23, other arithmetic, tie(): return array + jnp.where(w.q > 1000, first, jnp.zeros_like(first))  28 us
    all_gather x2, blocking collectives, forward_layer(): everything = lax.all_gather(payload, 'ctx')  25.4 us
    all_gather x2, blocking collectives, backward_layer(): everything = lax.all_gather(payload, 'ctx')  22.5 us
    slice x20, local copies, waits for them, and re-layouts, tie(): first = event[(0,) * event.ndim].astype(array.dtype)  15.3 us
  transfers between devices with their start and end apart: 74, of which 25 were waited for; matrix products, arithmetic and copies ran while one was open for 11% of the time, Pallas kernels for 16%

profile of v2, /device:TPU:0, one launch (start us, length us, event | category | flops | bytes accessed | tf_op | source)
XLA Modules:
  0.0 729.0 jit_solution(2319906780606336171)
XLA Ops:
  38.6 14.1 %collective-permute-start.11 = (f32[608,384]{1,0:T(8,128)S(1)}, f32[608,384]{1,0:T(8,128)S(1)}, u32[]{:S(2)}, u32[]{:S(2)}) collective-permute-start(f32[608,384]{1,0:T(8,128)S(1)} %broadcast_add_fusion.1), channel_id=1, source_target_pairs={{0,2},{1,3},{4,6},{5,7},{8,10},{9,11},{12,14},{13,15},{18,16},{19,... | collective-permute-start | bytes 2801672 | tf_op jit(solution)/shard_map/ppermute | solution.py:620
  60.2 13.3 %shard_map.290 = (f32[1024,768]{1,0:T(8,128)}, bf16[1024,768]{1,0:T(8,128)(2,1)}, f32[1024,640]{1,0:T(8,128)}, f32[8,640]{1,0:T(8,128)}, f32[1024,640]{1,0:T(8,1...) custom-call(s32[4]{0:T(128)} %pad_add_fusion.refs_0_, ...), custom_call_target="tpu_custom_call" | custom-call | flops 1006632960 | bytes 13211680 | tf_op jit(solution)/shard_map/pallas_call | solution.py:100
  77.4 12.5 %all-gather = f32[1568,128]{1,0:T(8,128)} all-gather(f32[392,128]{1,0:T(8,128)S(1)} %copy-done.38), channel_id=2, replica_groups=mesh['dp'=2,'ctx'=4,'tensor'=4] {'ctx'}, dimensions={0}, use_global_device_ids=true | all-gather | bytes 1003520 | tf_op jit(solution)/shard_map/all_gather | solution.py:962
  97.5 10.1 %shard_map.293 = (f32[1024,384]{1,0:T(8,128)}, f32[4,384,128]{2,1,0:T(8,128)}, f32[1040,768]{1,0:T(8,128)}) custom-call(s32[4]{0:T(128)} %pad_add_fusion.refs_0_, f32[4,392,128]{2,1,0:T(8,128)} %bitcast.139, f32[4,384,128]{2,1,0:T(8,128)} %get-tuple-element.119.refs_2_, f32[4,8,128]{2,1,0:T(8,128)} %get-tuple-element.120.refs_3_.refs_17_, ...), custom_call_target="tpu_custom_call" | custom-call | flops 603979776 | bytes 14442528 | tf_op jit(solution)/shard_map/pallas_call | solution.py:100
  127.1 9.7 %collective-permute-start.20 = (f32[1024,768]{1,0:T(8,128)}, f32[1024,768]{1,0:T(8,128)}, u32[]{:S(2)}, u32[]{:S(2)}) collective-permute-start(f32[1024,768]{1,0:T(8,128)} %convert_add_fusion), channel_id=1, source_target_pairs={{0,16},{1,17},{4,20},{5,21},{8,24},{9,25},{12,28},{13,29},{18,2},{... | collective-permute-start | bytes 9437192 | tf_op jit(solution)/shard_map/ppermute | solution.py:620
  144.5 11.2 %collective-permute-done.13 = f32[520,768]{1,0:T(8,128)} collective-permute-done((f32[520,768]{1,0:T(8,128)S(1)}, f32[520,768]{1,0:T(8,128)}, u32[]{:S(2)}, u32[]{:S(2)}) %collective-permute-start.13) | collective-permute-done | bytes 1597472 | tf_op jit(solution)/shard_map/ppermute | solution.py:620
  164.9 15.3 %shard_map.295 = (f32[1024,768]{1,0:T(8,128)}, bf16[1024,768]{1,0:T(8,128)(2,1)}, f32[1024,640]{1,0:T(8,128)}, f32[8,640]{1,0:T(8,128)}, f32[1024,640]{1,0:T(8,1...) custom-call(s32[4]{0:T(128)} %pad_add_fusion.refs_0_, ...), custom_call_target="tpu_custom_call" | custom-call | flops 1006632960 | bytes 15325216 | tf_op jit(solution)/shard_map/pallas_call | solution.py:100
  187.0 12.9 %all-gather.1 = f32[1568,128]{1,0:T(8,128)} all-gather(f32[392,128]{1,0:T(8,128)S(1)} %copy-done.47), channel_id=3, replica_groups=mesh['dp'=2,'ctx'=4,'tensor'=4] {'ctx'}, dimensions={0}, use_global_device_ids=true | all-gather | bytes 1003520 | tf_op jit(solution)/shard_map/all_gather | solution.py:962
  199.8 12.7 %shard_map.298 = (f32[1024,384]{1,0:T(8,128)}, f32[4,384,128]{2,1,0:T(8,128)}, f32[1024,768]{1,0:T(8,128)}, f32[4,8,256]{2,1,0:T(8,128)}, f32[1024,768]{1,0:T(8,128)}) custom-call(s32[4]{0:T(128)} %pad_add_fusion.refs_0_, f32[4,392,128]{2,1,0:T(8,128)} %bitcast.138, f32[4,384,128]{2,1,0:T(8,128)} %get-tuple-element.138.refs_2_, ...), custom_call_target="tpu_custom_call" | custom-call | flops 603979776 | bytes 23879712 | tf_op jit(solution)/shard_map/pallas_call | solution.py:100
  229.2 11.5 %shard_map.299 = (bf16[1024,384]{1,0:T(8,128)(2,1)}, bf16[1024,384]{1,0:T(8,128)(2,1)}, f32[4,384,384]{2,1,0:T(8,128)}, f32[8,384]{1,0:T(8,128)}, f32[4,384,128]{2,1,0:T(8,128)}, /*index=5*/f32[392,128]{1,0:T(8,128)}) custom-call(s32[4]{0:T(128)} %pad_add_fusion.refs_0_, f32[1024,768]{1,0:T(8,128)} %get-tuple-element.151.refs_1_, f32[4,8,256]{2,1,0:T(8,128)} %copy-done.48, ...), custom_call_target="tpu_custom_call" | custom-call | flops 1811939328 | bytes 23912480 | tf_op jit(solution)/shard_map/pallas_call | solution.py:100
  240.7 11.0 %all-gather.2 = f32[1568,128]{1,0:T(8,128)S(1)} all-gather(f32[392,128]{1,0:T(8,128)} %get-tuple-element.153), channel_id=4, replica_groups=mesh['dp'=2,'ctx'=4,'tensor'=4] {'ctx'}, dimensions={0}, use_global_device_ids=true | all-gather | bytes 1003520 | tf_op jit(solution)/shard_map/all_gather | solution.py:1027
  264.6 22.1 %shard_map.300 = (bf16[1024,640]{1,0:T(8,128)(2,1)}, f32[8,640]{1,0:T(8,128)}, bf16[1024,128]{1,0:T(8,128)(2,1)}, f32[8,640]{1,0:T(8,128)}, f32[8,640]{1,0:T(8,128)}, /*index=5*/f32[8,128]{1,0:T(8,128)}) custom-call(s32[4]{0:T(128)} %pad_add_fusion.refs_0_, f32[4,392,128]{2,1,0:T(8,128)} %bitcast.137, f32[4,384,128]{2,1,0:T(8,128)} %get-tuple-element.154.refs_2_, ...), custom_call_target="tpu_custom_call" | custom-call | flops 1207959552 | bytes 28557344 | tf_op jit(solution)/shard_map/pallas_call | solution.py:100
  318.7 11.4 %collective-permute-done.33 = f32[344,384]{1,0:T(8,128)S(1)} collective-permute-done((f32[344,384]{1,0:T(8,128)S(1)}, f32[344,384]{1,0:T(8,128)S(1)}, u32[]{:S(2)}, u32[]{:S(2)}) %collective-permute-start.33) | collective-permute-done | bytes 528416 | tf_op jit(solution)/shard_map/ppermute | solution.py:620
  330.1 11.7 %collective-permute-done.34 = f32[344,384]{1,0:T(8,128)S(1)} collective-permute-done((f32[344,384]{1,0:T(8,128)S(1)}, f32[344,384]{1,0:T(8,128)S(1)}, u32[]{:S(2)}, u32[]{:S(2)}) %collective-permute-start.34) | collective-permute-done | bytes 528416 | tf_op jit(solution)/shard_map/ppermute | solution.py:620
  360.0 15.0 %collective-permute-done.37.refs_20_ = f32[256,768]{1,0:T(8,128)S(1)} collective-permute-done((f32[256,768]{1,0:T(8,128)S(1)}, f32[256,768]{1,0:T(8,128)S(1)}, u32[]{:S(2)}, u32[]{:S(2)}) %collective-permute-start.37) | collective-permute-done | bytes 786464 | tf_op jit(solution)/shard_map/ppermute | solution.py:620
  379.5 15.8 %shard_map.302 = (f32[1024,768]{1,0:T(8,128)}, f32[8,768]{1,0:T(8,128)}, bf16[1024,384]{1,0:T(8,128)(2,1)}, bf16[1024,384]{1,0:T(8,128)(2,1)}, f32[4,384,384]{2,...) custom-call(s32[4]{0:T(128)} %pad_add_fusion.refs_0_, ...), custom_call_target="tpu_custom_call" | custom-call | flops 1811939328 | bytes 39680032 | tf_op jit(solution)/shard_map/pallas_call | solution.py:100
  395.3 11.5 %all-gather.3 = f32[1568,128]{1,0:T(8,128)S(1)} all-gather(f32[392,128]{1,0:T(8,128)} %get-tuple-element.173), channel_id=5, replica_groups=mesh['dp'=2,'ctx'=4,'tensor'=4] {'ctx'}, dimensions={0}, use_global_device_ids=true | all-gather | bytes 1003520 | tf_op jit(solution)/shard_map/all_gather | solution.py:1027
  434.9 22.1 %shard_map.303 = (bf16[1024,640]{1,0:T(8,128)(2,1)}, f32[8,640]{1,0:T(8,128)}, bf16[1024,128]{1,0:T(8,128)(2,1)}, f32[8,640]{1,0:T(8,128)}, f32[8,640]{1,0:T(8,128)}, /*index=5*/f32[8,128]{1,0:T(8,128)}) custom-call(s32[4]{0:T(128)} %pad_add_fusion.refs_0_, f32[4,392,128]{2,1,0:T(8,128)} %bitcast.141, f32[4,384,128]{2,1,0:T(8,128)} %get-tuple-element.174.refs_2_, ...), custom_call_target="tpu_custom_call" | custom-call | flops 1207959552 | bytes 32391200 | tf_op jit(solution)/shard_map/pallas_call | solution.py:100
  464.1 16.4 %collective-permute-done.44 = f32[152,384]{1,0:T(8,128)S(1)} collective-permute-done((f32[152,384]{1,0:T(8,128)S(1)}, f32[152,384]{1,0:T(8,128)S(1)}, u32[]{:S(2)}, u32[]{:S(2)}) %collective-permute-start.44) | collective-permute-done | bytes 233504 | tf_op jit(solution)/shard_map/ppermute | solution.py:620
  499.9 17.9 %collective-permute-done.50 = f32[256,768]{1,0:T(8,128)S(1)} collective-permute-done((f32[256,768]{1,0:T(8,128)S(1)}, f32[256,768]{1,0:T(8,128)S(1)}, u32[]{:S(2)}, u32[]{:S(2)}) %collective-permute-start.50) | collective-permute-done | bytes 786464 | tf_op jit(solution)/shard_map/ppermute | solution.py:620
  569.3 16.5 %collective-permute-done.63 = f32[152,384]{1,0:T(8,128)S(1)} collective-permute-done((f32[152,384]{1,0:T(8,128)S(1)}, f32[152,384]{1,0:T(8,128)S(1)}, u32[]{:S(2)}, u32[]{:S(2)}) %collective-permute-start.63) | collective-permute-done | bytes 233504 | tf_op jit(solution)/shard_map/ppermute | solution.py:620
  626.3 15.0 %collective-permute-done.67 = f32[736,384]{1,0:T(8,128)S(1)} collective-permute-done((f32[736,384]{1,0:T(8,128)S(1)}, f32[736,384]{1,0:T(8,128)S(1)}, u32[]{:S(2)}, u32[]{:S(2)}) %collective-permute-start.67) | collective-permute-done | bytes 1130528 | tf_op jit(solution)/shard_map/ppermute | solution.py:620
  650.2 12.8 %collective-permute-done.55 = f32[256,768]{1,0:T(8,128)S(1)} collective-permute-done((f32[256,768]{1,0:T(8,128)S(1)}, f32[256,768]{1,0:T(8,128)S(1)}, u32[]{:S(2)}, u32[]{:S(2)}) %collective-permute-start.55) | collective-permute-done | bytes 786464 | tf_op jit(solution)/shard_map/ppermute | solution.py:620
  668.5 11.3 %collective-permute-start.56 = (f32[256,768]{1,0:T(8,128)}, f32[256,768]{1,0:T(8,128)}, u32[]{:S(2)}, u32[]{:S(2)}) collective-permute-start(f32[256,768]{1,0:T(8,128)} %broadcast_add_fusion.3), channel_id=1, source_target_pairs={{0,1},{1,2},{2,3},{4,5},{5,6},{6,7},{8,9},{9,10},{10,11},{12,13},{... | collective-permute-start | bytes 2359304 | tf_op jit(solution)/shard_map/ppermute | solution.py:620
  (394 shorter events, 379.8 us)
Async XLA Ops:
  4.9 51.5 %collective-permute-start = (f32[1032,768]{1,0:T(8,128)}, f32[1032,768]{1,0:T(8,128)}, u32[]{:S(2)}, u32[]{:S(2)}) collective-permute-start(f32[1032,768]{1,0:T(8,128)} %pad_maximum_fusion.2), channel_id=1, source_target_pairs={{0,16},{1,17},{4,20},{5,21},{8,24},{9,25},{12,28},{13,29},{18,2},{... | collective-permute-start | bytes 9510920 | tf_op jit(solution)/shard_map/ppermute | solution.py:620
  38.6 51.3 %collective-permute-start.11 = (f32[608,384]{1,0:T(8,128)S(1)}, f32[608,384]{1,0:T(8,128)S(1)}, u32[]{:S(2)}, u32[]{:S(2)}) collective-permute-start(f32[608,384]{1,0:T(8,128)S(1)} %broadcast_add_fusion.1), channel_id=1, source_target_pairs={{0,2},{1,3},{4,6},{5,7},{8,10},{9,11},{12,14},{13,15},{18,16},{19,... | collective-permute-start | bytes 2801672 | tf_op jit(solution)/shard_map/ppermute | solution.py:620
  117.4 38.3 %collective-permute-start.13 = (f32[520,768]{1,0:T(8,128)S(1)}, f32[520,768]{1,0:T(8,128)}, u32[]{:S(2)}, u32[]{:S(2)}) collective-permute-start(f32[520,768]{1,0:T(8,128)S(1)} %dynamic-slice_add_fusion), channel_id=1, source_target_pairs={{0,1},{1,0},{2,3},{3,2},{4,5},{5,4},{6,7},{7,6},{8,9},{9,8},{10,11... | collective-permute-start | bytes 4792328 | tf_op jit(solution)/shard_map/ppermute | solution.py:620
  127.1 72.7 %collective-permute-start.20 = (f32[1024,768]{1,0:T(8,128)}, f32[1024,768]{1,0:T(8,128)}, u32[]{:S(2)}, u32[]{:S(2)}) collective-permute-start(f32[1024,768]{1,0:T(8,128)} %convert_add_fusion), channel_id=1, source_target_pairs={{0,16},{1,17},{4,20},{5,21},{8,24},{9,25},{12,28},{13,29},{18,2},{... | collective-permute-start | bytes 9437192 | tf_op jit(solution)/shard_map/ppermute | solution.py:620
  227.0 32.2 %collective-permute-start.24 = (f32[256,768]{1,0:T(8,128)S(1)}, f32[256,768]{1,0:T(8,128)S(1)}, u32[]{:S(2)}, u32[]{:S(2)}) collective-permute-start(f32[256,768]{1,0:T(8,128)S(1)} %dynamic-slice_add_fusion.5), channel_id=1, source_target_pairs={{0,1},{1,0},{2,3},{3,2},{4,5},{5,4},{6,7},{7,6},{8,9},{9,8},{10,11... | collective-permute-start | bytes 2359304 | tf_op jit(solution)/shard_map/ppermute | solution.py:620
  255.7 31.0 %collective-permute-start.28 = (f32[384,384]{1,0:T(8,128)}, f32[384,384]{1,0:T(8,128)S(1)}, u32[]{:S(2)}, u32[]{:S(2)}) collective-permute-start(f32[384,384]{1,0:T(8,128)} %get-tuple-element.288), channel_id=1, source_target_pairs={{0,4},{1,5},{2,6},{3,7},{4,0},{5,1},{6,2},{7,3},{8,12},{9,13},{10,... | collective-permute-start | bytes 1769480 | tf_op jit(solution)/shard_map/ppermute | solution.py:620
  256.8 31.2 %collective-permute-start.29 = (f32[384,384]{1,0:T(8,128)}, f32[384,384]{1,0:T(8,128)S(1)}, u32[]{:S(2)}, u32[]{:S(2)}) collective-permute-start(f32[384,384]{1,0:T(8,128)} %get-tuple-element.290), channel_id=1, source_target_pairs={{0,8},{1,9},{2,10},{3,11},{4,12},{5,13},{6,14},{7,15},{8,0},{9,1},... | collective-permute-start | bytes 1769480 | tf_op jit(solution)/shard_map/ppermute | solution.py:620
  257.8 30.3 %collective-permute-start.30 = (f32[384,384]{1,0:T(8,128)}, f32[384,384]{1,0:T(8,128)}, u32[]{:S(2)}, u32[]{:S(2)}) collective-permute-start(f32[384,384]{1,0:T(8,128)} %get-tuple-element.289), channel_id=1, source_target_pairs={{0,12},{1,13},{2,14},{3,15},{4,8},{5,9},{6,10},{7,11},{8,4},{9,5},... | collective-permute-start | bytes 1769480 | tf_op jit(solution)/shard_map/ppermute | solution.py:620
  260.6 32.0 %collective-permute-start.25 = (f32[256,768]{1,0:T(8,128)S(1)}, f32[256,768]{1,0:T(8,128)S(1)}, u32[]{:S(2)}, u32[]{:S(2)}) collective-permute-start(f32[256,768]{1,0:T(8,128)S(1)} %multiply_add_fusion.1.refs_18_), channel_id=1, source_target_pairs={{0,1},{1,2},{2,3},{4,5},{5,6},{6,7},{8,9},{9,10},{10,11},{12,13},{... | collective-permute-start | bytes 2359304 | tf_op jit(solution)/shard_map/ppermute | solution.py:620
  263.1 29.5 %collective-permute-start.27 = (f32[256,768]{1,0:T(8,128)S(1)}, f32[256,768]{1,0:T(8,128)}, u32[]{:S(2)}, u32[]{:S(2)}) collective-permute-start(f32[256,768]{1,0:T(8,128)S(1)} %multiply_add_fusion.1.refs_18_), channel_id=1, source_target_pairs={{1,0},{2,1},{3,2},{5,4},{6,5},{7,6},{9,8},{10,9},{11,10},{13,12},{... | collective-permute-start | bytes 2359304 | tf_op jit(solution)/shard_map/ppermute | solution.py:620
  307.7 39.6 %collective-permute-start.32 = (f32[512,768]{1,0:T(8,128)S(1)}, f32[512,768]{1,0:T(8,128)}, u32[]{:S(2)}, u32[]{:S(2)}) collective-permute-start(f32[512,768]{1,0:T(8,128)S(1)} %dynamic-slice_add_fusion.2), channel_id=1, source_target_pairs={{0,1},{1,0},{2,3},{3,2},{4,5},{5,4},{6,7},{7,6},{8,9},{9,8},{10,11... | collective-permute-start | bytes 4718600 | tf_op jit(solution)/shard_map/ppermute | solution.py:620
  413.8 45.1 %collective-permute-start.47 = (f32[384,384]{1,0:T(8,128)}, f32[384,384]{1,0:T(8,128)}, u32[]{:S(2)}, u32[]{:S(2)}) collective-permute-start(f32[384,384]{1,0:T(8,128)} %get-tuple-element.287), channel_id=1, source_target_pairs={{0,8},{1,9},{2,10},{3,11},{4,12},{5,13},{6,14},{7,15},{8,0},{9,1},... | collective-permute-start | bytes 1769480 | tf_op jit(solution)/shard_map/ppermute | solution.py:620
  414.7 45.5 %collective-permute-start.48 = (f32[384,384]{1,0:T(8,128)}, f32[384,384]{1,0:T(8,128)}, u32[]{:S(2)}, u32[]{:S(2)}) collective-permute-start(f32[384,384]{1,0:T(8,128)} %get-tuple-element.286), channel_id=1, source_target_pairs={{0,12},{1,13},{2,14},{3,15},{4,8},{5,9},{6,10},{7,11},{8,4},{9,5},... | collective-permute-start | bytes 1769480 | tf_op jit(solution)/shard_map/ppermute | solution.py:620
  417.1 63.4 %collective-permute-start.43 = (f32[584,384]{1,0:T(8,128)}, f32[584,384]{1,0:T(8,128)S(1)}, u32[]{:S(2)}, u32[]{:S(2)}) collective-permute-start(f32[584,384]{1,0:T(8,128)} %pad_maximum_fusion.8), channel_id=1, source_target_pairs={{2,0},{3,1},{6,4},{7,5},{10,8},{11,9},{14,12},{15,13},{16,18},{17,... | collective-permute-start | bytes 2691080 | tf_op jit(solution)/shard_map/ppermute | solution.py:620
  428.0 53.6 %collective-permute-start.38 = (f32[256,768]{1,0:T(8,128)}, f32[256,768]{1,0:T(8,128)}, u32[]{:S(2)}, u32[]{:S(2)}) collective-permute-start(f32[256,768]{1,0:T(8,128)} %broadcast_add_fusion.7), channel_id=1, source_target_pairs={{0,1},{1,2},{2,3},{4,5},{5,6},{6,7},{8,9},{9,10},{10,11},{12,13},{... | collective-permute-start | bytes 2359304 | tf_op jit(solution)/shard_map/ppermute | solution.py:620
  432.3 49.3 %collective-permute-start.45 = (f32[256,768]{1,0:T(8,128)}, f32[256,768]{1,0:T(8,128)}, u32[]{:S(2)}, u32[]{:S(2)}) collective-permute-start(f32[256,768]{1,0:T(8,128)} %broadcast_add_fusion.6), channel_id=1, source_target_pairs={{1,0},{2,1},{3,2},{5,4},{6,5},{7,6},{9,8},{10,9},{11,10},{13,12},{... | collective-permute-start | bytes 2359304 | tf_op jit(solution)/shard_map/ppermute | solution.py:620
  540.9 63.7 %collective-permute-start.70 = (f32[736,384]{1,0:T(8,128)}, f32[736,384]{1,0:T(8,128)}, u32[]{:S(2)}, u32[]{:S(2)}) collective-permute-start(f32[736,384]{1,0:T(8,128)} %fusion.4.refs_13_), channel_id=1, source_target_pairs={{0,4},{1,5},{4,0},{5,1},{8,12},{9,13},{12,8},{13,9},{18,22},{19,23... | collective-permute-start | bytes 3391496 | tf_op jit(solution)/shard_map/ppermute | solution.py:620
  559.8 29.6 %collective-permute-start.54 = (f32[256,768]{1,0:T(8,128)S(1)}, f32[256,768]{1,0:T(8,128)S(1)}, u32[]{:S(2)}, u32[]{:S(2)}) collective-permute-start(f32[256,768]{1,0:T(8,128)S(1)} %broadcast_add_fusion.5), channel_id=1, source_target_pairs={{0,1},{1,2},{2,3},{4,5},{5,6},{6,7},{8,9},{9,10},{10,11},{12,13},{... | collective-permute-start | bytes 2359304 | tf_op jit(solution)/shard_map/ppermute | solution.py:620
  564.0 33.3 %collective-permute-start.64 = (f32[584,384]{1,0:T(8,128)}, f32[584,384]{1,0:T(8,128)}, u32[]{:S(2)}, u32[]{:S(2)}) collective-permute-start(f32[584,384]{1,0:T(8,128)} %pad_maximum_fusion.9), channel_id=1, source_target_pairs={{2,0},{3,1},{6,4},{7,5},{10,8},{11,9},{14,12},{15,13},{16,18},{17,... | collective-permute-start | bytes 2691080 | tf_op jit(solution)/shard_map/ppermute | solution.py:620
  587.2 30.0 %collective-permute-start.71 = (f32[736,384]{1,0:T(8,128)}, f32[736,384]{1,0:T(8,128)}, u32[]{:S(2)}, u32[]{:S(2)}) collective-permute-start(f32[736,384]{1,0:T(8,128)} %fusion.4.refs_13_), channel_id=1, source_target_pairs={{0,8},{1,9},{4,12},{5,13},{8,0},{9,1},{12,4},{13,5},{18,26},{19,27... | collective-permute-start | bytes 3391496 | tf_op jit(solution)/shard_map/ppermute | solution.py:620
  601.4 39.9 %collective-permute-start.67 = (f32[736,384]{1,0:T(8,128)S(1)}, f32[736,384]{1,0:T(8,128)S(1)}, u32[]{:S(2)}, u32[]{:S(2)}) collective-permute-start(f32[736,384]{1,0:T(8,128)S(1)} %fusion.6), channel_id=1, source_target_pairs={{0,8},{1,9},{4,12},{5,13},{8,0},{9,1},{12,4},{13,5},{18,26},{19,27... | collective-permute-start | bytes 3391496 | tf_op jit(solution)/shard_map/ppermute | solution.py:620
  604.6 36.7 %collective-permute-start.68 = (f32[736,384]{1,0:T(8,128)S(1)}, f32[736,384]{1,0:T(8,128)S(1)}, u32[]{:S(2)}, u32[]{:S(2)}) collective-permute-start(f32[736,384]{1,0:T(8,128)S(1)} %fusion.6), channel_id=1, source_target_pairs={{0,12},{1,13},{4,8},{5,9},{8,4},{9,5},{12,0},{13,1},{18,30},{19,31... | collective-permute-start | bytes 3391496 | tf_op jit(solution)/shard_map/ppermute | solution.py:620
  621.5 84.9 %collective-permute-start.73 = (f32[4,736,384]{2,1,0:T(8,128)}, f32[4,736,384]{2,1,0:T(8,128)}, u32[]{:S(2)}, u32[]{:S(2)}) collective-permute-start(f32[4,736,384]{2,1,0:T(8,128)} %pad_maximum_fusion.1.refs_1_), channel_id=1, source_target_pairs={{0,16},{1,17},{4,20},{5,21},{8,24},{9,25},{12,28},{13,29},{18,2},{... | collective-permute-start | bytes 13565960 | tf_op jit(solution)/shard_map/ppermute | solution.py:620
  643.8 68.6 %collective-permute-start.69 = (f32[4,736,384]{2,1,0:T(8,128)}, f32[4,736,384]{2,1,0:T(8,128)}, u32[]{:S(2)}, u32[]{:S(2)}) collective-permute-start(f32[4,736,384]{2,1,0:T(8,128)} %pad_maximum_fusion.refs_1_), channel_id=1, source_target_pairs={{0,16},{1,17},{4,20},{5,21},{8,24},{9,25},{12,28},{13,29},{18,2},{... | collective-permute-start | bytes 13565960 | tf_op jit(solution)/shard_map/ppermute | solution.py:620
  (104 other events, 1179.1 us)

commit v3 on v2

--- a/solution.py
+++ b/solution.py
@@ -668,6 +668,10 @@
     return array + jnp.where(w.q > 1000, first, jnp.zeros_like(first))
 
 
+def event_of(*arrays):
+    return sum(array[(0,) * array.ndim].astype(FLOAT) for array in arrays).reshape(1, 1)
+
+
 def pack_kernel(flags, value, gate, out, taps, off, gain, bias, decay, skip, step, *outs, layers):
     lanes = value.shape[2]
     d = value.shape[1]
@@ -765,17 +769,23 @@
     return pl.BlockSpec((None,) + tuple(shape[1:]), lambda b: (layer,) + (0,) * (len(shape) - 1))
 
 
-def delivered_kernel(flags, own, got, *rest):
-    gate_o, value_o, out_o, rows_o, state_o, extra_o, gain_o, wide = rest[-8:]
+def delivered_kernel(flags, own, got, *rest, last):
+    if last:
+        (
+            gate_o, value_o, out_o, rows_o, state_o, gain_in_o, step_o, taps_o, off_o, state_taps_o, state_off_o,
+            bias_o, decay_o, skip_o, gain_o, wide,
+        ) = rest[-16:]
+        rows_1 = rest[0]
+    else:
+        gate_o, value_o, out_o, rows_o = rest
     count = own.shape[0]
     d, lanes = value_o.shape
     size = d // count
     half = size // 2
     rows = 3 * size
-    part = own.shape[1] - rows - 16
+    part = (own.shape[1] - rows - 16) // LAYERS
 
     def put(source):
-        total = jnp.zeros((8, lanes), FLOAT)
         for j in range(count):
             k = flags[0] ^ j
             gate_o[j * size : (j + 1) * size] = source[k, 0:size]
@@ -783,14 +793,22 @@
             out_o[j * half : (j + 1) * half, lanes:] = source[k, size + half : 2 * size]
             value_o[j * size : (j + 1) * size] = source[k, 2 * size : rows]
             rows_o[j * 8 : (j + 1) * 8] = source[k, rows : rows + 8]
-            total = total + source[k, rows + 8 + part :]
-        for j, group, side, row in common_places(count, part):
-            wide[row : row + part, side * LANES : (side + 1) * LANES] = source[
-                flags[0] ^ j, rows + 8 : rows + 8 + part, group * LANES : (group + 1) * LANES
-            ]
-        gain_o[...] = total
-        state_o[...] = wide[0:d]
-        extra_o[...] = wide[d : d + 8]
+        if last:
+            total = jnp.zeros((8, lanes), FLOAT)
+            for j in range(count):
+                total = total + source[j, rows + 8 + LAYERS * part :]
+            for l in range(LAYERS):
+                for k in range(d // lanes):
+                    at = l * (d // lanes) + k
+                    gain_in_o[l : l + 1, k * lanes : (k + 1) * lanes] = total[at : at + 1]
+                base = rows + 8 + l * part
+                for j, group, side, row in common_places(count, part):
+                    wide[row : row + part, side * LANES : (side + 1) * LANES] = source[
+                        flags[0] ^ j, base : base + part, group * LANES : (group + 1) * LANES
+                    ]
+                state_o[l] = wide[0:d]
+                state_taps_o[l] = wide[d : d + CONV]
+                state_off_o[l : l + 1] = wide[d + CONV : d + CONV + 1]
 
     @pl.when(flags[1] == 1)
     def _():
@@ -799,6 +817,20 @@
     @pl.when(flags[1] == 0)
     def _():
         put(got)
+
+    if last:
+        heads = bias_o.shape[1]
+        spread = spread_matrix(lanes, heads)
+        for l, mine in ((0, rows_o), (1, rows_1)):
+            taps_o[l] = mine[0:CONV]
+            off_o[l : l + 1] = mine[CONV : CONV + 1]
+            gain_o[l : l + 1] = mine[CONV + 1 : CONV + 2]
+            skip = nt(mine[0:8], spread, PRECISE)
+            skip_o[l : l + 1] = skip[6:7, 0:heads]
+            decay_o[l : l + 1] = mine[7:8, 0:heads]
+            bias_o[l : l + 1] = mine[7:8, LANES : LANES + heads]
+            step_o[l, 0:lanes] = mine[16:24].T[:, 0:heads]
+            step_o[l, lanes:] = mine[24:32].T[:, 0:heads]
 
 
 def joined_kernel(flags, have, got, out):
@@ -867,7 +899,7 @@
         [(w.flags, "smem"), (have, "whole"), (got, "whole")],
         [((2 * have.shape[0], have.shape[1]), BFLOAT, "rows")],
     )
-    return out
+    return out, got
 
 
 def over_outer(w, part):
@@ -885,40 +917,35 @@
     return [at(0)] + [move(at(k), lambda dp, q, t, k=k: (dp, q ^ k, t)) for k in range(1, w.count)]
 
 
-def total_middle(w, part_a, got, shard_rows, gains, event):
-    part = over_outer(w, tie(w, sum(got[1:], got[0]), event))
-
-    def across(array):
-        return move(array, lambda dp, q, t: None if at_home(dp, t) else (dp, q, t ^ 2))
-
-    main = jnp.concatenate([part_a, part[:shard_rows]])
-    main_far = across(main)
-    common = jnp.concatenate([part[shard_rows:], gains])
-    common = common + move(common, other_core)
-    common = common + move(common, beside)
-    return jnp.concatenate([main, common]), jnp.concatenate([main_far, across(common)])
-
-
-def total_spread(w, part, far, event):
-    part = tie(w, part + far, event)
+def across(array):
+    return move(array, lambda dp, q, t: None if at_home(dp, t) else (dp, q, t ^ 2))
+
+
+def total_spread(w, part):
     got = [
         move(part, lambda dp, q, t, k=k: (dp, q ^ k, t) if at_home(dp, t) else None) for k in range(1, w.count)
     ]
     return part, got
 
 
-def total_end(w, layer, part, got, shapes, before):
+def total_end(w, layer, part, got, shapes, before, small=()):
     own = jnp.stack([part] + got)
     got = move(own, lambda dp, q, t: (dp ^ 1, q, t) if at_home(dp, t) else None)
+    last = before is not None
     inputs = [(w.flags, "smem"), (own, "whole"), (got, "whole")]
-    aliases = {}
-    if before is not None:
-        aliases = {len(inputs) + i: i for i in range(len(before))}
-        inputs += [(array, pl.BlockSpec(memory_space=pl.ANY)) for array in before]
-    d, half = shapes[0][1], shapes[4][2]
+    outputs = [(shape, FLOAT, layer_spec(shape, layer)) for shape in shapes]
+    outputs.append(((32, shapes[0][2]), FLOAT, "whole"))
+    aliases, scratch = {}, []
+    if last:
+        inputs.append((before[-1], "whole"))
+        aliases = {len(inputs) + i: i for i in range(len(shapes))}
+        inputs += [(array, pl.BlockSpec(memory_space=pl.ANY)) for array in before[:-1]]
+        outputs += [(shape, FLOAT, "whole") for shape in small]
+        d = shapes[0][1]
+        part = (own.shape[1] - 3 * d // 4 - 16) // LAYERS
+        scratch = [pltpu.VMEM((6 * part, small[0][2]), FLOAT)]
     return call(
-        delivered_kernel, 1, inputs, [(shape, FLOAT, layer_spec(shape, layer)) for shape in shapes],
-        [pltpu.VMEM((6 * (own.shape[1] - 3 * d // 4 - 16), half), FLOAT)], aliases=aliases,
+        functools.partial(delivered_kernel, last=last), 1, inputs, outputs, scratch, aliases=aliases
     )
 
 
@@ -1197,30 +1224,32 @@
     shard_rows = size + 8
     none = jnp.zeros((8, lanes), FLOAT)
 
-    up, down = (tie(w, array, above_mine) for array in mixed_first)
-    mixed_second = hand_step(w, up, down)
-    mixed_third = hand_step(w, tie(w, mixed_second[0], mixed_second[1]), tie(w, mixed_second[1], mixed_second[0]))
-    mixed_steps = [mixed_first, mixed_second, mixed_third]
+    shapes = (
+        (LAYERS, d, lanes), (LAYERS, d, lanes), (LAYERS, lanes, d),
+    )
 
     def middle(event):
-        held["part"], held["far"] = total_middle(w, part_1, [held["start"]], shard_rows, none, event)
-        return [held["part"]] + list(mixed_second)
+        held["main"] = tie(w, jnp.concatenate([part_1, held["start"][:shard_rows]]), event)
+        held["far"] = across(held["main"])
+        up, down = (tie(w, array, event) for array in mixed_first)
+        up, down = held["second"] = hand_step(w, up, down)
+        held["third"] = hand_step(w, tie(w, up, down), tie(w, down, up))
+        return [held["main"], up, down]
 
     def spread(event):
-        held["part"], held["got"] = total_spread(w, held["part"], held["far"], event)
-        return [held["part"]] + list(mixed_third)
+        held["part"] = held["main"] + held["far"]
+        return [held["part"], *held["third"]]
 
     grad_normed, packed, (upstream, gain_1) = backward_layer(
         w, (cot, above_mine, above_other, x_1, in_gain[1][None], mine, other), wts[0], saved_0, geometry,
         ((), middle, spread),
     )
-    shapes = (
-        (LAYERS, d, lanes), (LAYERS, d, lanes), (LAYERS, lanes, d), (LAYERS, 32, lanes), (LAYERS, d, wide),
-        (LAYERS, 8, wide), (LAYERS, 8, lanes),
-    )
+    far_a = across(packed[0])
     first_half = halves(w, grad_normed)
     got = total_start(w, packed[1], first_half)
-    last_part = piece(first_half, w.low, 2) + move(piece(first_half, 1 - w.low, 2), beside)
+    last_got = move(piece(first_half, 1 - w.low, 2), beside)
+    part = over_outer(w, sum(got[1:], got[0]))
+    last_part = piece(first_half, w.low, 2) + tie(w, last_got, far_a)
     x = piece(x_0, quarter, 4)
     inv_rms = lax.rsqrt(jnp.mean(x * x, axis=1, keepdims=True) + EPSILON)
     scaled = x * inv_rms
@@ -1229,21 +1258,37 @@
     last = piece(upstream, quarter, 4) + inv_rms * (
         inner - scaled * jnp.mean(inner * scaled, axis=1, keepdims=True)
     )
-    steps = hand_out(w, last)
-    totals = total_end(w, 1, tie(w, held["part"], steps[0][0]), held["got"], shapes, None)
-    held["mixed"] = hand_out_end(w, mixed, mixed_steps[:2] + [(tie(w, mixed_third[0], last), mixed_third[1])])
+    last = tie(w, last, part)
+    first_step = hand_step(w, last, last)
+    totals = total_end(w, 1, *total_spread(w, tie(w, held["part"], part)), shapes, None)
+    third = (tie(w, held["third"][0], last), held["third"][1])
+    mixed_out, _ = hand_out_end(w, mixed, [mixed_first, held["second"], third])
     gains = jnp.concatenate([gain_0.reshape(-1, lanes), 0.25 * gain_1[0].reshape(-1, lanes)])
     gains = jnp.pad(gains, ((0, 8 - gains.shape[0]), (0, 0)))
-    part, far = total_middle(w, packed[0], got, shard_rows, gains, steps[0][0])
-    part, got = total_spread(w, part, far, steps[1][0])
-    input_grad = hand_out_end(w, last, steps)
-    grad_gate, grad_value, grad_out, rows, state, extra, gains = total_end(w, 0, part, got, shapes, totals)
-    step = jnp.concatenate([rows[:, 16:24], rows[:, 24:32]], axis=2)
-    step = jnp.swapaxes(step[:, :heads], 1, 2)
+    main_b = part[:shard_rows]
+    common = jnp.concatenate([part[shard_rows:], held["start"][shard_rows:], gains])
+    common = common + move(common, other_core)
+    common = common + move(common, beside)
+    rest_b = jnp.concatenate([main_b, common])
+    far_b = across(rest_b)
+    event = event_of(*first_step, rest_b[shard_rows:])
+    second_step = hand_step(w, *(tie(w, array, event) for array in first_step))
+    part, got = total_spread(w, jnp.concatenate([packed[0] + far_a, rest_b + far_b]))
+    third_step = hand_step(w, *(tie(w, array, event_of(*second_step, far_b)) for array in second_step))
+    steps = [first_step, second_step, tuple(tie(w, array, event_of(*got)) for array in third_step)]
+    input_grad, crossed = hand_out_end(w, last, steps)
+    part = tie(w, part, crossed)
+    small = (
+        (LAYERS, d, wide), (LAYERS, d), (LAYERS, d, heads), (LAYERS, CONV, lanes), (LAYERS, lanes),
+        (LAYERS, CONV, wide), (LAYERS, wide), (LAYERS, heads), (LAYERS, heads), (LAYERS, heads), (LAYERS, lanes),
+    )
+    (
+        grad_gate, grad_value, grad_out, _, state, gain_in, step, taps, off, state_taps, state_off, bias, decay, skip,
+        gain_out,
+    ) = total_end(w, 0, part, got, shapes, totals, small)
     return (
-        held["mixed"], input_grad, gains[0, :4].reshape(2, d), grad_gate, grad_value, state, step, rows[:, :CONV],
-        rows[:, CONV], extra[:, :CONV], extra[:, CONV], rows[:, 7, LANES : LANES + heads], rows[:, 7, :heads],
-        jnp.sum(rows[:, 6].reshape(LAYERS, heads, -1), axis=2), rows[:, 5], grad_out,
+        mixed_out, input_grad, gain_in, grad_gate, grad_value, state, step, taps, off, state_taps, state_off,
+        bias, decay, skip, gain_out, grad_out,
     )
 
 

time: 741 us -> 703 us (0.949)
  waiting for transfers between devices: 192 us -> 160 us
    ppermute x71 -> x68, waiting for transfers between devices: 189 us -> 156 us  [move(): return lax.ppermute(shard, AXES, pairs)]
    ppermute x71 -> x68, starting transfers between devices: 153 us -> 146 us  [move(): return lax.ppermute(shard, AXES, pairs)]
    add x23 -> x21, other arithmetic: 28 us -> 21.6 us  [tie(): return array + jnp.where(w.q > 1000, first, jnp.zeros_like(first))]
    slice x20 -> x17, local copies, waits for them, and re-layouts: 15.3 us -> 12.4 us  [tie(): first = event[(0,) * event.ndim].astype(array.dtype)]
    unnamed x114 -> x140, local copies, waits for them, and re-layouts: 14.8 us -> 17.3 us
  transfers between devices with their start and end apart: 74 -> 71, of which waited for: 25 -> 27; matrix products, arithmetic and copies ran while one was open for 11% -> 11% of each run, Pallas kernels for 16% -> 17%
where the time goes in v3:
time: 703 us; the launch traced here: 692 us
  Pallas kernels  189 us (27%)
  waiting for transfers between devices  160 us (23%)
  starting transfers between devices  152 us (22%)
  other arithmetic  72.1 us (10%)
  local copies, waits for them, and re-layouts  51.1 us (7%)
  blocking collectives  48.1 us (7%)
  between operations  19.4 us (3%)
    pallas_call x21, Pallas kernels, call(): pl.pallas_call(run, grid=(grid,), in_specs=[spec_of(a.shape, kind) for a,...  189 us
    ppermute x68, waiting for transfers between devices, move(): return lax.ppermute(shard, AXES, pairs)  156 us
    ppermute x68, starting transfers between devices, move(): return lax.ppermute(shard, AXES, pairs)  146 us
    all_gather x2, blocking collectives, forward_layer(): everything = lax.all_gather(payload, 'ctx')  25.4 us
    all_gather x2, blocking collectives, backward_layer(): everything = lax.all_gather(payload, 'ctx')  22.7 us
    add x21, other arithmetic, tie(): return array + jnp.where(w.q > 1000, first, jnp.zeros_like(first))  21.6 us
    unnamed x140, local copies, waits for them, and re-layouts  17.3 us
  transfers between devices with their start and end apart: 71, of which 27 were waited for; matrix products, arithmetic and copies ran while one was open for 11% of the time, Pallas kernels for 17%

profile of v3, /device:TPU:0, one launch (start us, length us, event | category | flops | bytes accessed | tf_op | source)
XLA Modules:
  0.0 692.4 jit_solution(3273220616583500730)
XLA Ops:
  38.6 14.1 %collective-permute-start.11 = (f32[608,384]{1,0:T(8,128)S(1)}, f32[608,384]{1,0:T(8,128)S(1)}, u32[]{:S(2)}, u32[]{:S(2)}) collective-permute-start(f32[608,384]{1,0:T(8,128)S(1)} %broadcast_add_fusion.1), channel_id=1, source_target_pairs={{0,2},{1,3},{4,6},{5,7},{8,10},{9,11},{12,14},{13,15},{18,16},{19,... | collective-permute-start | bytes 2801672 | tf_op jit(solution)/shard_map/ppermute | solution.py:620
  60.2 13.3 %shard_map.290 = (f32[1024,768]{1,0:T(8,128)}, bf16[1024,768]{1,0:T(8,128)(2,1)}, f32[1024,640]{1,0:T(8,128)}, f32[8,640]{1,0:T(8,128)}, f32[1024,640]{1,0:T(8,1...) custom-call(s32[4]{0:T(128)} %pad_add_fusion.refs_0_, ...), custom_call_target="tpu_custom_call" | custom-call | flops 1006632960 | bytes 13211680 | tf_op jit(solution)/shard_map/pallas_call | solution.py:100
  77.5 12.6 %all-gather = f32[1568,128]{1,0:T(8,128)} all-gather(f32[392,128]{1,0:T(8,128)S(1)} %copy-done.51), channel_id=2, replica_groups=mesh['dp'=2,'ctx'=4,'tensor'=4] {'ctx'}, dimensions={0}, use_global_device_ids=true | all-gather | bytes 1003520 | tf_op jit(solution)/shard_map/all_gather | solution.py:989
  97.6 10.1 %shard_map.293 = (f32[1024,384]{1,0:T(8,128)}, f32[4,384,128]{2,1,0:T(8,128)}, f32[1040,768]{1,0:T(8,128)}) custom-call(s32[4]{0:T(128)} %pad_add_fusion.refs_0_, f32[4,392,128]{2,1,0:T(8,128)} %bitcast.115, f32[4,384,128]{2,1,0:T(8,128)} %get-tuple-element.123.refs_2_, f32[4,8,128]{2,1,0:T(8,128)} %get-tuple-element.124.refs_3_.refs_17_, ...), custom_call_target="tpu_custom_call" | custom-call | flops 603979776 | bytes 14442528 | tf_op jit(solution)/shard_map/pallas_call | solution.py:100
  127.1 9.7 %collective-permute-start.20 = (f32[1024,768]{1,0:T(8,128)}, f32[1024,768]{1,0:T(8,128)}, u32[]{:S(2)}, u32[]{:S(2)}) collective-permute-start(f32[1024,768]{1,0:T(8,128)} %convert_add_fusion), channel_id=1, source_target_pairs={{0,16},{1,17},{4,20},{5,21},{8,24},{9,25},{12,28},{13,29},{18,2},{... | collective-permute-start | bytes 9437192 | tf_op jit(solution)/shard_map/ppermute | solution.py:620
  144.5 11.2 %collective-permute-done.13 = f32[520,768]{1,0:T(8,128)} collective-permute-done((f32[520,768]{1,0:T(8,128)S(1)}, f32[520,768]{1,0:T(8,128)}, u32[]{:S(2)}, u32[]{:S(2)}) %collective-permute-start.13) | collective-permute-done | bytes 1597472 | tf_op jit(solution)/shard_map/ppermute | solution.py:620
  165.0 15.3 %shard_map.295 = (f32[1024,768]{1,0:T(8,128)}, bf16[1024,768]{1,0:T(8,128)(2,1)}, f32[1024,640]{1,0:T(8,128)}, f32[8,640]{1,0:T(8,128)}, f32[1024,640]{1,0:T(8,1...) custom-call(s32[4]{0:T(128)} %pad_add_fusion.refs_0_, ...), custom_call_target="tpu_custom_call" | custom-call | flops 1006632960 | bytes 15325216 | tf_op jit(solution)/shard_map/pallas_call | solution.py:100
  187.0 12.8 %all-gather.1 = f32[1568,128]{1,0:T(8,128)} all-gather(f32[392,128]{1,0:T(8,128)S(1)} %copy-done.61), channel_id=3, replica_groups=mesh['dp'=2,'ctx'=4,'tensor'=4] {'ctx'}, dimensions={0}, use_global_device_ids=true | all-gather | bytes 1003520 | tf_op jit(solution)/shard_map/all_gather | solution.py:989
  199.9 12.7 %shard_map.298 = (f32[1024,384]{1,0:T(8,128)}, f32[4,384,128]{2,1,0:T(8,128)}, f32[1024,768]{1,0:T(8,128)}, f32[4,8,256]{2,1,0:T(8,128)}, f32[1024,768]{1,0:T(8,128)}) custom-call(s32[4]{0:T(128)} %pad_add_fusion.refs_0_, f32[4,392,128]{2,1,0:T(8,128)} %bitcast.114, f32[4,384,128]{2,1,0:T(8,128)} %get-tuple-element.142.refs_2_, ...), custom_call_target="tpu_custom_call" | custom-call | flops 603979776 | bytes 23879712 | tf_op jit(solution)/shard_map/pallas_call | solution.py:100
  227.9 11.5 %shard_map.299 = (bf16[1024,384]{1,0:T(8,128)(2,1)}, bf16[1024,384]{1,0:T(8,128)(2,1)}, f32[4,384,384]{2,1,0:T(8,128)}, f32[8,384]{1,0:T(8,128)}, f32[4,384,128]{2,1,0:T(8,128)}, /*index=5*/f32[392,128]{1,0:T(8,128)}) custom-call(s32[4]{0:T(128)} %pad_add_fusion.refs_0_, f32[1024,768]{1,0:T(8,128)} %get-tuple-element.155.refs_1_, f32[4,8,256]{2,1,0:T(8,128)} %copy-done.62, ...), custom_call_target="tpu_custom_call" | custom-call | flops 1811939328 | bytes 23912480 | tf_op jit(solution)/shard_map/pallas_call | solution.py:100
  239.4 10.9 %all-gather.2 = f32[1568,128]{1,0:T(8,128)S(1)} all-gather(f32[392,128]{1,0:T(8,128)} %get-tuple-element.157), channel_id=4, replica_groups=mesh['dp'=2,'ctx'=4,'tensor'=4] {'ctx'}, dimensions={0}, use_global_device_ids=true | all-gather | bytes 1003520 | tf_op jit(solution)/shard_map/all_gather | solution.py:1054
  263.8 22.1 %shard_map.300 = (bf16[1024,640]{1,0:T(8,128)(2,1)}, f32[8,640]{1,0:T(8,128)}, bf16[1024,128]{1,0:T(8,128)(2,1)}, f32[8,640]{1,0:T(8,128)}, f32[8,640]{1,0:T(8,128)}, /*index=5*/f32[8,128]{1,0:T(8,128)}) custom-call(s32[4]{0:T(128)} %pad_add_fusion.refs_0_, f32[4,392,128]{2,1,0:T(8,128)} %bitcast.113, f32[4,384,128]{2,1,0:T(8,128)} %get-tuple-element.158.refs_2_, ...), custom_call_target="tpu_custom_call" | custom-call | flops 1207959552 | bytes 28557344 | tf_op jit(solution)/shard_map/pallas_call | solution.py:100
  293.0 8.9 %shard_map.301 = (f32[1024,768]{1,0:T(8,128)}, f32[4,344,384]{2,1,0:T(8,128)}) custom-call(bf16[1024,768]{1,0:T(8,128)(2,1)} %get-tuple-element.144.refs_0_.refs_3_, bf16[1024,640]{1,0:T(8,128)(2,1)} %get-tuple-element.164.refs_1_, f32[8,640]{1,0:T(8,128)} %get-tuple-element.165.refs_2_, f32[8,640]{1,0:T(8,128)} %copy-done.67, ...), custom_call_target="tpu_custom_call" | custom-call | flops 3221225472 | bytes 15884288 | tf_op jit(solution)/shard_map/pallas_call | solution.py:100
  318.3 11.4 %collective-permute-done.33 = f32[344,384]{1,0:T(8,128)S(1)} collective-permute-done((f32[344,384]{1,0:T(8,128)S(1)}, f32[344,384]{1,0:T(8,128)S(1)}, u32[]{:S(2)}, u32[]{:S(2)}) %collective-permute-start.33) | collective-permute-done | bytes 528416 | tf_op jit(solution)/shard_map/ppermute | solution.py:620
  329.7 11.7 %collective-permute-done.34 = f32[344,384]{1,0:T(8,128)S(1)} collective-permute-done((f32[344,384]{1,0:T(8,128)S(1)}, f32[344,384]{1,0:T(8,128)S(1)}, u32[]{:S(2)}, u32[]{:S(2)}) %collective-permute-start.34) | collective-permute-done | bytes 528416 | tf_op jit(solution)/shard_map/ppermute | solution.py:620
  353.2 15.8 %shard_map.302 = (f32[1024,768]{1,0:T(8,128)}, f32[8,768]{1,0:T(8,128)}, bf16[1024,384]{1,0:T(8,128)(2,1)}, bf16[1024,384]{1,0:T(8,128)(2,1)}, f32[4,384,384]{2,...) custom-call(s32[4]{0:T(128)} %pad_add_fusion.refs_0_, ...), custom_call_target="tpu_custom_call" | custom-call | flops 1811939328 | bytes 39680032 | tf_op jit(solution)/shard_map/pallas_call | solution.py:100
  378.7 11.7 %all-gather.3 = f32[1568,128]{1,0:T(8,128)S(1)} all-gather(f32[392,128]{1,0:T(8,128)S(1)} %copy-done.60), channel_id=5, replica_groups=mesh['dp'=2,'ctx'=4,'tensor'=4] {'ctx'}, dimensions={0}, use_global_device_ids=true | all-gather | bytes 1003520 | tf_op jit(solution)/shard_map/all_gather | solution.py:1054
  412.7 22.1 %shard_map.303 = (bf16[1024,640]{1,0:T(8,128)(2,1)}, f32[8,640]{1,0:T(8,128)}, bf16[1024,128]{1,0:T(8,128)(2,1)}, f32[8,640]{1,0:T(8,128)}, f32[8,640]{1,0:T(8,128)}, /*index=5*/f32[8,128]{1,0:T(8,128)}) custom-call(s32[4]{0:T(128)} %pad_add_fusion.refs_0_, f32[4,392,128]{2,1,0:T(8,128)} %bitcast.117, f32[4,384,128]{2,1,0:T(8,128)} %get-tuple-element.178.refs_2_, ...), custom_call_target="tpu_custom_call" | custom-call | flops 1207959552 | bytes 31924256 | tf_op jit(solution)/shard_map/pallas_call | solution.py:100
  441.7 8.9 %shard_map.304 = (f32[1024,768]{1,0:T(8,128)}, f32[4,344,384]{2,1,0:T(8,128)}) custom-call(bf16[1024,768]{1,0:T(8,128)(2,1)} %get-tuple-element.125.refs_0_.refs_8_, bf16[1024,640]{1,0:T(8,128)(2,1)} %get-tuple-element.184.refs_1_, f32[8,640]{1,0:T(8,128)} %get-tuple-element.185.refs_2_, f32[8,640]{1,0:T(8,128)} %copy-done.66, ...), custom_call_target="tpu_custom_call" | custom-call | flops 3221225472 | bytes 17678336 | tf_op jit(solution)/shard_map/pallas_call | solution.py:100
  477.1 9.5 %collective-permute-done.51 = f32[344,384]{1,0:T(8,128)} collective-permute-done((f32[344,384]{1,0:T(8,128)}, f32[344,384]{1,0:T(8,128)}, u32[]{:S(2)}, u32[]{:S(2)}) %collective-permute-start.51) | collective-permute-done | bytes 528416 | tf_op jit(solution)/shard_map/ppermute | solution.py:620
  507.6 13.7 %collective-permute-done.53 = f32[256,768]{1,0:T(8,128)S(1)} collective-permute-done((f32[256,768]{1,0:T(8,128)S(1)}, f32[256,768]{1,0:T(8,128)S(1)}, u32[]{:S(2)}, u32[]{:S(2)}) %collective-permute-start.53) | collective-permute-done | bytes 786464 | tf_op jit(solution)/shard_map/ppermute | solution.py:620
  544.4 20.1 %collective-permute-done.59 = f32[496,384]{1,0:T(8,128)} collective-permute-done((f32[496,384]{1,0:T(8,128)S(1)}, f32[496,384]{1,0:T(8,128)}, u32[]{:S(2)}, u32[]{:S(2)}) %collective-permute-start.59) | collective-permute-done | bytes 761888 | tf_op jit(solution)/shard_map/ppermute | solution.py:620
  590.0 13.7 %collective-permute-done.62 = f32[880,384]{1,0:T(8,128)} collective-permute-done((f32[880,384]{1,0:T(8,128)}, f32[880,384]{1,0:T(8,128)}, u32[]{:S(2)}, u32[]{:S(2)}) %collective-permute-start.62) | collective-permute-done | bytes 1351712 | tf_op jit(solution)/shard_map/ppermute | solution.py:620
  642.7 13.2 %collective-permute-done.68 = f32[584,384]{1,0:T(8,128)S(1)} collective-permute-done((f32[584,384]{1,0:T(8,128)S(1)}, f32[584,384]{1,0:T(8,128)S(1)}, u32[]{:S(2)}, u32[]{:S(2)}) %collective-permute-start.68) | collective-permute-done | bytes 897056 | tf_op jit(solution)/shard_map/ppermute | solution.py:620
  (408 shorter events, 355.9 us)
Async XLA Ops:
  4.9 51.5 %collective-permute-start = (f32[1032,768]{1,0:T(8,128)}, f32[1032,768]{1,0:T(8,128)}, u32[]{:S(2)}, u32[]{:S(2)}) collective-permute-start(f32[1032,768]{1,0:T(8,128)} %pad_maximum_fusion.2), channel_id=1, source_target_pairs={{0,16},{1,17},{4,20},{5,21},{8,24},{9,25},{12,28},{13,29},{18,2},{... | collective-permute-start | bytes 9510920 | tf_op jit(solution)/shard_map/ppermute | solution.py:620
  38.6 51.4 %collective-permute-start.11 = (f32[608,384]{1,0:T(8,128)S(1)}, f32[608,384]{1,0:T(8,128)S(1)}, u32[]{:S(2)}, u32[]{:S(2)}) collective-permute-start(f32[608,384]{1,0:T(8,128)S(1)} %broadcast_add_fusion.1), channel_id=1, source_target_pairs={{0,2},{1,3},{4,6},{5,7},{8,10},{9,11},{12,14},{13,15},{18,16},{19,... | collective-permute-start | bytes 2801672 | tf_op jit(solution)/shard_map/ppermute | solution.py:620
  117.5 38.2 %collective-permute-start.13 = (f32[520,768]{1,0:T(8,128)S(1)}, f32[520,768]{1,0:T(8,128)}, u32[]{:S(2)}, u32[]{:S(2)}) collective-permute-start(f32[520,768]{1,0:T(8,128)S(1)} %dynamic-slice_add_fusion), channel_id=1, source_target_pairs={{0,1},{1,0},{2,3},{3,2},{4,5},{5,4},{6,7},{7,6},{8,9},{9,8},{10,11... | collective-permute-start | bytes 4792328 | tf_op jit(solution)/shard_map/ppermute | solution.py:620
  127.1 72.7 %collective-permute-start.20 = (f32[1024,768]{1,0:T(8,128)}, f32[1024,768]{1,0:T(8,128)}, u32[]{:S(2)}, u32[]{:S(2)}) collective-permute-start(f32[1024,768]{1,0:T(8,128)} %convert_add_fusion), channel_id=1, source_target_pairs={{0,16},{1,17},{4,20},{5,21},{8,24},{9,25},{12,28},{13,29},{18,2},{... | collective-permute-start | bytes 9437192 | tf_op jit(solution)/shard_map/ppermute | solution.py:620
  226.4 31.5 %collective-permute-start.24 = (f32[256,768]{1,0:T(8,128)S(1)}, f32[256,768]{1,0:T(8,128)S(1)}, u32[]{:S(2)}, u32[]{:S(2)}) collective-permute-start(f32[256,768]{1,0:T(8,128)S(1)} %dynamic-slice_add_fusion.4), channel_id=1, source_target_pairs={{0,1},{1,0},{2,3},{3,2},{4,5},{5,4},{6,7},{7,6},{8,9},{9,8},{10,11... | collective-permute-start | bytes 2359304 | tf_op jit(solution)/shard_map/ppermute | solution.py:620
  254.4 31.6 %collective-permute-start.28 = (f32[384,384]{1,0:T(8,128)}, f32[384,384]{1,0:T(8,128)S(1)}, u32[]{:S(2)}, u32[]{:S(2)}) collective-permute-start(f32[384,384]{1,0:T(8,128)} %get-tuple-element.296), channel_id=1, source_target_pairs={{0,4},{1,5},{2,6},{3,7},{4,0},{5,1},{6,2},{7,3},{8,12},{9,13},{10,... | collective-permute-start | bytes 1769480 | tf_op jit(solution)/shard_map/ppermute | solution.py:620
  255.5 31.8 %collective-permute-start.29 = (f32[384,384]{1,0:T(8,128)}, f32[384,384]{1,0:T(8,128)}, u32[]{:S(2)}, u32[]{:S(2)}) collective-permute-start(f32[384,384]{1,0:T(8,128)} %get-tuple-element.298), channel_id=1, source_target_pairs={{0,8},{1,9},{2,10},{3,11},{4,12},{5,13},{6,14},{7,15},{8,0},{9,1},... | collective-permute-start | bytes 1769480 | tf_op jit(solution)/shard_map/ppermute | solution.py:620
  256.4 30.9 %collective-permute-start.30 = (f32[384,384]{1,0:T(8,128)}, f32[384,384]{1,0:T(8,128)}, u32[]{:S(2)}, u32[]{:S(2)}) collective-permute-start(f32[384,384]{1,0:T(8,128)} %get-tuple-element.297), channel_id=1, source_target_pairs={{0,12},{1,13},{2,14},{3,15},{4,8},{5,9},{6,10},{7,11},{8,4},{9,5},... | collective-permute-start | bytes 1769480 | tf_op jit(solution)/shard_map/ppermute | solution.py:620
  259.2 32.7 %collective-permute-start.25 = (f32[256,768]{1,0:T(8,128)S(1)}, f32[256,768]{1,0:T(8,128)S(1)}, u32[]{:S(2)}, u32[]{:S(2)}) collective-permute-start(f32[256,768]{1,0:T(8,128)S(1)} %multiply_add_fusion.refs_18_), channel_id=1, source_target_pairs={{0,1},{1,2},{2,3},{4,5},{5,6},{6,7},{8,9},{9,10},{10,11},{12,13},{... | collective-permute-start | bytes 2359304 | tf_op jit(solution)/shard_map/ppermute | solution.py:620
  262.3 29.5 %collective-permute-start.27 = (f32[256,768]{1,0:T(8,128)S(1)}, f32[256,768]{1,0:T(8,128)S(1)}, u32[]{:S(2)}, u32[]{:S(2)}) collective-permute-start(f32[256,768]{1,0:T(8,128)S(1)} %multiply_add_fusion.refs_18_), channel_id=1, source_target_pairs={{1,0},{2,1},{3,2},{5,4},{6,5},{7,6},{9,8},{10,9},{11,10},{13,12},{... | collective-permute-start | bytes 2359304 | tf_op jit(solution)/shard_map/ppermute | solution.py:620
  307.2 39.7 %collective-permute-start.32 = (f32[512,768]{1,0:T(8,128)S(1)}, f32[512,768]{1,0:T(8,128)}, u32[]{:S(2)}, u32[]{:S(2)}) collective-permute-start(f32[512,768]{1,0:T(8,128)S(1)} %dynamic-slice_add_fusion.2), channel_id=1, source_target_pairs={{0,1},{1,0},{2,3},{3,2},{4,5},{5,4},{6,7},{7,6},{8,9},{9,8},{10,11... | collective-permute-start | bytes 4718600 | tf_op jit(solution)/shard_map/ppermute | solution.py:620
  374.1 26.5 %collective-permute-start.37 = (f32[256,768]{1,0:T(8,128)}, f32[256,768]{1,0:T(8,128)S(1)}, u32[]{:S(2)}, u32[]{:S(2)}) collective-permute-start(f32[256,768]{1,0:T(8,128)} %broadcast_add_fusion.10), channel_id=1, source_target_pairs={{0,1},{1,2},{2,3},{4,5},{5,6},{6,7},{8,9},{9,10},{10,11},{12,13},{... | collective-permute-start | bytes 2359304 | tf_op jit(solution)/shard_map/ppermute | solution.py:620
  395.0 39.8 %collective-permute-start.44 = (f32[384,384]{1,0:T(8,128)}, f32[384,384]{1,0:T(8,128)}, u32[]{:S(2)}, u32[]{:S(2)}) collective-permute-start(f32[384,384]{1,0:T(8,128)} %get-tuple-element.295), channel_id=1, source_target_pairs={{0,8},{1,9},{2,10},{3,11},{4,12},{5,13},{6,14},{7,15},{8,0},{9,1},... | collective-permute-start | bytes 1769480 | tf_op jit(solution)/shard_map/ppermute | solution.py:620
  396.6 39.6 %collective-permute-start.45 = (f32[384,384]{1,0:T(8,128)}, f32[384,384]{1,0:T(8,128)}, u32[]{:S(2)}, u32[]{:S(2)}) collective-permute-start(f32[384,384]{1,0:T(8,128)} %get-tuple-element.294), channel_id=1, source_target_pairs={{0,12},{1,13},{2,14},{3,15},{4,8},{5,9},{6,10},{7,11},{8,4},{9,5},... | collective-permute-start | bytes 1769480 | tf_op jit(solution)/shard_map/ppermute | solution.py:620
  398.2 40.7 %collective-permute-start.41 = (f32[584,384]{1,0:T(8,128)S(1)}, f32[584,384]{1,0:T(8,128)S(1)}, u32[]{:S(2)}, u32[]{:S(2)}) collective-permute-start(f32[584,384]{1,0:T(8,128)S(1)} %maximum_add_fusion.1.refs_18_), channel_id=1, source_target_pairs={{2,0},{3,1},{6,4},{7,5},{10,8},{11,9},{14,12},{15,13},{16,18},{17,... | collective-permute-start | bytes 2691080 | tf_op jit(solution)/shard_map/ppermute | solution.py:620
  401.7 39.2 %collective-permute-start.39 = (f32[256,768]{1,0:T(8,128)}, f32[256,768]{1,0:T(8,128)}, u32[]{:S(2)}, u32[]{:S(2)}) collective-permute-start(f32[256,768]{1,0:T(8,128)} %broadcast_add_fusion.8), channel_id=1, source_target_pairs={{0,1},{1,2},{2,3},{4,5},{5,6},{6,7},{8,9},{9,10},{10,11},{12,13},{... | collective-permute-start | bytes 2359304 | tf_op jit(solution)/shard_map/ppermute | solution.py:620
  411.2 29.7 %collective-permute-start.42 = (f32[256,768]{1,0:T(8,128)S(1)}, f32[256,768]{1,0:T(8,128)S(1)}, u32[]{:S(2)}, u32[]{:S(2)}) collective-permute-start(f32[256,768]{1,0:T(8,128)S(1)} %broadcast_add_fusion.7), channel_id=1, source_target_pairs={{1,0},{2,1},{3,2},{5,4},{6,5},{7,6},{9,8},{10,9},{11,10},{13,12},{... | collective-permute-start | bytes 2359304 | tf_op jit(solution)/shard_map/ppermute | solution.py:620
  504.8 29.5 %collective-permute-start.56 = (f32[296,384]{1,0:T(8,128)S(1)}, f32[296,384]{1,0:T(8,128)S(1)}, u32[]{:S(2)}, u32[]{:S(2)}) collective-permute-start(f32[296,384]{1,0:T(8,128)S(1)} %fusion.23), channel_id=1, source_target_pairs={{0,1},{1,0},{2,3},{3,2},{4,5},{5,4},{6,7},{7,6},{8,9},{9,8},{10,11... | collective-permute-start | bytes 1363976 | tf_op jit(solution)/shard_map/ppermute | solution.py:620
  534.9 29.5 %collective-permute-start.59 = (f32[496,384]{1,0:T(8,128)S(1)}, f32[496,384]{1,0:T(8,128)}, u32[]{:S(2)}, u32[]{:S(2)}) collective-permute-start(f32[496,384]{1,0:T(8,128)S(1)} %pad_maximum_fusion.8), channel_id=1, source_target_pairs={{2,0},{3,1},{6,4},{7,5},{10,8},{11,9},{14,12},{15,13},{16,18},{17,... | collective-permute-start | bytes 2285576 | tf_op jit(solution)/shard_map/ppermute | solution.py:620
  537.0 40.3 %collective-permute-start.58 = (f32[256,768]{1,0:T(8,128)S(1)}, f32[256,768]{1,0:T(8,128)S(1)}, u32[]{:S(2)}, u32[]{:S(2)}) collective-permute-start(f32[256,768]{1,0:T(8,128)S(1)} %broadcast_add_fusion.5), channel_id=1, source_target_pairs={{1,0},{2,1},{3,2},{5,4},{6,5},{7,6},{9,8},{10,9},{11,10},{13,12},{... | collective-permute-start | bytes 2359304 | tf_op jit(solution)/shard_map/ppermute | solution.py:620
  538.5 40.2 %collective-permute-start.57 = (f32[256,768]{1,0:T(8,128)S(1)}, f32[256,768]{1,0:T(8,128)S(1)}, u32[]{:S(2)}, u32[]{:S(2)}) collective-permute-start(f32[256,768]{1,0:T(8,128)S(1)} %broadcast_add_fusion.6), channel_id=1, source_target_pairs={{0,1},{1,2},{2,3},{4,5},{5,6},{6,7},{8,9},{9,10},{10,11},{12,13},{... | collective-permute-start | bytes 2359304 | tf_op jit(solution)/shard_map/ppermute | solution.py:620
  569.1 34.7 %collective-permute-start.62 = (f32[880,384]{1,0:T(8,128)}, f32[880,384]{1,0:T(8,128)}, u32[]{:S(2)}, u32[]{:S(2)}) collective-permute-start(f32[880,384]{1,0:T(8,128)} %pad_maximum_fusion.7), channel_id=1, source_target_pairs={{0,8},{1,9},{4,12},{5,13},{8,0},{9,1},{12,4},{13,5},{18,26},{19,27... | collective-permute-start | bytes 4055048 | tf_op jit(solution)/shard_map/ppermute | solution.py:620
  572.4 33.9 %collective-permute-start.63 = (f32[880,384]{1,0:T(8,128)}, f32[880,384]{1,0:T(8,128)}, u32[]{:S(2)}, u32[]{:S(2)}) collective-permute-start(f32[880,384]{1,0:T(8,128)} %pad_maximum_fusion.7), channel_id=1, source_target_pairs={{0,12},{1,13},{4,8},{5,9},{8,4},{9,5},{12,0},{13,1},{18,30},{19,31... | collective-permute-start | bytes 4055048 | tf_op jit(solution)/shard_map/ppermute | solution.py:620
  623.2 59.6 %collective-permute-start.66 = (f32[4,880,384]{2,1,0:T(8,128)}, f32[4,880,384]{2,1,0:T(8,128)}, u32[]{:S(2)}, u32[]{:S(2)}) collective-permute-start(f32[4,880,384]{2,1,0:T(8,128)} %pad_maximum_fusion.refs_1_), channel_id=1, source_target_pairs={{0,16},{1,17},{4,20},{5,21},{8,24},{9,25},{12,28},{13,29},{18,2},{... | collective-permute-start | bytes 16220168 | tf_op jit(solution)/shard_map/ppermute | solution.py:620
  (116 other events, 1130.5 us)
